TPU v7x, 32 devices: a whole 2x2x4 slice. The times are simulated.
32 devices in a mesh: clips: 2 (over y), frame: 4 (over z), row: 2 (over x), head: 2 (over core).
Axes of the slice: x: 2, y: 2, z: 4, core: 2. Of those that a mesh axis runs over, the one named last changes fastest.
Arguments:
- query: bfloat16 [64, 16, 8, 1536], P(('clips', 'frame'), 'row', None, 'head'), parts along dimension 0, may hold values from -7 to 7
- keys: bfloat16 [64, 16, 8, 1536], P(('clips', 'frame'), 'row', None, 'head'), parts along dimension 0, may hold values from -6 to 6
- values: bfloat16 [64, 16, 8, 1536], P(('clips', 'frame'), 'row', None, 'head'), parts along dimension 0, may hold values from -6 to 6
Outputs:
- attended: bfloat16 [64, 16, 8, 1536], P(('clips', 'frame'), 'row', None, 'head'), parts along dimension 0
There are 2 independent parts, one for each index of `clips`. A program takes and returns all parts, laid end to end along the dimension named above; each array names one. Nothing has to cross between parts.
All inputs are finite; a program needn't handle non-finite values.
Results may differ from a plain program's by a relative error of at most 0.0047.
Values may be sent and summed in bfloat16 or wider, within the bound.
No kernel may reach another device: no remote copies, remote signals or barrier semaphores. Data moves between devices by JAX's collectives and lax.ppermute only.
A program may use at most 64 MiB of HBM per device.

v0:
```python
import math

import jax
import jax.numpy as jnp
from jax import lax
from jax.sharding import PartitionSpec as P

HD = 128
TF = 4
TR = 8
TC = 8


def padded(cells, sides, width):
    for axis, dim in sides:
        count = lax.axis_size(axis)
        ends = count - 1
        head = lax.slice_in_dim(cells, 0, width, axis=dim)
        tail = lax.slice_in_dim(cells, cells.shape[dim] - width, cells.shape[dim], axis=dim)
        cells = jnp.concatenate(
            [
                lax.ppermute(tail, axis, [(i, (i + 1) % count) for i in range(ends)]),
                cells,
                lax.ppermute(head, axis, [((i + 1) % count, i) for i in range(ends)]),
            ],
            axis=dim,
        )
    return cells


def per_device(query, keys, values):
    features = query.shape[3]
    columns = query.shape[2]
    heads_here = features // HD
    tile_size = TF * TR * TC
    column_tiles = columns // TC
    block_rows = column_tiles * tile_size
    score_scale = 1.0 / math.sqrt(HD)
    stacked = jnp.stack((keys, values), 0).reshape(2, 2, TF, 1, TR, columns, features)
    extended = padded(stacked, (("frame", 1), ("row", 3)), 1)
    frame_index = lax.axis_index("frame")
    row_index = lax.axis_index("row")
    frame_count = lax.axis_size("frame")
    count_of_rows = lax.axis_size("row")
    offsets = jnp.arange(3, dtype=jnp.int32) - 1
    tile_frames = 2 * frame_index + jnp.arange(2, dtype=jnp.int32)[:, None] + offsets[None, :]
    frame_ok = (tile_frames >= 0) & (tile_frames < 2 * frame_count)
    tile_rows = row_index + offsets
    row_ok = (tile_rows >= 0) & (tile_rows < count_of_rows)
    tile_mask = frame_ok[:, :, None] & row_ok[None, None, :]
    allowed = jnp.broadcast_to(tile_mask[:, None, :, :, None], (2, block_rows, 3, 3, block_rows))
    allowed = allowed.reshape(2, block_rows, 9 * block_rows)
    tiled_queries = query.reshape(2, TF, TR, column_tiles, TC, features).transpose(0, 3, 1, 2, 4, 5)
    tiled_queries = tiled_queries.reshape(2, block_rows, features)

    def one_head(head_index):
        start = head_index * HD
        head_queries = lax.dynamic_slice_in_dim(tiled_queries, start, HD, 2)
        head_grid = lax.dynamic_slice_in_dim(extended, start, HD, 6)
        key_groups = jnp.stack((head_grid[:, 0:3], head_grid[:, 1:4]), 1)
        key_groups = key_groups.reshape(2, 2, 3, TF, 3, TR, column_tiles, TC, HD)
        key_groups = key_groups.transpose(0, 1, 2, 4, 6, 3, 5, 7, 8).reshape(
            2, 2, 9 * block_rows, HD
        )
        scores = (
            jnp.einsum(
                "jyh,jvh->jyv", head_queries, key_groups[0], preferred_element_type=jnp.float32
            )
            * score_scale
        )
        scores = jnp.where(allowed, scores, -jnp.inf)
        row_peak = jnp.max(scores, axis=-1, keepdims=True)
        weights = jnp.exp(scores - row_peak)
        row_total = jnp.sum(weights, axis=-1, keepdims=True)
        rounded_length = weights.astype(jnp.bfloat16)
        summed = jnp.einsum(
            "git,gth->gih", rounded_length, key_groups[1], preferred_element_type=jnp.float32
        )
        return (summed / row_total).astype(jnp.bfloat16)

    head_results = lax.map(one_head, jnp.arange(heads_here, dtype=jnp.int32))
    attention_output = head_results.transpose(1, 2, 0, 3).reshape(
        2, column_tiles, TF, TR, TC, features
    )
    return attention_output.transpose(0, 2, 3, 1, 4, 5).reshape(2 * TF, TR, columns, features)


def solution(mesh):
    return jax.shard_map(
        per_device,
        mesh=mesh,
        in_specs=(
            P(("clips", "frame"), "row", None, "head"),
            P(("clips", "frame"), "row", None, "head"),
            P(("clips", "frame"), "row", None, "head"),
        ),
        out_specs=P(("clips", "frame"), "row", None, "head"),
        check_vma=False,
    )
```

profile of v0, /device:TPU:0, one launch (start us, length us, event | category | flops | bytes accessed | tf_op | source)
XLA Modules:
  0.0 165.6 jit_solution(2696380435267602327)
XLA Ops:
  0.0 1.6 fusion.22
  1.6 5.0 %collective-permute-start = (bf16[2,1,4,1,8,8,768]{6,5,4,2,3,1,0:T(8,128)(2,1)S(1)}, bf16[2,1,4,1,8,8,768]{6,5,4,2,3,1,0:T(8,128)(2,1)S(1)}, u32[]{:S(2)}, u32[]{:S(2)}) collective-permute-start(bf16[2,1,4,1,8,8,768]{6,5,4,2,3,1,0:T(8,128)(2,1)S(1)} %get-tuple-element.71), channel_id=1, source_target_pairs={{0,4},{4,8},{8,12},{1,5},{5,9},{9,13},{2,6},{6,10},{10,14},{3,7},{... | collective-permute-start | bytes 2359304 | tf_op jit(solution)/shard_map/ppermute | solution.py:22
  6.6 1.3 collective-permute-start.1
  7.9 15.4 %collective-permute-done = bf16[2,1,4,1,8,8,768]{6,5,4,2,3,1,0:T(8,128)(2,1)S(1)} collective-permute-done((bf16[2,1,4,1,8,8,768]{6,5,4,2,3,1,0:T(8,128)(2,1)S(1)}, bf16[2,1,4,1,8,8,768]{6,5,4,2,3,1,0:T(8,128)(2,1)S(1)}, u32[]{:S(2)}, u32[]{:S(2)}) %collective-permute-start) | collective-permute-done | bytes 786464 | tf_op jit(solution)/shard_map/ppermute | solution.py:22
  23.3 4.2 %collective-permute-done.1 = bf16[2,1,4,1,8,8,768]{6,5,4,2,3,1,0:T(8,128)(2,1)S(1)} collective-permute-done((bf16[2,1,4,1,8,8,768]{6,5,4,2,3,1,0:T(8,128)(2,1)S(1)}, bf16[2,1,4,1,8,8,768]{6,5,4,2,3,1,0:T(8,128)(2,1)S(1)}, u32[]{:S(2)}, u32[]{:S(2)}) %collective-permute-start.1) | collective-permute-done | bytes 786464 | tf_op jit(solution)/shard_map/ppermute | solution.py:24
  27.5 1.8 %pad_maximum_fusion.1 = bf16[2,4,4,1,8,8,768]{6,5,4,2,3,1,0:T(8,128)(2,1)} fusion(bf16[2,1,4,1,8,8,768]{6,5,4,2,3,1,0:T(8,128)(2,1)S(1)} %collective-permute-done.1, bf16[1,2,4,1,8,8,768]{6,5,4,2,3,1,0:T(8,128)(2,1)S(1)} %bitcast.43, bf16[1,2,4,1,8,8,768]{6,5,4,2,3,1,0:T(8,128)(2,1)S(1)} %bitcast.40, ...), kind=kLoop, calls=%fused_computation.18 | loop fusion | flops 4718592 | bytes 6291456 | tf_op jit(solution)/shard_map/concatenate | solution.py:20
  29.3 5.0 %collective-permute-start.2 = (bf16[2,4,4,1,8,8,768]{6,5,4,2,3,1,0:T(8,128)(2,1)}, bf16[2,4,4,1,8,8,768]{6,5,4,2,3,1,0:T(8,128)(2,1)}, u32[]{:S(2)}, u32[]{:S(2)}) collective-permute-start(bf16[2,4,4,1,8,8,768]{6,5,4,2,3,1,0:T(8,128)(2,1)} %pad_maximum_fusion.1), channel_id=1, source_target_pairs={{0,2},{1,3},{4,6},{5,7},{8,10},{9,11},{12,14},{13,15},{16,18},{17,... | collective-permute-start | bytes 9437192 | tf_op jit(solution)/shard_map/ppermute | solution.py:22
  34.4 1.3 collective-permute-start.3
  36.0 63.2 %collective-permute-done.2 = bf16[2,4,4,1,8,8,768]{6,5,4,2,3,1,0:T(8,128)(2,1)} collective-permute-done((bf16[2,4,4,1,8,8,768]{6,5,4,2,3,1,0:T(8,128)(2,1)}, bf16[2,4,4,1,8,8,768]{6,5,4,2,3,1,0:T(8,128)(2,1)}, u32[]{:S(2)}, u32[]{:S(2)}) %collective-permute-start.2) | collective-permute-done | bytes 3145760 | tf_op jit(solution)/shard_map/ppermute | solution.py:22
  99.2 5.7 %collective-permute-done.3 = bf16[2,4,4,1,8,8,768]{6,5,4,2,3,1,0:T(8,128)(2,1)} collective-permute-done((bf16[2,4,4,1,8,8,768]{6,5,4,2,3,1,0:T(8,128)(2,1)}, bf16[2,4,4,1,8,8,768]{6,5,4,2,3,1,0:T(8,128)(2,1)}, u32[]{:S(2)}, u32[]{:S(2)}) %collective-permute-start.3) | collective-permute-done | bytes 3145760 | tf_op jit(solution)/shard_map/ppermute | solution.py:24
  104.9 7.0 %pad_maximum_fusion = bf16[2,4,4,3,8,8,768]{6,5,4,2,3,1,0:T(8,128)(2,1)} fusion(bf16[2,4,4,1,8,8,768]{6,5,4,2,3,1,0:T(8,128)(2,1)} %collective-permute-done.3, bf16[2,1,4,1,8,8,768]{6,5,4,2,3,1,0:T(8,128)(2,1)S(1)} %collective-permute-done.1, bf16[1,2,4,1,8,8,768]{6,5,4,2,3,1,0:T(8,128)(2,1)S(1)} %bitcast.44, ...), kind=kLoop, calls=%fused_computation.17 | loop fusion | flops 23592960 | bytes 18874368 | tf_op jit(solution)/shard_map/concatenate | solution.py:20
  111.9 50.2 %while.11 = (s32[]{:T(128)}, bf16[6,2,256,128]{3,2,1,0:T(8,128)(2,1)}, s32[6]{0:T(128)S(1)}, bf16[2,256,768]{2,1,0:T(8,128)(2,1)}, bf16[2,4,4,3,8,8,768]{6,5,4,2...) while((s32[]{:T(128)}, ...), condition=%wide.region_3.4_spmd.clone, body=%wide.region_0.3_spmd.clone.sunk | while | flops 613547008 | bytes 30948544 | solution.py:81
  111.9 0.6 dynamic_slice.20
  113.1 2.2 %dynamic-slice_bitcast_fusion.3 = (bf16[2,1,3,4,3,8,8,128]{7,6,5,3,4,2,0,1:T(8,128)(2,1)S(1)}, bf16[2,1,3,4,3,8,8,128]{7,6,5,3,4,2,0,1:T(8,128)(2,1)S(1)}) fusion(bf16[2,4,4,3,8,8,768]{6,5,4,2,3,1,0:T(8,128)(2,1)} %get-tuple-element.148, s32[]{:T(128)S(6)} %select_n.12, s32[]{:T(128)S(6)} %add.76), kind=kLoop, calls=%fused_computation.10.clone.1 | loop fusion | bytes 4718600 | tf_op jit(solution)/shard_map/while/body/eval_jaxpr/stack | solution.py:60
  115.5 0.6 fusion.37
  116.1 1.8 %fusion.38 = (f32[2,256]{1,0:T(2,128)S(1)}, f32[2,256,2304]{2,1,0:T(8,128)S(1)}) fusion(bf16[2,2304,128]{2,1,0:T(8,128)(2,1)S(1)} %bitcast.37, bf16[2,256,768]{2,1,0:T(8,128)(2,1)} %get-tuple-element.147, s32[]{:T(128)S(6)} %select_n.12, pred[2,2304]{1,0:T(4,128)(4,1)S(1)} %get-tuple-element.149), kind=kOutput, calls=%fused_computation.29.clone.1 | convolution fusion | flops 305528320 | bytes 6035972 | tf_op jit(solution)/shard_map/while/body/eval_jaxpr/jyh,jvh->jyv/dot_general | solution.py:66
  117.9 0.8 fusion.39
  118.7 1.6 fusion.40
  120.3 0.6 dynamic_slice.20
  121.4 2.2 %dynamic-slice_bitcast_fusion.3 = (bf16[2,1,3,4,3,8,8,128]{7,6,5,3,4,2,0,1:T(8,128)(2,1)S(1)}, bf16[2,1,3,4,3,8,8,128]{7,6,5,3,4,2,0,1:T(8,128)(2,1)S(1)}) fusion(bf16[2,4,4,3,8,8,768]{6,5,4,2,3,1,0:T(8,128)(2,1)} %get-tuple-element.148, s32[]{:T(128)S(6)} %select_n.12, s32[]{:T(128)S(6)} %add.76), kind=kLoop, calls=%fused_computation.10.clone.1 | loop fusion | bytes 4718600 | tf_op jit(solution)/shard_map/while/body/eval_jaxpr/stack | solution.py:60
  123.8 0.6 fusion.37
  124.4 1.8 %fusion.38 = (f32[2,256]{1,0:T(2,128)S(1)}, f32[2,256,2304]{2,1,0:T(8,128)S(1)}) fusion(bf16[2,2304,128]{2,1,0:T(8,128)(2,1)S(1)} %bitcast.37, bf16[2,256,768]{2,1,0:T(8,128)(2,1)} %get-tuple-element.147, s32[]{:T(128)S(6)} %select_n.12, pred[2,2304]{1,0:T(4,128)(4,1)S(1)} %get-tuple-element.149), kind=kOutput, calls=%fused_computation.29.clone.1 | convolution fusion | flops 305528320 | bytes 6035972 | tf_op jit(solution)/shard_map/while/body/eval_jaxpr/jyh,jvh->jyv/dot_general | solution.py:66
  126.2 0.8 fusion.39
  127.0 1.6 fusion.40
  128.6 0.6 dynamic_slice.20
  129.8 2.2 %dynamic-slice_bitcast_fusion.3 = (bf16[2,1,3,4,3,8,8,128]{7,6,5,3,4,2,0,1:T(8,128)(2,1)S(1)}, bf16[2,1,3,4,3,8,8,128]{7,6,5,3,4,2,0,1:T(8,128)(2,1)S(1)}) fusion(bf16[2,4,4,3,8,8,768]{6,5,4,2,3,1,0:T(8,128)(2,1)} %get-tuple-element.148, s32[]{:T(128)S(6)} %select_n.12, s32[]{:T(128)S(6)} %add.76), kind=kLoop, calls=%fused_computation.10.clone.1 | loop fusion | bytes 4718600 | tf_op jit(solution)/shard_map/while/body/eval_jaxpr/stack | solution.py:60
  132.2 0.6 fusion.37
  132.8 1.8 %fusion.38 = (f32[2,256]{1,0:T(2,128)S(1)}, f32[2,256,2304]{2,1,0:T(8,128)S(1)}) fusion(bf16[2,2304,128]{2,1,0:T(8,128)(2,1)S(1)} %bitcast.37, bf16[2,256,768]{2,1,0:T(8,128)(2,1)} %get-tuple-element.147, s32[]{:T(128)S(6)} %select_n.12, pred[2,2304]{1,0:T(4,128)(4,1)S(1)} %get-tuple-element.149), kind=kOutput, calls=%fused_computation.29.clone.1 | convolution fusion | flops 305528320 | bytes 6035972 | tf_op jit(solution)/shard_map/while/body/eval_jaxpr/jyh,jvh->jyv/dot_general | solution.py:66
  134.6 0.8 fusion.39
  135.4 1.6 fusion.40
  137.0 0.6 dynamic_slice.20
  138.1 2.2 %dynamic-slice_bitcast_fusion.3 = (bf16[2,1,3,4,3,8,8,128]{7,6,5,3,4,2,0,1:T(8,128)(2,1)S(1)}, bf16[2,1,3,4,3,8,8,128]{7,6,5,3,4,2,0,1:T(8,128)(2,1)S(1)}) fusion(bf16[2,4,4,3,8,8,768]{6,5,4,2,3,1,0:T(8,128)(2,1)} %get-tuple-element.148, s32[]{:T(128)S(6)} %select_n.12, s32[]{:T(128)S(6)} %add.76), kind=kLoop, calls=%fused_computation.10.clone.1 | loop fusion | bytes 4718600 | tf_op jit(solution)/shard_map/while/body/eval_jaxpr/stack | solution.py:60
  140.6 0.6 fusion.37
  141.2 1.8 %fusion.38 = (f32[2,256]{1,0:T(2,128)S(1)}, f32[2,256,2304]{2,1,0:T(8,128)S(1)}) fusion(bf16[2,2304,128]{2,1,0:T(8,128)(2,1)S(1)} %bitcast.37, bf16[2,256,768]{2,1,0:T(8,128)(2,1)} %get-tuple-element.147, s32[]{:T(128)S(6)} %select_n.12, pred[2,2304]{1,0:T(4,128)(4,1)S(1)} %get-tuple-element.149), kind=kOutput, calls=%fused_computation.29.clone.1 | convolution fusion | flops 305528320 | bytes 6035972 | tf_op jit(solution)/shard_map/while/body/eval_jaxpr/jyh,jvh->jyv/dot_general | solution.py:66
  143.0 0.8 fusion.39
  143.8 1.6 fusion.40
  145.4 0.6 dynamic_slice.20
  146.5 2.2 %dynamic-slice_bitcast_fusion.3 = (bf16[2,1,3,4,3,8,8,128]{7,6,5,3,4,2,0,1:T(8,128)(2,1)S(1)}, bf16[2,1,3,4,3,8,8,128]{7,6,5,3,4,2,0,1:T(8,128)(2,1)S(1)}) fusion(bf16[2,4,4,3,8,8,768]{6,5,4,2,3,1,0:T(8,128)(2,1)} %get-tuple-element.148, s32[]{:T(128)S(6)} %select_n.12, s32[]{:T(128)S(6)} %add.76), kind=kLoop, calls=%fused_computation.10.clone.1 | loop fusion | bytes 4718600 | tf_op jit(solution)/shard_map/while/body/eval_jaxpr/stack | solution.py:60
  149.6 1.8 %fusion.38 = (f32[2,256]{1,0:T(2,128)S(1)}, f32[2,256,2304]{2,1,0:T(8,128)S(1)}) fusion(bf16[2,2304,128]{2,1,0:T(8,128)(2,1)S(1)} %bitcast.37, bf16[2,256,768]{2,1,0:T(8,128)(2,1)} %get-tuple-element.147, s32[]{:T(128)S(6)} %select_n.12, pred[2,2304]{1,0:T(4,128)(4,1)S(1)} %get-tuple-element.149), kind=kOutput, calls=%fused_computation.29.clone.1 | convolution fusion | flops 305528320 | bytes 6035972 | tf_op jit(solution)/shard_map/while/body/eval_jaxpr/jyh,jvh->jyv/dot_general | solution.py:66
  151.4 0.8 fusion.39
  152.1 1.6 fusion.40
  153.8 0.6 dynamic_slice.20
  154.9 2.2 %dynamic-slice_bitcast_fusion.3 = (bf16[2,1,3,4,3,8,8,128]{7,6,5,3,4,2,0,1:T(8,128)(2,1)S(1)}, bf16[2,1,3,4,3,8,8,128]{7,6,5,3,4,2,0,1:T(8,128)(2,1)S(1)}) fusion(bf16[2,4,4,3,8,8,768]{6,5,4,2,3,1,0:T(8,128)(2,1)} %get-tuple-element.148, s32[]{:T(128)S(6)} %select_n.12, s32[]{:T(128)S(6)} %add.76), kind=kLoop, calls=%fused_computation.10.clone.1 | loop fusion | bytes 4718600 | tf_op jit(solution)/shard_map/while/body/eval_jaxpr/stack | solution.py:60
  158.0 1.8 %fusion.38 = (f32[2,256]{1,0:T(2,128)S(1)}, f32[2,256,2304]{2,1,0:T(8,128)S(1)}) fusion(bf16[2,2304,128]{2,1,0:T(8,128)(2,1)S(1)} %bitcast.37, bf16[2,256,768]{2,1,0:T(8,128)(2,1)} %get-tuple-element.147, s32[]{:T(128)S(6)} %select_n.12, pred[2,2304]{1,0:T(4,128)(4,1)S(1)} %get-tuple-element.149), kind=kOutput, calls=%fused_computation.29.clone.1 | convolution fusion | flops 305528320 | bytes 6035972 | tf_op jit(solution)/shard_map/while/body/eval_jaxpr/jyh,jvh->jyv/dot_general | solution.py:66
  159.7 0.8 fusion.39
  160.5 1.6 fusion.40
  162.2 1.7 %copy.5 = bf16[2,256,6,128]{3,2,1,0:T(8,128)(2,1)S(1)} copy(bf16[2,256,6,128]{3,1,0,2:T(8,128)(2,1)} %bitcast.45) | data formatting | bytes 1572864 | tf_op jit(solution)/shard_map/transpose | solution.py:82
  163.8 1.8 %reshape_transpose_reshape.7 = bf16[8,8,8,768]{3,2,1,0:T(8,128)(2,1)} reshape(bf16[2,256,6,128]{3,2,1,0:T(8,128)(2,1)S(1)} %copy.5) | data formatting | bytes 1572864 | tf_op jit(solution)/shard_map/reshape;transpose;reshape | solution.py:85
  (21 shorter events, 2.8 us)
Async XLA Ops:
  0.0 27.5 %copy-start = (bf16[8,8,8,768]{3,2,1,0:T(8,128)(2,1)S(1)}, bf16[8,8,8,768]{3,2,1,0:T(8,128)(2,1)}, u32[]{:S(2)}) copy-start(bf16[8,8,8,768]{3,2,1,0:T(8,128)(2,1)} %param.6) | copy-start | bytes 2359300
  0.0 27.5 %copy-start.1 = (bf16[8,8,8,768]{3,2,1,0:T(8,128)(2,1)S(1)}, bf16[8,8,8,768]{3,2,1,0:T(8,128)(2,1)}, u32[]{:S(2)}) copy-start(bf16[8,8,8,768]{3,2,1,0:T(8,128)(2,1)} %param.7) | copy-start | bytes 2359300
  1.6 21.7 %collective-permute-start = (bf16[2,1,4,1,8,8,768]{6,5,4,2,3,1,0:T(8,128)(2,1)S(1)}, bf16[2,1,4,1,8,8,768]{6,5,4,2,3,1,0:T(8,128)(2,1)S(1)}, u32[]{:S(2)}, u32[]{:S(2)}) collective-permute-start(bf16[2,1,4,1,8,8,768]{6,5,4,2,3,1,0:T(8,128)(2,1)S(1)} %get-tuple-element.71), channel_id=1, source_target_pairs={{0,4},{4,8},{8,12},{1,5},{5,9},{9,13},{2,6},{6,10},{10,14},{3,7},{... | collective-permute-start | bytes 2359304 | tf_op jit(solution)/shard_map/ppermute | solution.py:22
  6.6 20.9 %collective-permute-start.1 = (bf16[2,1,4,1,8,8,768]{6,5,4,2,3,1,0:T(8,128)(2,1)S(1)}, bf16[2,1,4,1,8,8,768]{6,5,4,2,3,1,0:T(8,128)(2,1)S(1)}, u32[]{:S(2)}, u32[]{:S(2)}) collective-permute-start(bf16[2,1,4,1,8,8,768]{6,5,4,2,3,1,0:T(8,128)(2,1)S(1)} %get-tuple-element.72), channel_id=1, source_target_pairs={{4,0},{8,4},{12,8},{5,1},{9,5},{13,9},{6,2},{10,6},{14,10},{7,3},{... | collective-permute-start | bytes 2359304 | tf_op jit(solution)/shard_map/ppermute | solution.py:24
  29.3 69.9 %collective-permute-start.2 = (bf16[2,4,4,1,8,8,768]{6,5,4,2,3,1,0:T(8,128)(2,1)}, bf16[2,4,4,1,8,8,768]{6,5,4,2,3,1,0:T(8,128)(2,1)}, u32[]{:S(2)}, u32[]{:S(2)}) collective-permute-start(bf16[2,4,4,1,8,8,768]{6,5,4,2,3,1,0:T(8,128)(2,1)} %pad_maximum_fusion.1), channel_id=1, source_target_pairs={{0,2},{1,3},{4,6},{5,7},{8,10},{9,11},{12,14},{13,15},{16,18},{17,... | collective-permute-start | bytes 9437192 | tf_op jit(solution)/shard_map/ppermute | solution.py:22
  34.4 70.6 %collective-permute-start.3 = (bf16[2,4,4,1,8,8,768]{6,5,4,2,3,1,0:T(8,128)(2,1)}, bf16[2,4,4,1,8,8,768]{6,5,4,2,3,1,0:T(8,128)(2,1)}, u32[]{:S(2)}, u32[]{:S(2)}) collective-permute-start(bf16[2,4,4,1,8,8,768]{6,5,4,2,3,1,0:T(8,128)(2,1)} %pad_maximum_fusion.1), channel_id=1, source_target_pairs={{2,0},{3,1},{6,4},{7,5},{10,8},{11,9},{14,12},{15,13},{18,16},{19,... | collective-permute-start | bytes 9437192 | tf_op jit(solution)/shard_map/ppermute | solution.py:24
where the time goes:
time: 166 us
  waiting for transfers between devices  88.6 us (53%)
  local copies, waits for them, and re-layouts  23.7 us (14%)
  matrix products  20.5 us (12%)
  other arithmetic  16.6 us (10%)
  starting transfers between devices  12.6 us (8%)
  loops' own time  3.57 us (2%)
    ppermute x2, waiting for transfers between devices, padded(): lax.ppermute(tail, axis, [(i, (i + 1) % count) for i in range(ends)])  78.7 us
    another operation x6, local copies, waits for them, and re-layouts, one_head(): key_groups = jnp.stack((head_grid[:, 0:3], head_grid[:, 1:4]), 1)  13.2 us
    dot_general x6, matrix products, one_head(): jnp.einsum('jyh,jvh->jyv', head_queries, key_groups[0], preferred_element...  10.8 us
    ppermute x2, starting transfers between devices, padded(): lax.ppermute(tail, axis, [(i, (i + 1) % count) for i in range(ends)])  10 us
    ppermute x2, waiting for transfers between devices, padded(): lax.ppermute(head, axis, [((i + 1) % count, i) for i in range(ends)])  9.9 us
    dot_general x6, matrix products, one_head(): jnp.einsum('git,gth->gih', rounded_length, key_groups[1], preferred_eleme...  9.7 us
    concatenate x2, other arithmetic, padded(): jnp.concatenate([lax.ppermute(tail, axis, [(i, (i + 1) % count) for i in...  8.82 us
    reduce_sum x6, other arithmetic, one_head(): row_total = jnp.sum(weights, axis=-1, keepdims=True)  4.71 us
  transfers between devices with their start and end apart: 4, of which 4 were waited for; matrix products, arithmetic and copies ran while one was open for 0% of the time, Pallas kernels for 0%

commit v1 on v0

v1 whole, which is shorter than its diff:
```python
import functools
import math

import jax
import jax.numpy as jnp
from jax import lax
from jax.experimental import pallas as pl
from jax.experimental.pallas import tpu as pltpu
from jax.sharding import PartitionSpec as P

HD = 128
TF = 4
TR = 8
TC = 8
TILE = TF * TR * TC
ROWS = 2 * TILE
EXPONENT = math.log2(math.e) / math.sqrt(HD)
NT = (((1,), (1,)), ((), ()))
NN = (((1,), (0,)), ((), ()))
STAT_ROWS = 3 * 8 * ROWS // HD
CHUNKS = (2, 4)


def dot(a, b, dims):
    return lax.dot_general(a, b, dims, preferred_element_type=jnp.float32)


def attend(q, k, v, before, after):
    place = lax.axis_index("frame")
    present = (place > 0, place < lax.axis_size("frame") - 1)
    outs, logs = [], []
    for t, side in enumerate((before, after)):
        qt = q[t * TILE : (t + 1) * TILE]
        k_side = jnp.where(present[t], side[:TILE], k[:TILE])
        v_side = side[TILE:]
        s_own = dot(qt, k, NT)
        s_side = dot(qt, k_side, NT)
        peak = jnp.maximum(
            jnp.max(s_own, axis=1, keepdims=True), jnp.max(s_side, axis=1, keepdims=True)
        )
        w_own = jnp.exp2((s_own - peak) * EXPONENT)
        w_side = jnp.exp2((s_side - peak) * EXPONENT)
        counted = jnp.where(present[t], 1.0, 0.0)
        total = jnp.sum(w_own, axis=1, keepdims=True) + counted * jnp.sum(
            w_side, axis=1, keepdims=True
        )
        summed = dot(w_own.astype(jnp.bfloat16), v, NN) + dot(
            w_side.astype(jnp.bfloat16), v_side, NN
        )
        outs.append(summed * (1.0 / total))
        logs.append(peak * EXPONENT + jnp.log2(total))
    return jnp.concatenate(outs, 0), jnp.concatenate(logs, 0)


def put_column(ref, j, column):
    lanes = lax.broadcasted_iota(jnp.int32, ref.shape, 1)
    ref[...] = jnp.where(lanes == j, column, ref[...])


def pack_logs(logs):
    flat = logs.T[:8]
    parts = []
    for _ in range(3):
        part = flat.astype(jnp.bfloat16).astype(jnp.float32)
        flat = flat - part
        parts += [part[:, i : i + HD] for i in range(0, ROWS, HD)]
    return jnp.concatenate(parts, 0).astype(jnp.bfloat16)


def unpack_logs(packed):
    parts = packed.astype(jnp.float32)
    third = STAT_ROWS // 3
    flat = parts[:third] + parts[third : 2 * third] + parts[2 * third :]
    flat = jnp.concatenate([flat[i : i + 8] for i in range(0, third, 8)], 1)
    return jnp.concatenate([flat, jnp.zeros((HD - 8, ROWS), jnp.float32)], 0).T


def remote_kernel(heads, q, k, v, before, after, out, logs):
    j = pl.program_id(0)

    @pl.when(j == 0)
    def _():
        logs[...] = jnp.zeros_like(logs)

    o, log = attend(q[...], k[...], v[...], before[...], after[...])
    out[pl.ds(pl.multiple_of(j * ROWS, ROWS), ROWS), :] = o.astype(out.dtype)
    put_column(logs, j, log)

    @pl.when(j == heads - 1)
    def _():
        out[heads * ROWS :, :] = pack_logs(logs[...])


def local_kernel(splits, q, k, v, *rest):
    sides, (out, logs) = rest[:-2], rest[-2:]
    j = pl.program_id(0)

    @pl.when(j == 0)
    def _():
        logs[...] = jnp.zeros_like(logs)

    start = 0
    for c, heads in enumerate(splits):
        @pl.when((j >= start) & (j < start + heads))
        def _(c=c):
            o, log = attend(q[...], k[...], v[...], sides[2 * c][...], sides[2 * c + 1][...])
            out[...] = o
            put_column(logs, j, log)

        start += heads


def combine_kernel(first, heads, groups, own, logs, *rest):
    theirs, out, columns = rest[:groups], rest[-2], rest[-1]
    j = pl.program_id(0)
    place = lax.axis_index("row")
    if groups == 1:
        there = (None,)
    else:
        there = (place < lax.axis_size("row") - 1, place > 0)

    @pl.when(j == 0)
    def _():
        for g in range(groups):
            got = unpack_logs(theirs[g][heads * ROWS :, :])
            if there[g] is not None:
                got = jnp.where(there[g], got, -jnp.inf)
            columns[g] = got

    lanes = lax.broadcasted_iota(jnp.int32, (ROWS, HD), 1)

    def column(block, at):
        return jnp.sum(jnp.where(lanes == at, block, 0.0), axis=1, keepdims=True)

    own_log = column(logs[...], first + j)
    their_logs = [column(columns[g], j) for g in range(groups)]
    top = functools.reduce(jnp.maximum, their_logs, own_log)
    weight = jnp.exp2(own_log - top)
    total = weight
    summed = weight * own[...]
    for g in range(groups):
        weight = jnp.exp2(their_logs[g] - top)
        total = total + weight
        block = theirs[g][pl.ds(pl.multiple_of(j * ROWS, ROWS), ROWS), :]
        summed = summed + weight * block.astype(jnp.float32)
    out[...] = (summed * (1.0 / total)).astype(out.dtype)


def cost(heads, tiles=6):
    pairs = heads * tiles * TILE * TILE
    return pl.CostEstimate(flops=4 * pairs * HD, bytes_accessed=heads * 8 * ROWS * HD, transcendentals=pairs)


def head_block(shift=0):
    return pl.BlockSpec((ROWS, HD), lambda j: (0, j + shift))


def whole_block(shape):
    return pl.BlockSpec(shape, lambda j: (0,) * len(shape))


def remote_part(first, heads, q, k, v, before, after):
    shape = (heads * ROWS + STAT_ROWS, HD)
    return pl.pallas_call(
        functools.partial(remote_kernel, heads),
        grid=(heads,),
        in_specs=[head_block(), head_block(first), head_block(first), head_block(), head_block()],
        out_specs=whole_block(shape),
        out_shape=jax.ShapeDtypeStruct(shape, jnp.bfloat16),
        scratch_shapes=[pltpu.VMEM((ROWS, HD), jnp.float32)],
        compiler_params=pltpu.CompilerParams(vmem_limit_bytes=32 * 1024 * 1024),
        cost_estimate=cost(heads),
        name="remote_part",
    )(q, k, v, before, after)


def local_part(splits, q, k, v, sides):
    heads = sum(splits)
    specs, start = [], 0
    for count in splits:
        spec = pl.BlockSpec(
            (ROWS, HD), lambda j, s=start, n=count: (0, jnp.clip(j - s, 0, n - 1))
        )
        specs += [spec, spec]
        start += count
    return pl.pallas_call(
        functools.partial(local_kernel, splits),
        grid=(heads,),
        in_specs=[head_block()] * 3 + specs,
        out_specs=[head_block(), whole_block((ROWS, HD))],
        out_shape=[
            jax.ShapeDtypeStruct((ROWS, heads * HD), jnp.float32),
            jax.ShapeDtypeStruct((ROWS, HD), jnp.float32),
        ],
        compiler_params=pltpu.CompilerParams(vmem_limit_bytes=32 * 1024 * 1024),
        cost_estimate=cost(heads),
        name="local_part",
    )(q, k, v, *sides)


def combine_part(first, heads, own, logs, theirs, width, prior):
    groups = len(theirs)
    specs = [head_block(first), whole_block((ROWS, HD))] + [whole_block(t.shape) for t in theirs]
    operands = [own, logs, *theirs]
    aliases = {}
    if prior is not None:
        specs.append(pl.BlockSpec(memory_space=pl.ANY))
        aliases = {len(operands): 0}
        operands.append(prior)
    return pl.pallas_call(
        functools.partial(combine_kernel, first, heads, groups),
        grid=(heads,),
        in_specs=specs,
        out_specs=head_block(first),
        out_shape=jax.ShapeDtypeStruct((ROWS, width), jnp.bfloat16),
        scratch_shapes=[pltpu.VMEM((groups, ROWS, HD), jnp.float32)],
        input_output_aliases=aliases,
        compiler_params=pltpu.CompilerParams(vmem_limit_bytes=32 * 1024 * 1024),
        cost_estimate=pl.CostEstimate(
            flops=8 * heads * ROWS * HD, bytes_accessed=heads * 8 * ROWS * HD, transcendentals=0
        ),
        name="combine_part",
    )(*operands)


def per_device(query, keys, values):
    features = query.shape[3]
    heads = features // HD
    splits = CHUNKS if sum(CHUNKS) == heads else (heads,)
    q = query.reshape(ROWS, features)
    k = keys.reshape(ROWS, features)
    v = values.reshape(ROWS, features)
    frames = lax.axis_size("frame")
    rows = lax.axis_size("row")
    later = [(i, i + 1) for i in range(frames - 1)]
    sooner = [(i + 1, i) for i in range(frames - 1)]
    if rows == 2:
        routes = [([(0, 1), (1, 0)], [(0, 1), (1, 0)])]
    else:
        down = [(i, i + 1) for i in range(rows - 1)]
        up = [(i + 1, i) for i in range(rows - 1)]
        routes = [(down, up), (up, down)]

    bounds, start = [], 0
    for count in splits:
        bounds.append((start, start + count))
        start += count

    got_q, sides = [], []
    for a, b in bounds:
        a, b = a * HD, b * HD
        got_q.append([lax.ppermute(q[:, a:b], "row", there) for there, _ in routes])
        tail = jnp.concatenate([k[TILE:, a:b], v[TILE:, a:b]], 0)
        head = jnp.concatenate([k[:TILE, a:b], v[:TILE, a:b]], 0)
        sides.append((lax.ppermute(tail, "frame", later), lax.ppermute(head, "frame", sooner)))

    answers = []
    for (a, b), chunk_q, (before, after) in zip(bounds, got_q, sides):
        parts = [remote_part(a, b - a, one, k, v, before, after) for one in chunk_q]
        answers.append(parts)

    q_local, _ = lax.optimization_barrier((q, answers[-1]))
    own, logs = local_part(splits, q_local, k, v, [s for pair in sides for s in pair])

    out = None
    for (a, b), parts in zip(bounds, answers):
        theirs = [lax.ppermute(p, "row", back) for p, (_, back) in zip(parts, routes)]
        out = combine_part(a, b - a, own, logs, theirs, features, out)
    return out.reshape(query.shape)


def solution(mesh):
    spec = P(("clips", "frame"), "row", None, "head")
    return jax.shard_map(
        per_device, mesh=mesh, in_specs=(spec,) * 3, out_specs=spec, check_vma=False
    )
```

time: 166 us -> 50 us (0.30)
  waiting for transfers between devices: 88.6 us -> 11.4 us
  local copies, waits for them, and re-layouts: 23.7 us -> 1.36 us
  matrix products: 20.5 us -> 0 us
  Pallas kernels: 0 us -> 19.3 us
  other arithmetic: 16.6 us -> 0.11 us
  starting transfers between devices: 12.6 us -> 17.4 us
  loops' own time: 3.57 us -> 0 us
    ppermute x4 -> x8, waiting for transfers between devices: 88.6 us -> 11.4 us  [the longest x2 5.09 us: per_device(): lax.ppermute(p, 'row', back)]
    dot_general x12 -> x0, matrix products: 20.5 us -> none  [the longest x6 10.8 us: one_head(): jnp.einsum('jyh,jvh->jyv', head_queries, key_groups[0], preferred_element...]
    pallas_call x0 -> x5, Pallas kernels: none -> 19.3 us  [the longest x1 7.88 us: local_part(): pl.pallas_call(functools.partial(local_kernel, splits), grid=(heads,), in...]
    another operation x7 -> x0, local copies, waits for them, and re-layouts: 14.9 us -> none  [the longest x6 13.2 us: one_head(): key_groups = jnp.stack((head_grid[:, 0:3], head_grid[:, 1:4]), 1)]
    concatenate x2 -> x4, other arithmetic: 8.82 us -> 0.11 us  [the longest x2 0.06 us: per_device(): tail = jnp.concatenate([k[TILE:, a:b], v[TILE:, a:b]], 0)]
    ppermute x4 -> x8, starting transfers between devices: 12.6 us -> 17.4 us  [the longest x2 9.65 us: per_device(): lax.ppermute(tail, 'frame', later)]
    reduce_sum x6 -> x0, other arithmetic: 4.71 us -> none  [one_head(): row_total = jnp.sum(weights, axis=-1, keepdims=True)]
    another operation x1 -> x0, loops' own time: 3.57 us -> none  [per_device(): head_results = lax.map(one_head, jnp.arange(heads_here, dtype=jnp.int32))]
  transfers between devices with their start and end apart: 4 -> 8, of which waited for: 4 -> 3; matrix products, arithmetic and copies ran while one was open for 0% -> 0% of each run, Pallas kernels for 0% -> 34%
where the time goes in v1:
time: 50 us; the launch traced here: 49.8 us
  Pallas kernels  19.3 us (39%)
  starting transfers between devices  17.4 us (35%)
  waiting for transfers between devices  11.4 us (23%)
  local copies, waits for them, and re-layouts  1.36 us (3%)
    ppermute x2, starting transfers between devices, per_device(): lax.ppermute(tail, 'frame', later)  9.65 us
    pallas_call x1, Pallas kernels, local_part(): pl.pallas_call(functools.partial(local_kernel, splits), grid=(heads,), in...  7.88 us
    pallas_call x2, Pallas kernels, remote_part(): pl.pallas_call(functools.partial(remote_kernel, heads), grid=(heads,), in...  7.68 us
    ppermute x2, waiting for transfers between devices, per_device(): lax.ppermute(p, 'row', back)  5.09 us
    pallas_call x2, Pallas kernels, combine_part(): pl.pallas_call(functools.partial(combine_kernel, first, heads, groups), g...  3.72 us
    ppermute x2, waiting for transfers between devices, per_device(): lax.ppermute(tail, 'frame', later)  3.33 us
    ppermute x2, starting transfers between devices, per_device(): got_q.append([lax.ppermute(q[:, a:b], 'row', there) for there, _ in routes])  3.05 us
    ppermute x2, waiting for transfers between devices, per_device(): lax.ppermute(head, 'frame', sooner)  3.02 us
  transfers between devices with their start and end apart: 8, of which 3 were waited for; matrix products, arithmetic and copies ran while one was open for 0% of the time, Pallas kernels for 34%

profile of v1, /device:TPU:0, one launch (start us, length us, event | category | flops | bytes accessed | tf_op | source)
XLA Modules:
  0.0 49.8 jit_solution(1496609195524737776)
XLA Ops:
  0.0 1.3 %fusion.2 = (bf16[256,512]{1,0:T(8,128)(2,1)S(1)}, bf16[256,512]{1,0:T(8,128)(2,1)S(1)}, bf16[256,512]{1,0:T(8,128)(2,1)S(1)}, bf16[256,512]{1,0:T(8,128)(2,1)S(1)}) fusion(bf16[512,768]{1,0:T(8,128)(2,1)} %bitcast.4, bf16[512,768]{1,0:T(8,128)(2,1)} %bitcast.9), kind=kLoop, calls=%fused_computation.6 | loop fusion | bytes 2097152 | tf_op jit(solution)/shard_map/slice | solution.py:254
  1.3 0.0 copy-start.2
  1.3 0.0 copy-start
  1.3 0.0 copy-start.1
  1.3 5.1 %collective-permute-start.1 = (bf16[512,512]{1,0:T(8,128)(2,1)S(1)}, bf16[512,512]{1,0:T(8,128)(2,1)S(1)}, u32[]{:S(2)}, u32[]{:S(2)}) collective-permute-start(bf16[512,512]{1,0:T(8,128)(2,1)S(1)} %pad_maximum_fusion), channel_id=1, source_target_pairs={{0,4},{4,8},{8,12},{1,5},{5,9},{9,13},{2,6},{6,10},{10,14},{3,7},{... | collective-permute-start | bytes 1572872 | tf_op jit(solution)/shard_map/ppermute | solution.py:255
  6.5 1.3 %collective-permute-start.2 = (bf16[512,512]{1,0:T(8,128)(2,1)S(1)}, bf16[512,512]{1,0:T(8,128)(2,1)S(1)}, u32[]{:S(2)}, u32[]{:S(2)}) collective-permute-start(bf16[512,512]{1,0:T(8,128)(2,1)S(1)} %pad_maximum_fusion.1), channel_id=1, source_target_pairs={{4,0},{8,4},{12,8},{5,1},{9,5},{13,9},{6,2},{10,6},{14,10},{7,3},{... | collective-permute-start | bytes 1572872 | tf_op jit(solution)/shard_map/ppermute | solution.py:255
  7.8 0.0 copy-done.2
  7.8 1.6 %collective-permute-start = (bf16[512,512]{1,0:T(8,128)(2,1)S(1)}, bf16[512,512]{1,0:T(8,128)(2,1)S(1)}, u32[]{:S(2)}, u32[]{:S(2)}) collective-permute-start(bf16[512,512]{1,0:T(8,128)(2,1)S(1)} %slice.40), channel_id=1, source_target_pairs={{0,2},{2,0},{1,3},{3,1},{4,6},{6,4},{5,7},{7,5},{8,10},{10,8},{9,1... | collective-permute-start | bytes 1572872 | tf_op jit(solution)/shard_map/ppermute | solution.py:252
  9.4 0.0 copy-done
  9.4 0.0 copy-done.1
  9.5 4.6 %collective-permute-start.3 = (bf16[512,256]{1,0:T(8,128)(2,1)S(1)}, bf16[512,256]{1,0:T(8,128)(2,1)S(1)}, u32[]{:S(2)}, u32[]{:S(2)}) collective-permute-start(bf16[512,256]{1,0:T(8,128)(2,1)S(1)} %pad_maximum_fusion.2), channel_id=1, source_target_pairs={{0,4},{4,8},{8,12},{1,5},{5,9},{9,13},{2,6},{6,10},{10,14},{3,7},{... | collective-permute-start | bytes 786440 | tf_op jit(solution)/shard_map/ppermute | solution.py:255
  14.1 1.3 %collective-permute-start.4 = (bf16[512,256]{1,0:T(8,128)(2,1)S(1)}, bf16[512,256]{1,0:T(8,128)(2,1)S(1)}, u32[]{:S(2)}, u32[]{:S(2)}) collective-permute-start(bf16[512,256]{1,0:T(8,128)(2,1)S(1)} %pad_maximum_fusion.3), channel_id=1, source_target_pairs={{4,0},{8,4},{12,8},{5,1},{9,5},{13,9},{6,2},{10,6},{14,10},{7,3},{... | collective-permute-start | bytes 786440 | tf_op jit(solution)/shard_map/ppermute | solution.py:255
  15.4 3.3 %collective-permute-done.1.before.rest_2_ = bf16[512,512]{1,0:T(8,128)(2,1)S(1)} collective-permute-done((bf16[512,512]{1,0:T(8,128)(2,1)S(1)}, bf16[512,512]{1,0:T(8,128)(2,1)S(1)}, u32[]{:S(2)}, u32[]{:S(2)}) %collective-permute-start.1) | collective-permute-done | bytes 524320 | tf_op jit(solution)/shard_map/ppermute | solution.py:255
  18.7 1.5 %collective-permute-start.6 = (bf16[512,256]{1,0:T(8,128)(2,1)S(1)}, bf16[512,256]{1,0:T(8,128)(2,1)S(1)}, u32[]{:S(2)}, u32[]{:S(2)}) collective-permute-start(bf16[512,256]{1,0:T(8,128)(2,1)S(1)} %slice.49), channel_id=1, source_target_pairs={{0,2},{2,0},{1,3},{3,1},{4,6},{6,4},{5,7},{7,5},{8,10},{10,8},{9,1... | collective-permute-start | bytes 786440 | tf_op jit(solution)/shard_map/ppermute | solution.py:252
  20.2 3.0 %collective-permute-done.2.after.rest_3_ = bf16[512,512]{1,0:T(8,128)(2,1)S(1)} collective-permute-done((bf16[512,512]{1,0:T(8,128)(2,1)S(1)}, bf16[512,512]{1,0:T(8,128)(2,1)S(1)}, u32[]{:S(2)}, u32[]{:S(2)}) %collective-permute-start.2) | collective-permute-done | bytes 524320 | tf_op jit(solution)/shard_map/ppermute | solution.py:255
  23.2 0.0 collective-permute-done.q
  23.2 5.1 %remote_part.2 = bf16[2144,128]{1,0:T(8,128)(2,1)S(1)} custom-call(bf16[512,512]{1,0:T(8,128)(2,1)S(1)} %collective-permute-done.q, bf16[512,768]{1,0:T(8,128)(2,1)S(1)} %bitcast.6, bf16[512,768]{1,0:T(8,128)(2,1)S(1)} %bitcast.11, bf16[512,512]{1,0:T(8,128)(2,1)S(1)} %collective-permute-done.1.before.rest_2_, ...), custom_call_target="tpu_custom_call" | custom-call | flops 805306368 | bytes 2097152 | tf_op jit(solution)/shard_map/remote_part/pallas_call | solution.py:164
  28.3 1.6 %collective-permute-start.5 = (bf16[2144,128]{1,0:T(8,128)(2,1)S(1)}, bf16[2144,128]{1,0:T(8,128)(2,1)S(1)}, u32[]{:S(2)}, u32[]{:S(2)}) collective-permute-start(bf16[2144,128]{1,0:T(8,128)(2,1)S(1)} %remote_part.2), channel_id=1, source_target_pairs={{0,2},{2,0},{1,3},{3,1},{4,6},{6,4},{5,7},{7,5},{8,10},{10,8},{9,1... | collective-permute-start | bytes 1646600 | tf_op jit(solution)/shard_map/ppermute | solution.py:267
  29.9 0.0 collective-permute-done.3.rest_0_.before
  29.9 0.0 collective-permute-done.4.rest_1_.after
  29.9 0.0 collective-permute-done.6.q
  29.9 2.6 %remote_part.3 = bf16[1120,128]{1,0:T(8,128)(2,1)S(1)} custom-call(bf16[512,256]{1,0:T(8,128)(2,1)S(1)} %collective-permute-done.6.q, bf16[512,768]{1,0:T(8,128)(2,1)S(1)} %bitcast.7, bf16[512,768]{1,0:T(8,128)(2,1)S(1)} %bitcast.12, bf16[512,256]{1,0:T(8,128)(2,1)S(1)} %collective-permute-done.3.rest_0_.before, ...), custom_call_target="tpu_custom_call" | custom-call | flops 402653184 | bytes 1048576 | tf_op jit(solution)/shard_map/remote_part/pallas_call | solution.py:164
  32.5 0.6 %collective-permute-start.7 = (bf16[1120,128]{1,0:T(8,128)(2,1)S(1)}, bf16[1120,128]{1,0:T(8,128)(2,1)S(1)}, u32[]{:S(2)}, u32[]{:S(2)}) collective-permute-start(bf16[1120,128]{1,0:T(8,128)(2,1)S(1)} %remote_part.3), channel_id=1, source_target_pairs={{0,2},{2,0},{1,3},{3,1},{4,6},{6,4},{5,7},{7,5},{8,10},{10,8},{9,1... | collective-permute-start | bytes 860168 | tf_op jit(solution)/shard_map/ppermute | solution.py:267
  33.1 7.9 %local_part.1 = (f32[512,768]{1,0:T(8,128)S(1)}, f32[512,128]{1,0:T(8,128)S(1)}) custom-call(bf16[512,768]{1,0:T(8,128)(2,1)S(1)} %bitcast.16, bf16[512,768]{1,0:T(8,128)(2,1)S(1)} %bitcast.8, bf16[512,768]{1,0:T(8,128)(2,1)S(1)} %bitcast.13, bf16[512,256]{1,0:T(8,128)(2,1)S(1)} %collective-permute-done.3.rest_0_.before, ...), custom_call_target="tpu_custom_call" | custom-call | flops 1207959552 | bytes 3145728 | tf_op jit(solution)/shard_map/local_part/pallas_call | solution.py:186
  41.0 5.1 %collective-permute-done.7.rest_0_ = bf16[1120,128]{1,0:T(8,128)(2,1)S(1)} collective-permute-done((bf16[1120,128]{1,0:T(8,128)(2,1)S(1)}, bf16[1120,128]{1,0:T(8,128)(2,1)S(1)}, u32[]{:S(2)}, u32[]{:S(2)}) %collective-permute-start.7) | collective-permute-done | bytes 286752 | tf_op jit(solution)/shard_map/ppermute | solution.py:267
  46.1 1.4 %combine_part.2.rest_1_ = bf16[512,768]{1,0:T(8,128)(2,1)} custom-call(f32[512,768]{1,0:T(8,128)S(1)} %get-tuple-element.9.own, f32[512,128]{1,0:T(8,128)S(1)} %get-tuple-element.10.logs, bf16[1120,128]{1,0:T(8,128)(2,1)S(1)} %collective-permute-done.7.rest_0_), custom_call_target="tpu_custom_call" | custom-call | flops 1048576 | bytes 1048576 | tf_op jit(solution)/shard_map/combine_part/pallas_call | solution.py:210
  47.5 0.0 collective-permute-done.5.rest_0_
  47.5 2.3 %combine_part.3 = bf16[512,768]{1,0:T(8,128)(2,1)} custom-call(f32[512,768]{1,0:T(8,128)S(1)} %get-tuple-element.9.own, f32[512,128]{1,0:T(8,128)S(1)} %get-tuple-element.10.logs, bf16[2144,128]{1,0:T(8,128)(2,1)S(1)} %collective-permute-done.5.rest_0_, bf16[512,768]{1,0:T(8,128)(2,1)} %combine_part.2.rest_1_), custom_call_target="tpu_custom_call", output_to_operand_aliasing={{}: (3, {})} | custom-call | flops 2097152 | bytes 2097152 | tf_op jit(solution)/shard_map/combine_part/pallas_call | solution.py:210
  (7 shorter events, 0.2 us)
Async XLA Ops:
  1.3 6.5 %copy-start.2 = (bf16[8,8,8,768]{3,2,1,0:T(8,128)(2,1)S(1)}, bf16[8,8,8,768]{3,2,1,0:T(8,128)(2,1)}, u32[]{:S(2)}) copy-start(bf16[8,8,8,768]{3,2,1,0:T(8,128)(2,1)} %param.3) | copy-start | bytes 2359300
  1.3 8.1 %copy-start = (bf16[8,8,8,768]{3,2,1,0:T(8,128)(2,1)S(1)}, bf16[8,8,8,768]{3,2,1,0:T(8,128)(2,1)}, u32[]{:S(2)}) copy-start(bf16[8,8,8,768]{3,2,1,0:T(8,128)(2,1)} %param.4) | copy-start | bytes 2359300
  1.3 8.1 %copy-start.1 = (bf16[8,8,8,768]{3,2,1,0:T(8,128)(2,1)S(1)}, bf16[8,8,8,768]{3,2,1,0:T(8,128)(2,1)}, u32[]{:S(2)}) copy-start(bf16[8,8,8,768]{3,2,1,0:T(8,128)(2,1)} %param.5) | copy-start | bytes 2359300
  1.3 17.4 %collective-permute-start.1 = (bf16[512,512]{1,0:T(8,128)(2,1)S(1)}, bf16[512,512]{1,0:T(8,128)(2,1)S(1)}, u32[]{:S(2)}, u32[]{:S(2)}) collective-permute-start(bf16[512,512]{1,0:T(8,128)(2,1)S(1)} %pad_maximum_fusion), channel_id=1, source_target_pairs={{0,4},{4,8},{8,12},{1,5},{5,9},{9,13},{2,6},{6,10},{10,14},{3,7},{... | collective-permute-start | bytes 1572872 | tf_op jit(solution)/shard_map/ppermute | solution.py:255
  6.5 16.7 %collective-permute-start.2 = (bf16[512,512]{1,0:T(8,128)(2,1)S(1)}, bf16[512,512]{1,0:T(8,128)(2,1)S(1)}, u32[]{:S(2)}, u32[]{:S(2)}) collective-permute-start(bf16[512,512]{1,0:T(8,128)(2,1)S(1)} %pad_maximum_fusion.1), channel_id=1, source_target_pairs={{4,0},{8,4},{12,8},{5,1},{9,5},{13,9},{6,2},{10,6},{14,10},{7,3},{... | collective-permute-start | bytes 1572872 | tf_op jit(solution)/shard_map/ppermute | solution.py:255
  7.8 15.4 %collective-permute-start = (bf16[512,512]{1,0:T(8,128)(2,1)S(1)}, bf16[512,512]{1,0:T(8,128)(2,1)S(1)}, u32[]{:S(2)}, u32[]{:S(2)}) collective-permute-start(bf16[512,512]{1,0:T(8,128)(2,1)S(1)} %slice.40), channel_id=1, source_target_pairs={{0,2},{2,0},{1,3},{3,1},{4,6},{6,4},{5,7},{7,5},{8,10},{10,8},{9,1... | collective-permute-start | bytes 1572872 | tf_op jit(solution)/shard_map/ppermute | solution.py:252
  9.5 20.4 %collective-permute-start.3 = (bf16[512,256]{1,0:T(8,128)(2,1)S(1)}, bf16[512,256]{1,0:T(8,128)(2,1)S(1)}, u32[]{:S(2)}, u32[]{:S(2)}) collective-permute-start(bf16[512,256]{1,0:T(8,128)(2,1)S(1)} %pad_maximum_fusion.2), channel_id=1, source_target_pairs={{0,4},{4,8},{8,12},{1,5},{5,9},{9,13},{2,6},{6,10},{10,14},{3,7},{... | collective-permute-start | bytes 786440 | tf_op jit(solution)/shard_map/ppermute | solution.py:255
  14.1 15.8 %collective-permute-start.4 = (bf16[512,256]{1,0:T(8,128)(2,1)S(1)}, bf16[512,256]{1,0:T(8,128)(2,1)S(1)}, u32[]{:S(2)}, u32[]{:S(2)}) collective-permute-start(bf16[512,256]{1,0:T(8,128)(2,1)S(1)} %pad_maximum_fusion.3), channel_id=1, source_target_pairs={{4,0},{8,4},{12,8},{5,1},{9,5},{13,9},{6,2},{10,6},{14,10},{7,3},{... | collective-permute-start | bytes 786440 | tf_op jit(solution)/shard_map/ppermute | solution.py:255
  18.7 11.2 %collective-permute-start.6 = (bf16[512,256]{1,0:T(8,128)(2,1)S(1)}, bf16[512,256]{1,0:T(8,128)(2,1)S(1)}, u32[]{:S(2)}, u32[]{:S(2)}) collective-permute-start(bf16[512,256]{1,0:T(8,128)(2,1)S(1)} %slice.49), channel_id=1, source_target_pairs={{0,2},{2,0},{1,3},{3,1},{4,6},{6,4},{5,7},{7,5},{8,10},{10,8},{9,1... | collective-permute-start | bytes 786440 | tf_op jit(solution)/shard_map/ppermute | solution.py:252
  28.3 19.1 %collective-permute-start.5 = (bf16[2144,128]{1,0:T(8,128)(2,1)S(1)}, bf16[2144,128]{1,0:T(8,128)(2,1)S(1)}, u32[]{:S(2)}, u32[]{:S(2)}) collective-permute-start(bf16[2144,128]{1,0:T(8,128)(2,1)S(1)} %remote_part.2), channel_id=1, source_target_pairs={{0,2},{2,0},{1,3},{3,1},{4,6},{6,4},{5,7},{7,5},{8,10},{10,8},{9,1... | collective-permute-start | bytes 1646600 | tf_op jit(solution)/shard_map/ppermute | solution.py:267
  32.5 13.6 %collective-permute-start.7 = (bf16[1120,128]{1,0:T(8,128)(2,1)S(1)}, bf16[1120,128]{1,0:T(8,128)(2,1)S(1)}, u32[]{:S(2)}, u32[]{:S(2)}) collective-permute-start(bf16[1120,128]{1,0:T(8,128)(2,1)S(1)} %remote_part.3), channel_id=1, source_target_pairs={{0,2},{2,0},{1,3},{3,1},{4,6},{6,4},{5,7},{7,5},{8,10},{10,8},{9,1... | collective-permute-start | bytes 860168 | tf_op jit(solution)/shard_map/ppermute | solution.py:267

commit v2 on v1

v2 whole, which is shorter than its diff:
```python
import functools
import math

import jax
import jax.numpy as jnp
from jax import lax
from jax.experimental import pallas as pl
from jax.experimental.pallas import tpu as pltpu
from jax.sharding import PartitionSpec as P

HD = 128
TF = 4
TR = 8
TC = 8
TILE = TF * TR * TC
ROWS = 2 * TILE
EXPONENT = math.log2(math.e) / math.sqrt(HD)
NT = (((1,), (1,)), ((), ()))
NN = (((1,), (0,)), ((), ()))
BLOCKS = ROWS // HD
LOG_ROWS = 16
CHUNKS = (3, 3)
VMEM_BYTES = 48 * 1024 * 1024


def dot(a, b, dims):
    return lax.dot_general(a, b, dims, preferred_element_type=jnp.float32)


def attend(first, heads, q, k, v, even, odd, store):
    place = lax.axis_index("frame")
    present = (place > 0, place < lax.axis_size("frame") - 1)
    is_even = lax.rem(place, 2) == 0
    ones = jnp.ones((ROWS, HD), jnp.bfloat16)
    lanes = lax.broadcasted_iota(jnp.int32, (HD, HD), 1)
    logs = jnp.zeros((HD, HD), jnp.float32)
    for t in range(2):
        rows = slice(t * TILE, (t + 1) * TILE)
        near, far = (odd, even) if t == 0 else (even, odd)
        for j in range(heads):
            here = slice(j * HD, (j + 1) * HD)
            own = slice((first + j) * HD, (first + j + 1) * HD)
            q_tile = q[rows, here]
            k_own = k[:, own]
            v_own = jnp.concatenate([v[:, own], ones], 1)
            side = jnp.where(is_even, near[:, here], far[:, here])
            k_side = jnp.where(present[t], side[:TILE], k_own[:TILE])
            v_side = jnp.concatenate([side[TILE:], ones[:TILE]], 1)
            v_side = jnp.where(present[t], v_side, jnp.zeros_like(v_side))
            s_own = dot(q_tile, k_own, NT)
            s_side = dot(q_tile, k_side, NT)
            peak = jnp.maximum(
                jnp.max(s_own, axis=1, keepdims=True), jnp.max(s_side, axis=1, keepdims=True)
            )
            w_own = jnp.exp2((s_own - peak) * EXPONENT).astype(jnp.bfloat16)
            w_side = jnp.exp2((s_side - peak) * EXPONENT).astype(jnp.bfloat16)
            summed = dot(w_own, v_own, NN) + dot(w_side, v_side, NN)
            total = summed[:, HD:]
            store(rows, here, summed[:, :HD] / total)
            log = peak * EXPONENT + jnp.log2(total[:, :1])
            for i in range(TILE // HD):
                at = (t * (TILE // HD) + i) * (LOG_ROWS // BLOCKS) + j
                logs = jnp.where(lanes == at, log[i * HD : (i + 1) * HD], logs)
    return logs


def pack_logs(logs):
    flat = logs.T[:LOG_ROWS]
    parts = []
    for _ in range(3):
        part = flat.astype(jnp.bfloat16)
        flat = flat - part.astype(jnp.float32)
        parts.append(part)
    return jnp.concatenate(parts, 1)


def unpack_logs(packed):
    parts = packed.astype(jnp.float32)
    flat = parts[:, :HD] + parts[:, HD : 2 * HD] + parts[:, 2 * HD :]
    return jnp.concatenate([flat, jnp.zeros((HD - LOG_ROWS, HD), jnp.float32)], 0).T


def remote_kernel(first, heads, q, k, v, even, odd, out):
    def store(rows, here, block):
        out[rows, here] = block.astype(out.dtype)

    logs = attend(first, heads, q, k, v, even, odd, store)
    out[ROWS:, :] = pack_logs(logs)


def local_kernel(splits, q, k, v, *rest):
    sides, (out, logs) = rest[:-2], rest[-2:]
    first = 0
    for c, heads in enumerate(splits):
        columns = slice(first * HD, (first + heads) * HD)

        def store(rows, here, block, first=first):
            out[rows, first * HD + here.start : first * HD + here.stop] = block

        logs[c] = attend(
            first, heads, q.at[:, columns], k, v, sides[2 * c], sides[2 * c + 1], store
        )
        first += heads


def combine_kernel(chunk, heads, groups, own, logs, *rest):
    theirs, out = rest[:groups], rest[-1]
    place = lax.axis_index("row")
    if groups == 1:
        there = (None,)
    else:
        there = (place < lax.axis_size("row") - 1, place > 0)
    all_logs = [logs[0]]
    for g in range(groups):
        got = unpack_logs(theirs[g][ROWS:, :])
        if there[g] is not None:
            got = jnp.where(there[g], got, -jnp.inf)
        all_logs.append(got)
    top = functools.reduce(jnp.maximum, all_logs)
    weights = [jnp.exp2(x - top) for x in all_logs]
    total = functools.reduce(jnp.add, weights)
    shares = [w / total for w in weights]
    for b in range(BLOCKS):
        rows = slice(b * HD, (b + 1) * HD)
        for j in range(heads):
            here = slice(j * HD, (j + 1) * HD)
            at = b * (LOG_ROWS // BLOCKS) + j
            summed = shares[0][:, at : at + 1] * own[rows, here]
            for g in range(groups):
                block = theirs[g][rows, here].astype(jnp.float32)
                summed = summed + shares[g + 1][:, at : at + 1] * block
            out[rows, here] = summed.astype(out.dtype)


def cost(heads, tiles=6):
    pairs = heads * tiles * TILE * TILE
    return pl.CostEstimate(
        flops=4 * pairs * HD, bytes_accessed=heads * 8 * ROWS * HD, transcendentals=pairs
    )


def in_vmem():
    return pl.BlockSpec(memory_space=pltpu.VMEM)


def remote_part(first, heads, q, k, v, even, odd):
    return pl.pallas_call(
        functools.partial(remote_kernel, first, heads),
        in_specs=[in_vmem()] * 5,
        out_specs=in_vmem(),
        out_shape=jax.ShapeDtypeStruct((ROWS + LOG_ROWS, heads * HD), jnp.bfloat16),
        compiler_params=pltpu.CompilerParams(vmem_limit_bytes=VMEM_BYTES),
        cost_estimate=cost(heads),
        name="remote_part",
    )(q, k, v, even, odd)


def local_part(splits, q, k, v, sides):
    heads = sum(splits)
    return pl.pallas_call(
        functools.partial(local_kernel, splits),
        in_specs=[in_vmem()] * (3 + len(sides)),
        out_specs=[in_vmem()] * 2,
        out_shape=[
            jax.ShapeDtypeStruct((ROWS, heads * HD), jnp.float32),
            jax.ShapeDtypeStruct((len(splits), HD, HD), jnp.float32),
        ],
        compiler_params=pltpu.CompilerParams(vmem_limit_bytes=VMEM_BYTES),
        cost_estimate=cost(heads),
        name="local_part",
    )(q, k, v, *sides)


def combine_part(chunk, heads, own, logs, theirs, prior):
    groups = len(theirs)
    block = pl.BlockSpec((ROWS, heads * HD), lambda i: (0, chunk))
    specs = [block, pl.BlockSpec((1, HD, HD), lambda i: (chunk, 0, 0))]
    specs += [pl.BlockSpec(t.shape, lambda i: (0, 0)) for t in theirs]
    operands = [own, logs, *theirs]
    aliases = {}
    if prior is not None:
        specs.append(pl.BlockSpec(memory_space=pl.ANY))
        aliases = {len(operands): 0}
        operands.append(prior)
    return pl.pallas_call(
        functools.partial(combine_kernel, chunk, heads, groups),
        grid=(1,),
        in_specs=specs,
        out_specs=block,
        out_shape=jax.ShapeDtypeStruct(own.shape, jnp.bfloat16),
        input_output_aliases=aliases,
        compiler_params=pltpu.CompilerParams(vmem_limit_bytes=VMEM_BYTES),
        cost_estimate=pl.CostEstimate(
            flops=8 * heads * ROWS * HD, bytes_accessed=heads * 8 * ROWS * HD, transcendentals=0
        ),
        name="combine_part",
    )(*operands)


def frame_pairs(first, frames, cores):
    partner = {}
    for i in range(first, frames - 1, 2):
        partner[i], partner[i + 1] = i + 1, i
    return [
        (i * cores + c, partner[i] * cores + c if i in partner else i * cores + cores - 1 - c)
        for i in range(frames)
        for c in range(cores)
    ]


def per_device(query, keys, values):
    features = query.shape[3]
    heads = features // HD
    splits = CHUNKS
    assert sum(splits) == heads
    q = query.reshape(ROWS, features)
    k = keys.reshape(ROWS, features)
    v = values.reshape(ROWS, features)
    frames = lax.axis_size("frame")
    rows = lax.axis_size("row")
    pairs = [frame_pairs(first, frames, lax.axis_size("head")) for first in (0, 1)]
    place = lax.axis_index("frame")
    if rows == 2:
        routes = [([(0, 1), (1, 0)], [(0, 1), (1, 0)])]
    else:
        down = [(i, i + 1) for i in range(rows - 1)]
        up = [(i + 1, i) for i in range(rows - 1)]
        routes = [(down, up), (up, down)]

    bounds, start = [], 0
    for count in splits:
        bounds.append((start, start + count))
        start += count

    got_q, sides = [], []
    q_now, gate = q, ()
    for a, b in bounds:
        a, b = a * HD, b * HD
        sent = q_now[:, a:b]
        got_q.append([lax.ppermute(sent, "row", there) for there, _ in routes])
        k_now, v_now, _ = lax.optimization_barrier((k, v, (sent, gate)))
        gate = got_q[-1]
        halves = []
        for first in (0, 1):
            row = jnp.where(lax.rem(place, 2) == first, TILE, 0)
            half = [lax.dynamic_slice(x, (row, a), (TILE, b - a)) for x in (k_now, v_now)]
            halves.append(jnp.concatenate(half, 0))
        q_now, _ = lax.optimization_barrier((q, halves))
        sides.append([lax.ppermute(h, ("frame", "head"), p) for h, p in zip(halves, pairs)])

    answers = []
    k_now, v_now = k, v
    for (a, b), chunk_q, (even, odd) in zip(bounds, got_q, sides):
        parts = [remote_part(a, b - a, one, k_now, v_now, even, odd) for one in chunk_q]
        answers.append(parts)
        k_now, v_now, _ = lax.optimization_barrier((k, v, parts))

    q_local, _ = lax.optimization_barrier((q, answers))
    own, logs = local_part(splits, q_local, k, v, [s for pair in sides for s in pair])

    out = None
    for c, ((a, b), parts) in enumerate(zip(bounds, answers)):
        theirs = [lax.ppermute(p, "row", back) for p, (_, back) in zip(parts, routes)]
        out = combine_part(c, b - a, own, logs, theirs, out)
    return out.reshape(query.shape)


def solution(mesh):
    spec = P(("clips", "frame"), "row", None, "head")
    return jax.shard_map(
        per_device, mesh=mesh, in_specs=(spec,) * 3, out_specs=spec, check_vma=False
    )
```

time: 50 us -> 40.6 us (0.81)
  Pallas kernels: 19.3 us -> 10.1 us
  starting transfers between devices: 17.4 us -> 9.3 us
  waiting for transfers between devices: 11.4 us -> 18.1 us
  local copies, waits for them, and re-layouts: 1.36 us -> 2.55 us
    pallas_call x5, Pallas kernels: 19.3 us -> 10.1 us  [the longest x2 4.03 us: remote_part(): pl.pallas_call(functools.partial(remote_kernel, first, heads), in_specs=[...]
    ppermute x6, starting transfers between devices: 15.3 us -> 7.6 us  [the longest x4 3.99 us: per_device(): lax.ppermute(h, ('frame', 'head'), p)]
    ppermute x6, waiting for transfers between devices: 6.35 us -> 11 us  [the longest x2 7.6 us: per_device(): got_q.append([lax.ppermute(sent, 'row', there) for there, _ in routes])]
    ppermute x2, waiting for transfers between devices: 5.09 us -> 7.1 us  [per_device(): lax.ppermute(p, 'row', back)]
    dynamic_slice x0 -> x3, local copies, waits for them, and re-layouts: none -> 1.45 us  [per_device(): lax.dynamic_slice(x, (row, a), (TILE, b - a))]
    slice x4 -> x2, local copies, waits for them, and re-layouts: 1.34 us -> 1.08 us  [per_device(): sent = q_now[:, a:b]]
  transfers between devices with their start and end apart: 8 -> 8, of which waited for: 3 -> 6; matrix products, arithmetic and copies ran while one was open for 0% -> 4% of each run, Pallas kernels for 34% -> 22%
where the time goes in v2:
time: 40.6 us; the launch traced here: 40.4 us
  waiting for transfers between devices  18.1 us (45%)
  Pallas kernels  10.1 us (25%)
  starting transfers between devices  9.3 us (23%)
  local copies, waits for them, and re-layouts  2.55 us (6%)
    ppermute x2, waiting for transfers between devices, per_device(): got_q.append([lax.ppermute(sent, 'row', there) for there, _ in routes])  7.6 us
    ppermute x2, waiting for transfers between devices, per_device(): lax.ppermute(p, 'row', back)  7.1 us
    pallas_call x2, Pallas kernels, remote_part(): pl.pallas_call(functools.partial(remote_kernel, first, heads), in_specs=[...  4.03 us
    ppermute x4, starting transfers between devices, per_device(): lax.ppermute(h, ('frame', 'head'), p)  3.99 us
    ppermute x2, starting transfers between devices, per_device(): got_q.append([lax.ppermute(sent, 'row', there) for there, _ in routes])  3.6 us
    ppermute x4, waiting for transfers between devices, per_device(): lax.ppermute(h, ('frame', 'head'), p)  3.41 us
    pallas_call x1, Pallas kernels, local_part(): pl.pallas_call(functools.partial(local_kernel, splits), in_specs=[in_vmem...  3.39 us
    pallas_call x2, Pallas kernels, combine_part(): pl.pallas_call(functools.partial(combine_kernel, chunk, heads, groups), g...  2.73 us
  transfers between devices with their start and end apart: 8, of which 6 were waited for; matrix products, arithmetic and copies ran while one was open for 4% of the time, Pallas kernels for 22%

profile of v2, /device:TPU:0, one launch (start us, length us, event | category | flops | bytes accessed | tf_op | source)
XLA Modules:
  0.0 40.4 jit_solution(15342423003099562734)
XLA Ops:
  0.0 1.0 %slice.8 = bf16[512,384]{1,0:T(8,128)(2,1)S(1)} slice(bf16[512,768]{1,0:T(8,128)(2,1)} %bitcast.14), slice={[0:512], [0:384]} | slice | bytes 786432 | tf_op jit(solution)/shard_map/slice | solution.py:239
  1.0 3.0 %collective-permute-start = (bf16[512,384]{1,0:T(8,128)(2,1)S(1)}, bf16[512,384]{1,0:T(8,128)(2,1)S(1)}, u32[]{:S(2)}, u32[]{:S(2)}) collective-permute-start(bf16[512,384]{1,0:T(8,128)(2,1)S(1)} %slice.8), channel_id=1, source_target_pairs={{0,2},{2,0},{1,3},{3,1},{4,6},{6,4},{5,7},{7,5},{8,10},{10,8},{9,1... | collective-permute-start | bytes 1179656 | tf_op jit(solution)/shard_map/ppermute | solution.py:240
  4.0 0.0 copy-start.2
  4.0 1.4 %constant_dynamic-slice_fusion.4 = (bf16[256,384]{1,0:T(8,128)(2,1)S(1)}, bf16[256,384]{1,0:T(8,128)(2,1)S(1)}, bf16[256,384]{1,0:T(8,128)(2,1)S(1)}, bf16[256,384]{1,0:T(8,128)(2,1)S(1)}) fusion(bf16[512,768]{1,0:T(8,128)(2,1)} %bitcast.9, s32[]{:T(128)S(6)} %select_n.18, s32[]{:T(128)S(6)} %select_n.9, bf16[512,768]{1,0:T(8,128)(2,1)} %bitcast.4), kind=kLoop, calls=%fused_computation.8 | loop fusion | bytes 1572872 | tf_op jit(solution)/shard_map/dynamic_slice | solution.py:246
  5.4 0.0 copy-start
  5.4 0.0 copy-start.1
  5.5 1.6 %collective-permute-start.1 = (bf16[512,384]{1,0:T(8,128)(2,1)S(1)}, bf16[512,384]{1,0:T(8,128)(2,1)S(1)}, u32[]{:S(2)}, u32[]{:S(2)}) collective-permute-start(bf16[512,384]{1,0:T(8,128)(2,1)S(1)} %pad_maximum_fusion), channel_id=1, source_target_pairs={{0,4},{1,5},{4,0},{5,1},{8,12},{9,13},{12,8},{13,9},{2,6},{3,7},{6... | collective-permute-start | bytes 1179656 | tf_op jit(solution)/shard_map/ppermute | solution.py:249
  7.2 0.1 collective-permute-start.2
  7.2 0.0 copy-done.2
  7.3 0.6 %collective-permute-start.3 = (bf16[512,384]{1,0:T(8,128)(2,1)S(1)}, bf16[512,384]{1,0:T(8,128)(2,1)S(1)}, u32[]{:S(2)}, u32[]{:S(2)}) collective-permute-start(bf16[512,384]{1,0:T(8,128)(2,1)S(1)} %slice.7), channel_id=1, source_target_pairs={{0,2},{2,0},{1,3},{3,1},{4,6},{6,4},{5,7},{7,5},{8,10},{10,8},{9,1... | collective-permute-start | bytes 1179656 | tf_op jit(solution)/shard_map/ppermute | solution.py:240
  7.9 6.1 %collective-permute-done.q = bf16[512,384]{1,0:T(8,128)(2,1)S(1)} collective-permute-done((bf16[512,384]{1,0:T(8,128)(2,1)S(1)}, bf16[512,384]{1,0:T(8,128)(2,1)S(1)}, u32[]{:S(2)}, u32[]{:S(2)}) %collective-permute-start) | collective-permute-done | bytes 393248 | tf_op jit(solution)/shard_map/ppermute | solution.py:240
  14.0 0.0 copy-done
  14.0 0.0 copy-done.1
  14.0 0.1 constant_dynamic-slice_fusion
  14.2 2.2 %collective-permute-start.4 = (bf16[512,384]{1,0:T(8,128)(2,1)S(1)}, bf16[512,384]{1,0:T(8,128)(2,1)S(1)}, u32[]{:S(2)}, u32[]{:S(2)}) collective-permute-start(bf16[512,384]{1,0:T(8,128)(2,1)S(1)} %pad_maximum_fusion.2), channel_id=1, source_target_pairs={{0,4},{1,5},{4,0},{5,1},{8,12},{9,13},{12,8},{13,9},{2,6},{3,7},{6... | collective-permute-start | bytes 1179656 | tf_op jit(solution)/shard_map/ppermute | solution.py:249
  16.4 0.1 collective-permute-start.5
  16.5 0.4 %collective-permute-done.1.even.rest_0_ = bf16[512,384]{1,0:T(8,128)(2,1)S(1)} collective-permute-done((bf16[512,384]{1,0:T(8,128)(2,1)S(1)}, bf16[512,384]{1,0:T(8,128)(2,1)S(1)}, u32[]{:S(2)}, u32[]{:S(2)}) %collective-permute-start.1) | collective-permute-done | bytes 393248 | tf_op jit(solution)/shard_map/ppermute | solution.py:249
  16.9 0.0 collective-permute-done.2.odd.rest_1_
  16.9 2.0 %remote_part.2 = bf16[528,384]{1,0:T(8,128)(2,1)S(1)} custom-call(bf16[512,384]{1,0:T(8,128)(2,1)S(1)} %collective-permute-done.q, bf16[512,768]{1,0:T(8,128)(2,1)S(1)} %bitcast.6, bf16[512,768]{1,0:T(8,128)(2,1)S(1)} %bitcast.11, bf16[512,384]{1,0:T(8,128)(2,1)S(1)} %collective-permute-done.1.even.rest_0_, ...), custom_call_target="tpu_custom_call" | custom-call | flops 603979776 | bytes 1572864 | tf_op jit(solution)/shard_map/remote_part/pallas_call | solution.py:147
  18.9 1.1 %collective-permute-start.7 = (bf16[528,384]{1,0:T(8,128)(2,1)S(1)}, bf16[528,384]{1,0:T(8,128)(2,1)S(1)}, u32[]{:S(2)}, u32[]{:S(2)}) collective-permute-start(bf16[528,384]{1,0:T(8,128)(2,1)S(1)} %remote_part.2), channel_id=1, source_target_pairs={{0,2},{2,0},{1,3},{3,1},{4,6},{6,4},{5,7},{7,5},{8,10},{10,8},{9,1... | collective-permute-start | bytes 1216520 | tf_op jit(solution)/shard_map/ppermute | solution.py:263
  20.1 1.5 %collective-permute-done.3.q = bf16[512,384]{1,0:T(8,128)(2,1)S(1)} collective-permute-done((bf16[512,384]{1,0:T(8,128)(2,1)S(1)}, bf16[512,384]{1,0:T(8,128)(2,1)S(1)}, u32[]{:S(2)}, u32[]{:S(2)}) %collective-permute-start.3) | collective-permute-done | bytes 393248 | tf_op jit(solution)/shard_map/ppermute | solution.py:240
  21.6 3.0 %collective-permute-done.4.even.rest_2_ = bf16[512,384]{1,0:T(8,128)(2,1)S(1)} collective-permute-done((bf16[512,384]{1,0:T(8,128)(2,1)S(1)}, bf16[512,384]{1,0:T(8,128)(2,1)S(1)}, u32[]{:S(2)}, u32[]{:S(2)}) %collective-permute-start.4) | collective-permute-done | bytes 393248 | tf_op jit(solution)/shard_map/ppermute | solution.py:249
  24.6 0.0 collective-permute-done.5.odd.rest_3_
  24.6 2.0 %remote_part.3 = bf16[528,384]{1,0:T(8,128)(2,1)S(1)} custom-call(bf16[512,384]{1,0:T(8,128)(2,1)S(1)} %collective-permute-done.3.q, bf16[512,768]{1,0:T(8,128)(2,1)S(1)} %bitcast.7, bf16[512,768]{1,0:T(8,128)(2,1)S(1)} %bitcast.12, bf16[512,384]{1,0:T(8,128)(2,1)S(1)} %collective-permute-done.4.even.rest_2_, ...), custom_call_target="tpu_custom_call" | custom-call | flops 603979776 | bytes 1572864 | tf_op jit(solution)/shard_map/remote_part/pallas_call | solution.py:147
  26.6 0.6 %collective-permute-start.6 = (bf16[528,384]{1,0:T(8,128)(2,1)S(1)}, bf16[528,384]{1,0:T(8,128)(2,1)S(1)}, u32[]{:S(2)}, u32[]{:S(2)}) collective-permute-start(bf16[528,384]{1,0:T(8,128)(2,1)S(1)} %remote_part.3), channel_id=1, source_target_pairs={{0,2},{2,0},{1,3},{3,1},{4,6},{6,4},{5,7},{7,5},{8,10},{10,8},{9,1... | collective-permute-start | bytes 1216520 | tf_op jit(solution)/shard_map/ppermute | solution.py:263
  27.2 3.4 %local_part.1 = (f32[512,768]{1,0:T(8,128)S(1)}, f32[2,128,128]{2,1,0:T(8,128)S(1)}) custom-call(bf16[512,768]{1,0:T(8,128)(2,1)S(1)} %bitcast.16, bf16[512,768]{1,0:T(8,128)(2,1)S(1)} %bitcast.8, bf16[512,768]{1,0:T(8,128)(2,1)S(1)} %bitcast.13, bf16[512,384]{1,0:T(8,128)(2,1)S(1)} %collective-permute-done.1.even.rest_0_, ...), custom_call_target="tpu_custom_call" | custom-call | flops 1207959552 | bytes 3145728 | tf_op jit(solution)/shard_map/local_part/pallas_call | solution.py:160
  30.6 0.7 %collective-permute-done.7.rest_0_ = bf16[528,384]{1,0:T(8,128)(2,1)S(1)} collective-permute-done((bf16[528,384]{1,0:T(8,128)(2,1)S(1)}, bf16[528,384]{1,0:T(8,128)(2,1)S(1)}, u32[]{:S(2)}, u32[]{:S(2)}) %collective-permute-start.7) | collective-permute-done | bytes 405536 | tf_op jit(solution)/shard_map/ppermute | solution.py:263
  31.2 1.4 %combine_part.2.rest_1_ = bf16[512,768]{1,0:T(8,128)(2,1)} custom-call(f32[512,768]{1,0:T(8,128)S(1)} %get-tuple-element.23.own, f32[2,128,128]{2,1,0:T(8,128)S(1)} %get-tuple-element.24.logs, bf16[528,384]{1,0:T(8,128)(2,1)S(1)} %collective-permute-done.7.rest_0_), custom_call_target="tpu_custom_call" | custom-call | flops 1572864 | bytes 1572864 | tf_op jit(solution)/shard_map/combine_part/pallas_call | solution.py:185
  32.6 6.4 %collective-permute-done.6.rest_0_ = bf16[528,384]{1,0:T(8,128)(2,1)S(1)} collective-permute-done((bf16[528,384]{1,0:T(8,128)(2,1)S(1)}, bf16[528,384]{1,0:T(8,128)(2,1)S(1)}, u32[]{:S(2)}, u32[]{:S(2)}) %collective-permute-start.6) | collective-permute-done | bytes 405536 | tf_op jit(solution)/shard_map/ppermute | solution.py:263
  39.0 1.4 %combine_part.3 = bf16[512,768]{1,0:T(8,128)(2,1)} custom-call(f32[512,768]{1,0:T(8,128)S(1)} %get-tuple-element.23.own, f32[2,128,128]{2,1,0:T(8,128)S(1)} %get-tuple-element.24.logs, bf16[528,384]{1,0:T(8,128)(2,1)S(1)} %collective-permute-done.6.rest_0_, bf16[512,768]{1,0:T(8,128)(2,1)} %combine_part.2.rest_1_), custom_call_target="tpu_custom_call", output_to_operand_aliasing={{}: (3, {})} | custom-call | flops 1572864 | bytes 1572864 | tf_op jit(solution)/shard_map/combine_part/pallas_call | solution.py:185
  (6 shorter events, 0.2 us)
Async XLA Ops:
  1.0 12.9 %collective-permute-start = (bf16[512,384]{1,0:T(8,128)(2,1)S(1)}, bf16[512,384]{1,0:T(8,128)(2,1)S(1)}, u32[]{:S(2)}, u32[]{:S(2)}) collective-permute-start(bf16[512,384]{1,0:T(8,128)(2,1)S(1)} %slice.8), channel_id=1, source_target_pairs={{0,2},{2,0},{1,3},{3,1},{4,6},{6,4},{5,7},{7,5},{8,10},{10,8},{9,1... | collective-permute-start | bytes 1179656 | tf_op jit(solution)/shard_map/ppermute | solution.py:240
  4.0 3.2 %copy-start.2 = (bf16[8,8,8,768]{3,2,1,0:T(8,128)(2,1)S(1)}, bf16[8,8,8,768]{3,2,1,0:T(8,128)(2,1)}, u32[]{:S(2)}) copy-start(bf16[8,8,8,768]{3,2,1,0:T(8,128)(2,1)} %param.3) | copy-start | bytes 2359300
  5.4 8.6 %copy-start = (bf16[8,8,8,768]{3,2,1,0:T(8,128)(2,1)S(1)}, bf16[8,8,8,768]{3,2,1,0:T(8,128)(2,1)}, u32[]{:S(2)}) copy-start(bf16[8,8,8,768]{3,2,1,0:T(8,128)(2,1)} %param.4) | copy-start | bytes 2359300
  5.4 8.6 %copy-start.1 = (bf16[8,8,8,768]{3,2,1,0:T(8,128)(2,1)S(1)}, bf16[8,8,8,768]{3,2,1,0:T(8,128)(2,1)}, u32[]{:S(2)}) copy-start(bf16[8,8,8,768]{3,2,1,0:T(8,128)(2,1)} %param.5) | copy-start | bytes 2359300
  5.5 11.4 %collective-permute-start.1 = (bf16[512,384]{1,0:T(8,128)(2,1)S(1)}, bf16[512,384]{1,0:T(8,128)(2,1)S(1)}, u32[]{:S(2)}, u32[]{:S(2)}) collective-permute-start(bf16[512,384]{1,0:T(8,128)(2,1)S(1)} %pad_maximum_fusion), channel_id=1, source_target_pairs={{0,4},{1,5},{4,0},{5,1},{8,12},{9,13},{12,8},{13,9},{2,6},{3,7},{6... | collective-permute-start | bytes 1179656 | tf_op jit(solution)/shard_map/ppermute | solution.py:249
  7.2 9.8 %collective-permute-start.2 = (bf16[512,384]{1,0:T(8,128)(2,1)S(1)}, bf16[512,384]{1,0:T(8,128)(2,1)S(1)}, u32[]{:S(2)}, u32[]{:S(2)}) collective-permute-start(bf16[512,384]{1,0:T(8,128)(2,1)S(1)} %pad_maximum_fusion.1), channel_id=1, source_target_pairs={{0,1},{1,0},{4,8},{5,9},{8,4},{9,5},{12,13},{13,12},{2,3},{3,2},{6... | collective-permute-start | bytes 1179656 | tf_op jit(solution)/shard_map/ppermute | solution.py:249
  7.3 14.3 %collective-permute-start.3 = (bf16[512,384]{1,0:T(8,128)(2,1)S(1)}, bf16[512,384]{1,0:T(8,128)(2,1)S(1)}, u32[]{:S(2)}, u32[]{:S(2)}) collective-permute-start(bf16[512,384]{1,0:T(8,128)(2,1)S(1)} %slice.7), channel_id=1, source_target_pairs={{0,2},{2,0},{1,3},{3,1},{4,6},{6,4},{5,7},{7,5},{8,10},{10,8},{9,1... | collective-permute-start | bytes 1179656 | tf_op jit(solution)/shard_map/ppermute | solution.py:240
  14.2 10.4 %collective-permute-start.4 = (bf16[512,384]{1,0:T(8,128)(2,1)S(1)}, bf16[512,384]{1,0:T(8,128)(2,1)S(1)}, u32[]{:S(2)}, u32[]{:S(2)}) collective-permute-start(bf16[512,384]{1,0:T(8,128)(2,1)S(1)} %pad_maximum_fusion.2), channel_id=1, source_target_pairs={{0,4},{1,5},{4,0},{5,1},{8,12},{9,13},{12,8},{13,9},{2,6},{3,7},{6... | collective-permute-start | bytes 1179656 | tf_op jit(solution)/shard_map/ppermute | solution.py:249
  16.4 8.2 %collective-permute-start.5 = (bf16[512,384]{1,0:T(8,128)(2,1)S(1)}, bf16[512,384]{1,0:T(8,128)(2,1)S(1)}, u32[]{:S(2)}, u32[]{:S(2)}) collective-permute-start(bf16[512,384]{1,0:T(8,128)(2,1)S(1)} %pad_maximum_fusion.3), channel_id=1, source_target_pairs={{0,1},{1,0},{4,8},{5,9},{8,4},{9,5},{12,13},{13,12},{2,3},{3,2},{6... | collective-permute-start | bytes 1179656 | tf_op jit(solution)/shard_map/ppermute | solution.py:249
  18.9 12.3 %collective-permute-start.7 = (bf16[528,384]{1,0:T(8,128)(2,1)S(1)}, bf16[528,384]{1,0:T(8,128)(2,1)S(1)}, u32[]{:S(2)}, u32[]{:S(2)}) collective-permute-start(bf16[528,384]{1,0:T(8,128)(2,1)S(1)} %remote_part.2), channel_id=1, source_target_pairs={{0,2},{2,0},{1,3},{3,1},{4,6},{6,4},{5,7},{7,5},{8,10},{10,8},{9,1... | collective-permute-start | bytes 1216520 | tf_op jit(solution)/shard_map/ppermute | solution.py:263
  26.6 12.5 %collective-permute-start.6 = (bf16[528,384]{1,0:T(8,128)(2,1)S(1)}, bf16[528,384]{1,0:T(8,128)(2,1)S(1)}, u32[]{:S(2)}, u32[]{:S(2)}) collective-permute-start(bf16[528,384]{1,0:T(8,128)(2,1)S(1)} %remote_part.3), channel_id=1, source_target_pairs={{0,2},{2,0},{1,3},{3,1},{4,6},{6,4},{5,7},{7,5},{8,10},{10,8},{9,1... | collective-permute-start | bytes 1216520 | tf_op jit(solution)/shard_map/ppermute | solution.py:263

commit v3 on v2

--- a/solution.py
+++ b/solution.py
@@ -20,6 +20,7 @@
 BLOCKS = ROWS // HD
 LOG_ROWS = 16
 CHUNKS = (3, 3)
+TAILS = (0, 1)
 VMEM_BYTES = 48 * 1024 * 1024
 
 
@@ -66,30 +67,32 @@
 
 def pack_logs(logs):
     flat = logs.T[:LOG_ROWS]
-    parts = []
-    for _ in range(3):
-        part = flat.astype(jnp.bfloat16)
-        flat = flat - part.astype(jnp.float32)
-        parts.append(part)
-    return jnp.concatenate(parts, 1)
+    high = flat.astype(jnp.bfloat16)
+    return jnp.concatenate([high, (flat - high.astype(jnp.float32)).astype(jnp.bfloat16)], 1)
 
 
 def unpack_logs(packed):
     parts = packed.astype(jnp.float32)
-    flat = parts[:, :HD] + parts[:, HD : 2 * HD] + parts[:, 2 * HD :]
+    flat = parts[:, :HD] + parts[:, HD:]
     return jnp.concatenate([flat, jnp.zeros((HD - LOG_ROWS, HD), jnp.float32)], 0).T
 
 
-def remote_kernel(first, heads, q, k, v, even, odd, out):
+def remote_kernel(first, heads, tail, q, k, v, even, odd, out, *last):
     def store(rows, here, block):
-        out[rows, here] = block.astype(out.dtype)
-
-    logs = attend(first, heads, q, k, v, even, odd, store)
-    out[ROWS:, :] = pack_logs(logs)
+        start = here.start - (heads - tail) * HD
+        if start < 0:
+            out[rows, here] = block.astype(out.dtype)
+        else:
+            last[0][rows, start : start + HD] = block.astype(out.dtype)
+
+    packed = pack_logs(attend(first, heads, q, k, v, even, odd, store))
+    out[ROWS:, : 2 * HD] = packed
+    if out.shape[1] > 2 * HD:
+        out[ROWS:, 2 * HD :] = jnp.zeros((LOG_ROWS, out.shape[1] - 2 * HD), out.dtype)
 
 
 def local_kernel(splits, q, k, v, *rest):
-    sides, (out, logs) = rest[:-2], rest[-2:]
+    sides, out, logs = rest[: -1 - len(splits)], rest[-1 - len(splits)], rest[-len(splits) :]
     first = 0
     for c, heads in enumerate(splits):
         columns = slice(first * HD, (first + heads) * HD)
@@ -97,39 +100,83 @@
         def store(rows, here, block, first=first):
             out[rows, first * HD + here.start : first * HD + here.stop] = block
 
-        logs[c] = attend(
+        logs[c][...] = attend(
             first, heads, q.at[:, columns], k, v, sides[2 * c], sides[2 * c + 1], store
         )
         first += heads
 
 
-def combine_kernel(chunk, heads, groups, own, logs, *rest):
-    theirs, out = rest[:groups], rest[-1]
+def shares_of(logs, theirs):
     place = lax.axis_index("row")
-    if groups == 1:
+    if len(theirs) == 1:
         there = (None,)
     else:
         there = (place < lax.axis_size("row") - 1, place > 0)
-    all_logs = [logs[0]]
-    for g in range(groups):
-        got = unpack_logs(theirs[g][ROWS:, :])
-        if there[g] is not None:
-            got = jnp.where(there[g], got, -jnp.inf)
-        all_logs.append(got)
+    all_logs = [logs[...]]
+    for valid, part in zip(there, theirs):
+        got = unpack_logs(part[ROWS:, : 2 * HD])
+        all_logs.append(got if valid is None else jnp.where(valid, got, -jnp.inf))
     top = functools.reduce(jnp.maximum, all_logs)
     weights = [jnp.exp2(x - top) for x in all_logs]
     total = functools.reduce(jnp.add, weights)
-    shares = [w / total for w in weights]
+    return [w / total for w in weights]
+
+
+def write_columns(first, heads, mixed, out, done, fill):
+    copies = []
     for b in range(BLOCKS):
         rows = slice(b * HD, (b + 1) * HD)
+        fill(b, rows)
+        copies.append(
+            pltpu.make_async_copy(
+                mixed.at[rows, :],
+                out.at[rows, first * HD : (first + heads) * HD],
+                done.at[b],
+            )
+        )
+        copies[-1].start()
+    return copies
+
+
+def merge_kernel(first, heads, tail, groups, own, logs, *rest):
+    theirs, (mixed, done) = rest[:groups], rest[-2:]
+    out, *later = rest[-3 - (1 + groups) * (tail > 0) : -2]
+    shares = shares_of(logs, theirs)
+
+    def fill(b, rows):
         for j in range(heads):
             here = slice(j * HD, (j + 1) * HD)
             at = b * (LOG_ROWS // BLOCKS) + j
-            summed = shares[0][:, at : at + 1] * own[rows, here]
-            for g in range(groups):
-                block = theirs[g][rows, here].astype(jnp.float32)
-                summed = summed + shares[g + 1][:, at : at + 1] * block
-            out[rows, here] = summed.astype(out.dtype)
+            summed = shares[0][:, at : at + 1] * own[rows, (first + j) * HD : (first + j + 1) * HD]
+            for share, part in zip(shares[1:], theirs):
+                summed = summed + share[:, at : at + 1] * part[rows, here].astype(jnp.float32)
+            mixed[rows, here] = summed.astype(mixed.dtype)
+
+    copies = write_columns(first, heads, mixed, out, done, fill)
+    for b in range(BLOCKS):
+        for j in range(tail):
+            rows, here = slice(b * HD, (b + 1) * HD), slice(j * HD, (j + 1) * HD)
+            at = b * (LOG_ROWS // BLOCKS) + heads + j
+            own_at = (first + heads + j) * HD
+            later[0][rows, here] = shares[0][:, at : at + 1] * own[rows, own_at : own_at + HD]
+            for share, spread in zip(shares[1:], later[1:]):
+                spread[rows, here] = jnp.broadcast_to(share[:, at : at + 1], (HD, HD))
+    for copy in copies:
+        copy.wait()
+
+
+def finish_kernel(first, heads, groups, scaled, *rest):
+    shares, theirs = rest[:groups], rest[groups : 2 * groups]
+    out, mixed, done = rest[-3:]
+
+    def fill(b, rows):
+        summed = scaled[rows, :]
+        for share, part in zip(shares, theirs):
+            summed = summed + share[rows, :] * part[rows, :].astype(jnp.float32)
+        mixed[rows, :] = summed.astype(mixed.dtype)
+
+    for copy in write_columns(first, heads, mixed, out, done, fill):
+        copy.wait()
 
 
 def cost(heads, tiles=6):
@@ -143,12 +190,13 @@
     return pl.BlockSpec(memory_space=pltpu.VMEM)
 
 
-def remote_part(first, heads, q, k, v, even, odd):
+def remote_part(first, heads, tail, q, k, v, even, odd):
+    shapes = [(ROWS + LOG_ROWS, (heads - tail) * HD)] + [(ROWS, tail * HD)] * (tail > 0)
     return pl.pallas_call(
-        functools.partial(remote_kernel, first, heads),
+        functools.partial(remote_kernel, first, heads, tail),
         in_specs=[in_vmem()] * 5,
-        out_specs=in_vmem(),
-        out_shape=jax.ShapeDtypeStruct((ROWS + LOG_ROWS, heads * HD), jnp.bfloat16),
+        out_specs=[in_vmem()] * len(shapes),
+        out_shape=[jax.ShapeDtypeStruct(shape, jnp.bfloat16) for shape in shapes],
         compiler_params=pltpu.CompilerParams(vmem_limit_bytes=VMEM_BYTES),
         cost_estimate=cost(heads),
         name="remote_part",
@@ -160,10 +208,10 @@
     return pl.pallas_call(
         functools.partial(local_kernel, splits),
         in_specs=[in_vmem()] * (3 + len(sides)),
-        out_specs=[in_vmem()] * 2,
+        out_specs=[in_vmem()] * (1 + len(splits)),
         out_shape=[
             jax.ShapeDtypeStruct((ROWS, heads * HD), jnp.float32),
-            jax.ShapeDtypeStruct((len(splits), HD, HD), jnp.float32),
+            *[jax.ShapeDtypeStruct((HD, HD), jnp.float32) for _ in splits],
         ],
         compiler_params=pltpu.CompilerParams(vmem_limit_bytes=VMEM_BYTES),
         cost_estimate=cost(heads),
@@ -171,30 +219,46 @@
     )(q, k, v, *sides)
 
 
-def combine_part(chunk, heads, own, logs, theirs, prior):
+def merge_cost(heads):
+    return pl.CostEstimate(
+        flops=4 * heads * ROWS * HD, bytes_accessed=heads * 8 * ROWS * HD, transcendentals=0
+    )
+
+
+def copy_scratch(heads):
+    return [pltpu.VMEM((ROWS, heads * HD), jnp.bfloat16), pltpu.SemaphoreType.DMA((BLOCKS,))]
+
+
+def merge_part(first, heads, tail, own, logs, theirs, prior):
     groups = len(theirs)
-    block = pl.BlockSpec((ROWS, heads * HD), lambda i: (0, chunk))
-    specs = [block, pl.BlockSpec((1, HD, HD), lambda i: (chunk, 0, 0))]
-    specs += [pl.BlockSpec(t.shape, lambda i: (0, 0)) for t in theirs]
-    operands = [own, logs, *theirs]
-    aliases = {}
-    if prior is not None:
-        specs.append(pl.BlockSpec(memory_space=pl.ANY))
-        aliases = {len(operands): 0}
-        operands.append(prior)
+    later = [jax.ShapeDtypeStruct((ROWS, tail * HD), jnp.float32)] * ((1 + groups) * (tail > 0))
+    out, *later = pl.pallas_call(
+        functools.partial(merge_kernel, first, heads, tail, groups),
+        in_specs=[in_vmem()] * (2 + groups) + [pl.BlockSpec(memory_space=pl.ANY)] * len(prior),
+        out_specs=[pl.BlockSpec(memory_space=pl.ANY)] + [in_vmem()] * len(later),
+        out_shape=[jax.ShapeDtypeStruct(own.shape, jnp.bfloat16)] + later,
+        scratch_shapes=copy_scratch(heads),
+        input_output_aliases={2 + groups: 0} if prior else {},
+        compiler_params=pltpu.CompilerParams(vmem_limit_bytes=VMEM_BYTES),
+        cost_estimate=merge_cost(heads + tail),
+        name="merge_part",
+    )(own, logs, *theirs, *prior)
+    return out, later
+
+
+def finish_part(first, heads, scaled, shares, theirs, out):
+    groups = len(theirs)
     return pl.pallas_call(
-        functools.partial(combine_kernel, chunk, heads, groups),
-        grid=(1,),
-        in_specs=specs,
-        out_specs=block,
-        out_shape=jax.ShapeDtypeStruct(own.shape, jnp.bfloat16),
-        input_output_aliases=aliases,
+        functools.partial(finish_kernel, first, heads, groups),
+        in_specs=[in_vmem()] * (1 + 2 * groups) + [pl.BlockSpec(memory_space=pl.ANY)],
+        out_specs=pl.BlockSpec(memory_space=pl.ANY),
+        out_shape=jax.ShapeDtypeStruct(out.shape, out.dtype),
+        scratch_shapes=copy_scratch(heads),
+        input_output_aliases={1 + 2 * groups: 0},
         compiler_params=pltpu.CompilerParams(vmem_limit_bytes=VMEM_BYTES),
-        cost_estimate=pl.CostEstimate(
-            flops=8 * heads * ROWS * HD, bytes_accessed=heads * 8 * ROWS * HD, transcendentals=0
-        ),
-        name="combine_part",
-    )(*operands)
+        cost_estimate=merge_cost(heads),
+        name="finish_part",
+    )(scaled, *shares, *theirs, out)
 
 
 def frame_pairs(first, frames, cores):
@@ -250,18 +314,27 @@
 
     answers = []
     k_now, v_now = k, v
-    for (a, b), chunk_q, (even, odd) in zip(bounds, got_q, sides):
-        parts = [remote_part(a, b - a, one, k_now, v_now, even, odd) for one in chunk_q]
-        answers.append(parts)
+    for (a, b), tail, chunk_q, (even, odd) in zip(bounds, TAILS, got_q, sides):
+        parts = [remote_part(a, b - a, tail, one, k_now, v_now, even, odd) for one in chunk_q]
+        answers.append([list(x) for x in zip(*parts)])
         k_now, v_now, _ = lax.optimization_barrier((k, v, parts))
 
+    back = [route for _, route in routes]
+
+    def send_back(parts):
+        return [lax.ppermute(x, "row", p) for x, p in zip(parts, back)]
+
     q_local, _ = lax.optimization_barrier((q, answers))
-    own, logs = local_part(splits, q_local, k, v, [s for pair in sides for s in pair])
-
-    out = None
-    for c, ((a, b), parts) in enumerate(zip(bounds, answers)):
-        theirs = [lax.ppermute(p, "row", back) for p, (_, back) in zip(parts, routes)]
-        out = combine_part(c, b - a, own, logs, theirs, out)
+    own, *logs = local_part(splits, q_local, k, v, [s for pair in sides for s in pair])
+    out = ()
+    for (a, b), tail, log, parts in zip(bounds, TAILS, logs, answers):
+        theirs = send_back(parts[0])
+        out, later = merge_part(a, b - a - tail, tail, own, log, theirs, out)
+        if tail:
+            last, _ = lax.optimization_barrier((parts[1], log))
+            out = finish_part(b - tail, tail, later[0], later[1:], send_back(last), out)
+        out = (out,)
+    (out,) = out
     return out.reshape(query.shape)
 
 

time: 40.6 us -> 39.8 us (0.980)
  waiting for transfers between devices: 18.1 us -> 15.4 us
  starting transfers between devices: 9.3 us -> 10.8 us
  Pallas kernels: 10.1 us -> 10.6 us
    ppermute x2 -> x3, waiting for transfers between devices: 7.1 us -> 4.4 us  [send_back(): return [lax.ppermute(x, 'row', p) for x, p in zip(parts, back)]]
    ppermute x2 -> x3, starting transfers between devices: 1.7 us -> 3.24 us  [send_back(): return [lax.ppermute(x, 'row', p) for x, p in zip(parts, back)]]
    pallas_call x4 -> x5, Pallas kernels: 6.76 us -> 7.17 us  [the longest x2 4.04 us: remote_part(): pl.pallas_call(functools.partial(remote_kernel, first, heads, tail), in_s...]
  transfers between devices with their start and end apart: 8 -> 9, of which waited for: 6 -> 6; matrix products, arithmetic and copies ran while one was open for 4% -> 4% of each run, Pallas kernels for 22% -> 25%
where the time goes in v3:
time: 39.8 us; the launch traced here: 39.6 us
  waiting for transfers between devices  15.4 us (39%)
  starting transfers between devices  10.8 us (27%)
  Pallas kernels  10.6 us (27%)
  local copies, waits for them, and re-layouts  2.55 us (6%)
    ppermute x2, waiting for transfers between devices, per_device(): got_q.append([lax.ppermute(sent, 'row', there) for there, _ in routes])  7.6 us
    ppermute x3, waiting for transfers between devices, send_back(): return [lax.ppermute(x, 'row', p) for x, p in zip(parts, back)]  4.4 us
    pallas_call x2, Pallas kernels, remote_part(): pl.pallas_call(functools.partial(remote_kernel, first, heads, tail), in_s...  4.04 us
    ppermute x4, starting transfers between devices, per_device(): lax.ppermute(h, ('frame', 'head'), p)  3.99 us
    ppermute x2, starting transfers between devices, per_device(): got_q.append([lax.ppermute(sent, 'row', there) for there, _ in routes])  3.6 us
    ppermute x4, waiting for transfers between devices, per_device(): lax.ppermute(h, ('frame', 'head'), p)  3.41 us
    pallas_call x1, Pallas kernels, local_part(): pl.pallas_call(functools.partial(local_kernel, splits), in_specs=[in_vmem...  3.39 us
    ppermute x3, starting transfers between devices, send_back(): return [lax.ppermute(x, 'row', p) for x, p in zip(parts, back)]  3.24 us
  transfers between devices with their start and end apart: 9, of which 6 were waited for; matrix products, arithmetic and copies ran while one was open for 4% of the time, Pallas kernels for 25%

profile of v3, /device:TPU:0, one launch (start us, length us, event | category | flops | bytes accessed | tf_op | source)
XLA Modules:
  0.0 39.6 jit_solution(4670649262006870678)
XLA Ops:
  0.0 1.0 %slice.8 = bf16[512,384]{1,0:T(8,128)(2,1)S(1)} slice(bf16[512,768]{1,0:T(8,128)(2,1)} %bitcast.14), slice={[0:512], [0:384]} | slice | bytes 786432 | tf_op jit(solution)/shard_map/slice | solution.py:303
  1.0 3.0 %collective-permute-start = (bf16[512,384]{1,0:T(8,128)(2,1)S(1)}, bf16[512,384]{1,0:T(8,128)(2,1)S(1)}, u32[]{:S(2)}, u32[]{:S(2)}) collective-permute-start(bf16[512,384]{1,0:T(8,128)(2,1)S(1)} %slice.8), channel_id=1, source_target_pairs={{0,2},{2,0},{1,3},{3,1},{4,6},{6,4},{5,7},{7,5},{8,10},{10,8},{9,1... | collective-permute-start | bytes 1179656 | tf_op jit(solution)/shard_map/ppermute | solution.py:304
  4.0 0.0 copy-start.2
  4.0 1.4 %constant_dynamic-slice_fusion.4 = (bf16[256,384]{1,0:T(8,128)(2,1)S(1)}, bf16[256,384]{1,0:T(8,128)(2,1)S(1)}, bf16[256,384]{1,0:T(8,128)(2,1)S(1)}, bf16[256,384]{1,0:T(8,128)(2,1)S(1)}) fusion(bf16[512,768]{1,0:T(8,128)(2,1)} %bitcast.9, s32[]{:T(128)S(6)} %select_n.18, s32[]{:T(128)S(6)} %select_n.9, bf16[512,768]{1,0:T(8,128)(2,1)} %bitcast.4), kind=kLoop, calls=%fused_computation.8 | loop fusion | bytes 1572872 | tf_op jit(solution)/shard_map/dynamic_slice | solution.py:310
  5.4 0.0 copy-start
  5.4 0.0 copy-start.1
  5.5 1.6 %collective-permute-start.1 = (bf16[512,384]{1,0:T(8,128)(2,1)S(1)}, bf16[512,384]{1,0:T(8,128)(2,1)S(1)}, u32[]{:S(2)}, u32[]{:S(2)}) collective-permute-start(bf16[512,384]{1,0:T(8,128)(2,1)S(1)} %pad_maximum_fusion), channel_id=1, source_target_pairs={{0,4},{1,5},{4,0},{5,1},{8,12},{9,13},{12,8},{13,9},{2,6},{3,7},{6... | collective-permute-start | bytes 1179656 | tf_op jit(solution)/shard_map/ppermute | solution.py:313
  7.2 0.1 collective-permute-start.2
  7.2 0.0 copy-done.2
  7.3 0.6 %collective-permute-start.3 = (bf16[512,384]{1,0:T(8,128)(2,1)S(1)}, bf16[512,384]{1,0:T(8,128)(2,1)S(1)}, u32[]{:S(2)}, u32[]{:S(2)}) collective-permute-start(bf16[512,384]{1,0:T(8,128)(2,1)S(1)} %slice.7), channel_id=1, source_target_pairs={{0,2},{2,0},{1,3},{3,1},{4,6},{6,4},{5,7},{7,5},{8,10},{10,8},{9,1... | collective-permute-start | bytes 1179656 | tf_op jit(solution)/shard_map/ppermute | solution.py:304
  7.9 6.1 %collective-permute-done.q = bf16[512,384]{1,0:T(8,128)(2,1)S(1)} collective-permute-done((bf16[512,384]{1,0:T(8,128)(2,1)S(1)}, bf16[512,384]{1,0:T(8,128)(2,1)S(1)}, u32[]{:S(2)}, u32[]{:S(2)}) %collective-permute-start) | collective-permute-done | bytes 393248 | tf_op jit(solution)/shard_map/ppermute | solution.py:304
  14.0 0.0 copy-done
  14.0 0.0 copy-done.1
  14.0 0.1 constant_dynamic-slice_fusion
  14.2 2.2 %collective-permute-start.4 = (bf16[512,384]{1,0:T(8,128)(2,1)S(1)}, bf16[512,384]{1,0:T(8,128)(2,1)S(1)}, u32[]{:S(2)}, u32[]{:S(2)}) collective-permute-start(bf16[512,384]{1,0:T(8,128)(2,1)S(1)} %pad_maximum_fusion.2), channel_id=1, source_target_pairs={{0,4},{1,5},{4,0},{5,1},{8,12},{9,13},{12,8},{13,9},{2,6},{3,7},{6... | collective-permute-start | bytes 1179656 | tf_op jit(solution)/shard_map/ppermute | solution.py:313
  16.4 0.1 collective-permute-start.5
  16.5 0.4 %collective-permute-done.1.even.rest_0_ = bf16[512,384]{1,0:T(8,128)(2,1)S(1)} collective-permute-done((bf16[512,384]{1,0:T(8,128)(2,1)S(1)}, bf16[512,384]{1,0:T(8,128)(2,1)S(1)}, u32[]{:S(2)}, u32[]{:S(2)}) %collective-permute-start.1) | collective-permute-done | bytes 393248 | tf_op jit(solution)/shard_map/ppermute | solution.py:313
  16.9 0.0 collective-permute-done.2.odd.rest_1_
  16.9 2.0 %remote_part.2 = bf16[528,384]{1,0:T(8,128)(2,1)S(1)} custom-call(bf16[512,384]{1,0:T(8,128)(2,1)S(1)} %collective-permute-done.q, bf16[512,768]{1,0:T(8,128)(2,1)S(1)} %bitcast.6, bf16[512,768]{1,0:T(8,128)(2,1)S(1)} %bitcast.11, bf16[512,384]{1,0:T(8,128)(2,1)S(1)} %collective-permute-done.1.even.rest_0_, ...), custom_call_target="tpu_custom_call" | custom-call | flops 603979776 | bytes 1572864 | tf_op jit(solution)/shard_map/remote_part/pallas_call | solution.py:195
  19.0 1.1 %collective-permute-start.7 = (bf16[528,384]{1,0:T(8,128)(2,1)S(1)}, bf16[528,384]{1,0:T(8,128)(2,1)S(1)}, u32[]{:S(2)}, u32[]{:S(2)}) collective-permute-start(bf16[528,384]{1,0:T(8,128)(2,1)S(1)} %remote_part.2), channel_id=1, source_target_pairs={{0,2},{2,0},{1,3},{3,1},{4,6},{6,4},{5,7},{7,5},{8,10},{10,8},{9,1... | collective-permute-start | bytes 1216520 | tf_op jit(solution)/shard_map/ppermute | solution.py:325
  20.1 1.5 %collective-permute-done.3.q = bf16[512,384]{1,0:T(8,128)(2,1)S(1)} collective-permute-done((bf16[512,384]{1,0:T(8,128)(2,1)S(1)}, bf16[512,384]{1,0:T(8,128)(2,1)S(1)}, u32[]{:S(2)}, u32[]{:S(2)}) %collective-permute-start.3) | collective-permute-done | bytes 393248 | tf_op jit(solution)/shard_map/ppermute | solution.py:304
  21.6 3.0 %collective-permute-done.4.even.rest_2_ = bf16[512,384]{1,0:T(8,128)(2,1)S(1)} collective-permute-done((bf16[512,384]{1,0:T(8,128)(2,1)S(1)}, bf16[512,384]{1,0:T(8,128)(2,1)S(1)}, u32[]{:S(2)}, u32[]{:S(2)}) %collective-permute-start.4) | collective-permute-done | bytes 393248 | tf_op jit(solution)/shard_map/ppermute | solution.py:313
  24.6 0.0 collective-permute-done.5.odd.rest_3_
  24.6 2.0 %remote_part.3 = (bf16[528,256]{1,0:T(8,128)(2,1)S(1)}, bf16[512,128]{1,0:T(8,128)(2,1)S(1)}) custom-call(bf16[512,384]{1,0:T(8,128)(2,1)S(1)} %collective-permute-done.3.q, bf16[512,768]{1,0:T(8,128)(2,1)S(1)} %bitcast.7, bf16[512,768]{1,0:T(8,128)(2,1)S(1)} %bitcast.12, bf16[512,384]{1,0:T(8,128)(2,1)S(1)} %collective-permute-done.4.even.rest_2_, ...), custom_call_target="tpu_custom_call" | custom-call | flops 603979776 | bytes 1572864 | tf_op jit(solution)/shard_map/remote_part/pallas_call | solution.py:195
  26.6 0.6 %collective-permute-start.6 = (bf16[528,256]{1,0:T(8,128)(2,1)S(1)}, bf16[528,256]{1,0:T(8,128)(2,1)S(1)}, u32[]{:S(2)}, u32[]{:S(2)}) collective-permute-start(bf16[528,256]{1,0:T(8,128)(2,1)S(1)} %get-tuple-element.29), channel_id=1, source_target_pairs={{0,2},{2,0},{1,3},{3,1},{4,6},{6,4},{5,7},{7,5},{8,10},{10,8},{9,1... | collective-permute-start | bytes 811016 | tf_op jit(solution)/shard_map/ppermute | solution.py:325
  27.2 3.4 %local_part.1 = (f32[512,768]{1,0:T(8,128)S(1)}, f32[128,128]{1,0:T(8,128)S(1)}, f32[128,128]{1,0:T(8,128)S(1)}) custom-call(bf16[512,768]{1,0:T(8,128)(2,1)S(1)} %bitcast.16, bf16[512,768]{1,0:T(8,128)(2,1)S(1)} %bitcast.8, bf16[512,768]{1,0:T(8,128)(2,1)S(1)} %bitcast.13, bf16[512,384]{1,0:T(8,128)(2,1)S(1)} %collective-permute-done.1.even.rest_0_, ...), custom_call_target="tpu_custom_call" | custom-call | flops 1207959552 | bytes 3145728 | tf_op jit(solution)/shard_map/local_part/pallas_call | solution.py:208
  30.6 1.5 %collective-permute-start.8 = (bf16[512,128]{1,0:T(8,128)(2,1)S(1)}, bf16[512,128]{1,0:T(8,128)(2,1)S(1)}, u32[]{:S(2)}, u32[]{:S(2)}) collective-permute-start(bf16[512,128]{1,0:T(8,128)(2,1)S(1)} %get-tuple-element.37), channel_id=1, source_target_pairs={{0,2},{2,0},{1,3},{3,1},{4,6},{6,4},{5,7},{7,5},{8,10},{10,8},{9,1... | collective-permute-start | bytes 393224 | tf_op jit(solution)/shard_map/ppermute | solution.py:325
  32.1 0.0 collective-permute-done.7.rest_0_
  32.1 1.3 %merge_part.2.rest_1_ = bf16[512,768]{1,0:T(8,128)(2,1)} custom-call(f32[512,768]{1,0:T(8,128)S(1)} %get-tuple-element.32.own, f32[128,128]{1,0:T(8,128)S(1)} %get-tuple-element.34.logs, bf16[528,384]{1,0:T(8,128)(2,1)S(1)} %collective-permute-done.7.rest_0_), custom_call_target="tpu_custom_call" | custom-call | flops 786432 | bytes 1572864 | tf_op jit(solution)/shard_map/merge_part/pallas_call | solution.py:235
  33.4 3.6 %collective-permute-done.6.rest_0_ = bf16[528,256]{1,0:T(8,128)(2,1)S(1)} collective-permute-done((bf16[528,256]{1,0:T(8,128)(2,1)S(1)}, bf16[528,256]{1,0:T(8,128)(2,1)S(1)}, u32[]{:S(2)}, u32[]{:S(2)}) %collective-permute-start.6) | collective-permute-done | bytes 270368 | tf_op jit(solution)/shard_map/ppermute | solution.py:325
  37.0 1.1 %merge_part.3 = (bf16[512,768]{1,0:T(8,128)(2,1)}, f32[512,128]{1,0:T(8,128)S(1)}, f32[512,128]{1,0:T(8,128)S(1)}) custom-call(f32[512,768]{1,0:T(8,128)S(1)} %get-tuple-element.32.own, f32[128,128]{1,0:T(8,128)S(1)} %get-tuple-element.33.logs, bf16[528,256]{1,0:T(8,128)(2,1)S(1)} %collective-permute-done.6.rest_0_, ...), custom_call_target="tpu_custom_call", output_to_operand_aliasing={{0}: (3, {})} | custom-call | flops 786432 | bytes 1572864 | tf_op jit(solution)/shard_map/merge_part/pallas_call | solution.py:235
  38.2 0.8 %collective-permute-done.8.rest_1_ = bf16[512,128]{1,0:T(8,128)(2,1)S(1)} collective-permute-done((bf16[512,128]{1,0:T(8,128)(2,1)S(1)}, bf16[512,128]{1,0:T(8,128)(2,1)S(1)}, u32[]{:S(2)}, u32[]{:S(2)}) %collective-permute-start.8) | collective-permute-done | bytes 131104 | tf_op jit(solution)/shard_map/ppermute | solution.py:325
  38.9 0.7 %finish_part.1 = bf16[512,768]{1,0:T(8,128)(2,1)} custom-call(f32[512,128]{1,0:T(8,128)S(1)} %get-tuple-element.35.scaled, f32[512,128]{1,0:T(8,128)S(1)} %get-tuple-element.36.rest_0_, bf16[512,128]{1,0:T(8,128)(2,1)S(1)} %collective-permute-done.8.rest_1_, bf16[512,768]{1,0:T(8,128)(2,1)} %get-tuple-element.38.rest_2_), custom_call_target="tpu_custom_call", output_to_operand_aliasing={{}: (3, {})} | custom-call | flops 262144 | bytes 524288 | tf_op jit(solution)/shard_map/finish_part/pallas_call | solution.py:251
  (6 shorter events, 0.2 us)
Async XLA Ops:
  1.0 12.9 %collective-permute-start = (bf16[512,384]{1,0:T(8,128)(2,1)S(1)}, bf16[512,384]{1,0:T(8,128)(2,1)S(1)}, u32[]{:S(2)}, u32[]{:S(2)}) collective-permute-start(bf16[512,384]{1,0:T(8,128)(2,1)S(1)} %slice.8), channel_id=1, source_target_pairs={{0,2},{2,0},{1,3},{3,1},{4,6},{6,4},{5,7},{7,5},{8,10},{10,8},{9,1... | collective-permute-start | bytes 1179656 | tf_op jit(solution)/shard_map/ppermute | solution.py:304
  4.0 3.2 %copy-start.2 = (bf16[8,8,8,768]{3,2,1,0:T(8,128)(2,1)S(1)}, bf16[8,8,8,768]{3,2,1,0:T(8,128)(2,1)}, u32[]{:S(2)}) copy-start(bf16[8,8,8,768]{3,2,1,0:T(8,128)(2,1)} %param.3) | copy-start | bytes 2359300
  5.4 8.6 %copy-start = (bf16[8,8,8,768]{3,2,1,0:T(8,128)(2,1)S(1)}, bf16[8,8,8,768]{3,2,1,0:T(8,128)(2,1)}, u32[]{:S(2)}) copy-start(bf16[8,8,8,768]{3,2,1,0:T(8,128)(2,1)} %param.4) | copy-start | bytes 2359300
  5.4 8.6 %copy-start.1 = (bf16[8,8,8,768]{3,2,1,0:T(8,128)(2,1)S(1)}, bf16[8,8,8,768]{3,2,1,0:T(8,128)(2,1)}, u32[]{:S(2)}) copy-start(bf16[8,8,8,768]{3,2,1,0:T(8,128)(2,1)} %param.5) | copy-start | bytes 2359300
  5.5 11.4 %collective-permute-start.1 = (bf16[512,384]{1,0:T(8,128)(2,1)S(1)}, bf16[512,384]{1,0:T(8,128)(2,1)S(1)}, u32[]{:S(2)}, u32[]{:S(2)}) collective-permute-start(bf16[512,384]{1,0:T(8,128)(2,1)S(1)} %pad_maximum_fusion), channel_id=1, source_target_pairs={{0,4},{1,5},{4,0},{5,1},{8,12},{9,13},{12,8},{13,9},{2,6},{3,7},{6... | collective-permute-start | bytes 1179656 | tf_op jit(solution)/shard_map/ppermute | solution.py:313
  7.2 9.8 %collective-permute-start.2 = (bf16[512,384]{1,0:T(8,128)(2,1)S(1)}, bf16[512,384]{1,0:T(8,128)(2,1)S(1)}, u32[]{:S(2)}, u32[]{:S(2)}) collective-permute-start(bf16[512,384]{1,0:T(8,128)(2,1)S(1)} %pad_maximum_fusion.1), channel_id=1, source_target_pairs={{0,1},{1,0},{4,8},{5,9},{8,4},{9,5},{12,13},{13,12},{2,3},{3,2},{6... | collective-permute-start | bytes 1179656 | tf_op jit(solution)/shard_map/ppermute | solution.py:313
  7.3 14.3 %collective-permute-start.3 = (bf16[512,384]{1,0:T(8,128)(2,1)S(1)}, bf16[512,384]{1,0:T(8,128)(2,1)S(1)}, u32[]{:S(2)}, u32[]{:S(2)}) collective-permute-start(bf16[512,384]{1,0:T(8,128)(2,1)S(1)} %slice.7), channel_id=1, source_target_pairs={{0,2},{2,0},{1,3},{3,1},{4,6},{6,4},{5,7},{7,5},{8,10},{10,8},{9,1... | collective-permute-start | bytes 1179656 | tf_op jit(solution)/shard_map/ppermute | solution.py:304
  14.2 10.4 %collective-permute-start.4 = (bf16[512,384]{1,0:T(8,128)(2,1)S(1)}, bf16[512,384]{1,0:T(8,128)(2,1)S(1)}, u32[]{:S(2)}, u32[]{:S(2)}) collective-permute-start(bf16[512,384]{1,0:T(8,128)(2,1)S(1)} %pad_maximum_fusion.2), channel_id=1, source_target_pairs={{0,4},{1,5},{4,0},{5,1},{8,12},{9,13},{12,8},{13,9},{2,6},{3,7},{6... | collective-permute-start | bytes 1179656 | tf_op jit(solution)/shard_map/ppermute | solution.py:313
  16.4 8.2 %collective-permute-start.5 = (bf16[512,384]{1,0:T(8,128)(2,1)S(1)}, bf16[512,384]{1,0:T(8,128)(2,1)S(1)}, u32[]{:S(2)}, u32[]{:S(2)}) collective-permute-start(bf16[512,384]{1,0:T(8,128)(2,1)S(1)} %pad_maximum_fusion.3), channel_id=1, source_target_pairs={{0,1},{1,0},{4,8},{5,9},{8,4},{9,5},{12,13},{13,12},{2,3},{3,2},{6... | collective-permute-start | bytes 1179656 | tf_op jit(solution)/shard_map/ppermute | solution.py:313
  19.0 13.1 %collective-permute-start.7 = (bf16[528,384]{1,0:T(8,128)(2,1)S(1)}, bf16[528,384]{1,0:T(8,128)(2,1)S(1)}, u32[]{:S(2)}, u32[]{:S(2)}) collective-permute-start(bf16[528,384]{1,0:T(8,128)(2,1)S(1)} %remote_part.2), channel_id=1, source_target_pairs={{0,2},{2,0},{1,3},{3,1},{4,6},{6,4},{5,7},{7,5},{8,10},{10,8},{9,1... | collective-permute-start | bytes 1216520 | tf_op jit(solution)/shard_map/ppermute | solution.py:325
  26.6 10.5 %collective-permute-start.6 = (bf16[528,256]{1,0:T(8,128)(2,1)S(1)}, bf16[528,256]{1,0:T(8,128)(2,1)S(1)}, u32[]{:S(2)}, u32[]{:S(2)}) collective-permute-start(bf16[528,256]{1,0:T(8,128)(2,1)S(1)} %get-tuple-element.29), channel_id=1, source_target_pairs={{0,2},{2,0},{1,3},{3,1},{4,6},{6,4},{5,7},{7,5},{8,10},{10,8},{9,1... | collective-permute-start | bytes 811016 | tf_op jit(solution)/shard_map/ppermute | solution.py:325
  30.6 8.4 %collective-permute-start.8 = (bf16[512,128]{1,0:T(8,128)(2,1)S(1)}, bf16[512,128]{1,0:T(8,128)(2,1)S(1)}, u32[]{:S(2)}, u32[]{:S(2)}) collective-permute-start(bf16[512,128]{1,0:T(8,128)(2,1)S(1)} %get-tuple-element.37), channel_id=1, source_target_pairs={{0,2},{2,0},{1,3},{3,1},{4,6},{6,4},{5,7},{7,5},{8,10},{10,8},{9,1... | collective-permute-start | bytes 393224 | tf_op jit(solution)/shard_map/ppermute | solution.py:325

commit v4 on v3

--- a/solution.py
+++ b/solution.py
@@ -20,7 +20,9 @@
 BLOCKS = ROWS // HD
 LOG_ROWS = 16
 CHUNKS = (3, 3)
+LEADS = (1, 0)
 TAILS = (0, 1)
+CYCLES = (((2, 0), (0, 1), (1, 3), (3, 2)), ((0, 2), (2, 3), (3, 1), (1, 0)))
 VMEM_BYTES = 48 * 1024 * 1024
 
 
@@ -28,7 +30,7 @@
     return lax.dot_general(a, b, dims, preferred_element_type=jnp.float32)
 
 
-def attend(first, heads, q, k, v, even, odd, store):
+def attend(first, heads, q, k, v, even, odd, store, slot=0):
     place = lax.axis_index("frame")
     present = (place > 0, place < lax.axis_size("frame") - 1)
     is_even = lax.rem(place, 2) == 0
@@ -60,7 +62,7 @@
             store(rows, here, summed[:, :HD] / total)
             log = peak * EXPONENT + jnp.log2(total[:, :1])
             for i in range(TILE // HD):
-                at = (t * (TILE // HD) + i) * (LOG_ROWS // BLOCKS) + j
+                at = (t * (TILE // HD) + i) * (LOG_ROWS // BLOCKS) + slot + j
                 logs = jnp.where(lanes == at, log[i * HD : (i + 1) * HD], logs)
     return logs
 
@@ -77,7 +79,16 @@
     return jnp.concatenate([flat, jnp.zeros((HD - LOG_ROWS, HD), jnp.float32)], 0).T
 
 
-def remote_kernel(first, heads, tail, q, k, v, even, odd, out, *last):
+def lead_kernel(first, heads, q, k, v, even, odd, out, logs):
+    def store(rows, here, block):
+        out[rows, here] = block.astype(out.dtype)
+
+    logs[...] = attend(first, heads, q, k, v, even, odd, store)
+
+
+def remote_kernel(first, heads, lead, tail, q, k, v, even, odd, *rest):
+    earlier, (out, *last) = rest[: lead > 0], rest[lead > 0 :]
+
     def store(rows, here, block):
         start = here.start - (heads - tail) * HD
         if start < 0:
@@ -85,7 +96,10 @@
         else:
             last[0][rows, start : start + HD] = block.astype(out.dtype)
 
-    packed = pack_logs(attend(first, heads, q, k, v, even, odd, store))
+    q_here = q.at[:, lead * HD : (lead + heads) * HD]
+    sides = [x.at[:, lead * HD : (lead + heads) * HD] for x in (even, odd)]
+    logs = attend(first, heads, q_here, k, v, *sides, store, lead)
+    packed = pack_logs(logs + earlier[0][...] if lead else logs)
     out[ROWS:, : 2 * HD] = packed
     if out.shape[1] > 2 * HD:
         out[ROWS:, 2 * HD :] = jnp.zeros((LOG_ROWS, out.shape[1] - 2 * HD), out.dtype)
@@ -138,7 +152,8 @@
     return copies
 
 
-def merge_kernel(first, heads, tail, groups, own, logs, *rest):
+def merge_kernel(first, lead, heads, tail, groups, own, logs, *rest):
+    leads, rest = rest[: groups * (lead > 0)], rest[groups * (lead > 0) :]
     theirs, (mixed, done) = rest[:groups], rest[-2:]
     out, *later = rest[-3 - (1 + groups) * (tail > 0) : -2]
     shares = shares_of(logs, theirs)
@@ -148,8 +163,10 @@
             here = slice(j * HD, (j + 1) * HD)
             at = b * (LOG_ROWS // BLOCKS) + j
             summed = shares[0][:, at : at + 1] * own[rows, (first + j) * HD : (first + j + 1) * HD]
-            for share, part in zip(shares[1:], theirs):
-                summed = summed + share[:, at : at + 1] * part[rows, here].astype(jnp.float32)
+            parts, start = (leads, j * HD) if j < lead else (theirs, (j - lead) * HD)
+            for share, part in zip(shares[1:], parts):
+                block = part[rows, start : start + HD].astype(jnp.float32)
+                summed = summed + share[:, at : at + 1] * block
             mixed[rows, here] = summed.astype(mixed.dtype)
 
     copies = write_columns(first, heads, mixed, out, done, fill)
@@ -165,7 +182,7 @@
         copy.wait()
 
 
-def finish_kernel(first, heads, groups, scaled, *rest):
+def finish_kernel(first, heads, groups, turn, scaled, *rest):
     shares, theirs = rest[:groups], rest[groups : 2 * groups]
     out, mixed, done = rest[-3:]
 
@@ -175,8 +192,15 @@
             summed = summed + share[rows, :] * part[rows, :].astype(jnp.float32)
         mixed[rows, :] = summed.astype(mixed.dtype)
 
-    for copy in write_columns(first, heads, mixed, out, done, fill):
-        copy.wait()
+    def finish():
+        for copy in write_columns(first, heads, mixed, out, done, fill):
+            copy.wait()
+
+    if turn is None:
+        finish()
+    else:
+        place = lax.axis_index("row") + lax.axis_index("head")
+        pl.when(lax.rem(place, 2) == turn)(finish)
 
 
 def cost(heads, tiles=6):
@@ -190,17 +214,32 @@
     return pl.BlockSpec(memory_space=pltpu.VMEM)
 
 
-def remote_part(first, heads, tail, q, k, v, even, odd):
+def lead_part(first, heads, q, k, v, even, odd):
+    return pl.pallas_call(
+        functools.partial(lead_kernel, first, heads),
+        in_specs=[in_vmem()] * 5,
+        out_specs=[in_vmem()] * 2,
+        out_shape=[
+            jax.ShapeDtypeStruct((ROWS, heads * HD), jnp.bfloat16),
+            jax.ShapeDtypeStruct((HD, HD), jnp.float32),
+        ],
+        compiler_params=pltpu.CompilerParams(vmem_limit_bytes=VMEM_BYTES),
+        cost_estimate=cost(heads),
+        name="lead_part",
+    )(q, k, v, even, odd)
+
+
+def remote_part(first, heads, lead, tail, q, k, v, even, odd, *earlier):
     shapes = [(ROWS + LOG_ROWS, (heads - tail) * HD)] + [(ROWS, tail * HD)] * (tail > 0)
     return pl.pallas_call(
-        functools.partial(remote_kernel, first, heads, tail),
-        in_specs=[in_vmem()] * 5,
+        functools.partial(remote_kernel, first, heads, lead, tail),
+        in_specs=[in_vmem()] * (5 + len(earlier)),
         out_specs=[in_vmem()] * len(shapes),
         out_shape=[jax.ShapeDtypeStruct(shape, jnp.bfloat16) for shape in shapes],
         compiler_params=pltpu.CompilerParams(vmem_limit_bytes=VMEM_BYTES),
         cost_estimate=cost(heads),
         name="remote_part",
-    )(q, k, v, even, odd)
+    )(q, k, v, even, odd, *earlier)
 
 
 def local_part(splits, q, k, v, sides):
@@ -229,27 +268,28 @@
     return [pltpu.VMEM((ROWS, heads * HD), jnp.bfloat16), pltpu.SemaphoreType.DMA((BLOCKS,))]
 
 
-def merge_part(first, heads, tail, own, logs, theirs, prior):
+def merge_part(first, lead, heads, tail, own, logs, leads, theirs, prior):
     groups = len(theirs)
+    count = len(leads) + groups
     later = [jax.ShapeDtypeStruct((ROWS, tail * HD), jnp.float32)] * ((1 + groups) * (tail > 0))
     out, *later = pl.pallas_call(
-        functools.partial(merge_kernel, first, heads, tail, groups),
-        in_specs=[in_vmem()] * (2 + groups) + [pl.BlockSpec(memory_space=pl.ANY)] * len(prior),
+        functools.partial(merge_kernel, first, lead, heads, tail, groups),
+        in_specs=[in_vmem()] * (2 + count) + [pl.BlockSpec(memory_space=pl.ANY)] * len(prior),
         out_specs=[pl.BlockSpec(memory_space=pl.ANY)] + [in_vmem()] * len(later),
         out_shape=[jax.ShapeDtypeStruct(own.shape, jnp.bfloat16)] + later,
         scratch_shapes=copy_scratch(heads),
-        input_output_aliases={2 + groups: 0} if prior else {},
+        input_output_aliases={2 + count: 0} if prior else {},
         compiler_params=pltpu.CompilerParams(vmem_limit_bytes=VMEM_BYTES),
         cost_estimate=merge_cost(heads + tail),
         name="merge_part",
-    )(own, logs, *theirs, *prior)
+    )(own, logs, *leads, *theirs, *prior)
     return out, later
 
 
-def finish_part(first, heads, scaled, shares, theirs, out):
+def finish_part(first, heads, scaled, shares, theirs, out, turn=None):
     groups = len(theirs)
     return pl.pallas_call(
-        functools.partial(finish_kernel, first, heads, groups),
+        functools.partial(finish_kernel, first, heads, groups, turn),
         in_specs=[in_vmem()] * (1 + 2 * groups) + [pl.BlockSpec(memory_space=pl.ANY)],
         out_specs=pl.BlockSpec(memory_space=pl.ANY),
         out_shape=jax.ShapeDtypeStruct(out.shape, out.dtype),
@@ -312,27 +352,41 @@
         q_now, _ = lax.optimization_barrier((q, halves))
         sides.append([lax.ppermute(h, ("frame", "head"), p) for h, p in zip(halves, pairs)])
 
-    answers = []
-    k_now, v_now = k, v
-    for (a, b), tail, chunk_q, (even, odd) in zip(bounds, TAILS, got_q, sides):
-        parts = [remote_part(a, b - a, tail, one, k_now, v_now, even, odd) for one in chunk_q]
-        answers.append([list(x) for x in zip(*parts)])
-        k_now, v_now, _ = lax.optimization_barrier((k, v, parts))
-
     back = [route for _, route in routes]
 
     def send_back(parts):
         return [lax.ppermute(x, "row", p) for x, p in zip(parts, back)]
+
+    answers, led = [], []
+    k_now, v_now = k, v
+    for (a, b), lead, tail, chunk_q, (even, odd) in zip(bounds, LEADS, TAILS, got_q, sides):
+        parts, firsts = [], []
+        for one in chunk_q:
+            operands, earlier = (one, k_now, v_now, even, odd), ()
+            if lead:
+                block, *earlier = lead_part(a, lead, *operands)
+                firsts.append(block)
+                k_now, v_now, _ = lax.optimization_barrier((k, v, block))
+                operands = (one, k_now, v_now, even, odd)
+            parts.append(remote_part(a + lead, b - a - lead, lead, tail, *operands, *earlier))
+        led.append(send_back(firsts))
+        answers.append([list(x) for x in zip(*parts)])
+        k_now, v_now, _ = lax.optimization_barrier((k, v, (parts, led[-1])))
 
     q_local, _ = lax.optimization_barrier((q, answers))
     own, *logs = local_part(splits, q_local, k, v, [s for pair in sides for s in pair])
     out = ()
-    for (a, b), tail, log, parts in zip(bounds, TAILS, logs, answers):
+    for (a, b), lead, tail, log, leads, parts in zip(bounds, LEADS, TAILS, logs, led, answers):
         theirs = send_back(parts[0])
-        out, later = merge_part(a, b - a - tail, tail, own, log, theirs, out)
+        out, later = merge_part(a, lead, b - a - tail, tail, own, log, leads, theirs, out)
         if tail:
             last, _ = lax.optimization_barrier((parts[1], log))
-            out = finish_part(b - tail, tail, later[0], later[1:], send_back(last), out)
+            if rows == 2 and lax.axis_size("head") == 2:
+                for turn, cycle in enumerate(CYCLES):
+                    came = [lax.ppermute(last[0], ("row", "head"), cycle)]
+                    out = finish_part(b - tail, tail, later[0], later[1:], came, out, turn)
+            else:
+                out = finish_part(b - tail, tail, later[0], later[1:], send_back(last), out)
         out = (out,)
     (out,) = out
     return out.reshape(query.shape)

time: 39.8 us -> 39.7 us (level)
  waiting for transfers between devices: 15.4 us -> 11.9 us
  starting transfers between devices: 10.8 us -> 13.9 us
  Pallas kernels: 10.6 us -> 11 us
    ppermute x4, waiting for transfers between devices: 3.41 us -> 0.45 us  [per_device(): lax.ppermute(h, ('frame', 'head'), p)]
    ppermute x0 -> x2, starting transfers between devices: none -> 2.03 us  [per_device(): came = [lax.ppermute(last[0], ('row', 'head'), cycle)]]
    ppermute x2, waiting for transfers between devices: 7.6 us -> 6.08 us  [per_device(): got_q.append([lax.ppermute(sent, 'row', there) for there, _ in routes])]
    ppermute x3, starting transfers between devices: 3.24 us -> 4.22 us  [send_back(): return [lax.ppermute(x, 'row', p) for x, p in zip(parts, back)]]
    ppermute x0 -> x2, waiting for transfers between devices: none -> 0.83 us  [per_device(): came = [lax.ppermute(last[0], ('row', 'head'), cycle)]]
    pallas_call x5 -> x7, Pallas kernels: 7.17 us -> 7.64 us  [the longest x2 3.46 us: remote_part(): pl.pallas_call(functools.partial(remote_kernel, first, heads, lead, tail)...]
  transfers between devices with their start and end apart: 9 -> 11, of which waited for: 6 -> 5; matrix products, arithmetic and copies ran while one was open for 4% -> 4% of each run, Pallas kernels for 25% -> 28%
where the time goes in v4:
time: 39.7 us; the launch traced here: 39.6 us
  starting transfers between devices  13.9 us (35%)
  waiting for transfers between devices  11.9 us (30%)
  Pallas kernels  11 us (28%)
  local copies, waits for them, and re-layouts  2.55 us (6%)
    ppermute x2, waiting for transfers between devices, per_device(): got_q.append([lax.ppermute(sent, 'row', there) for there, _ in routes])  6.08 us
    ppermute x3, waiting for transfers between devices, send_back(): return [lax.ppermute(x, 'row', p) for x, p in zip(parts, back)]  4.52 us
    ppermute x3, starting transfers between devices, send_back(): return [lax.ppermute(x, 'row', p) for x, p in zip(parts, back)]  4.22 us
    ppermute x4, starting transfers between devices, per_device(): lax.ppermute(h, ('frame', 'head'), p)  3.99 us
    ppermute x2, starting transfers between devices, per_device(): got_q.append([lax.ppermute(sent, 'row', there) for there, _ in routes])  3.6 us
    pallas_call x2, Pallas kernels, remote_part(): pl.pallas_call(functools.partial(remote_kernel, first, heads, lead, tail)...  3.46 us
    pallas_call x1, Pallas kernels, local_part(): pl.pallas_call(functools.partial(local_kernel, splits), in_specs=[in_vmem...  3.33 us
    pallas_call x2, Pallas kernels, merge_part(): pl.pallas_call(functools.partial(merge_kernel, first, lead, heads, tail,...  2.44 us
  transfers between devices with their start and end apart: 11, of which 5 were waited for; matrix products, arithmetic and copies ran while one was open for 4% of the time, Pallas kernels for 28%

profile of v4, /device:TPU:0, one launch (start us, length us, event | category | flops | bytes accessed | tf_op | source)
XLA Modules:
  0.0 39.6 jit_solution(17718766362251163551)
XLA Ops:
  0.0 1.0 %slice.8 = bf16[512,384]{1,0:T(8,128)(2,1)S(1)} slice(bf16[512,768]{1,0:T(8,128)(2,1)} %bitcast.16), slice={[0:512], [0:384]} | slice | bytes 786432 | tf_op jit(solution)/shard_map/slice | solution.py:343
  1.0 3.0 %collective-permute-start = (bf16[512,384]{1,0:T(8,128)(2,1)S(1)}, bf16[512,384]{1,0:T(8,128)(2,1)S(1)}, u32[]{:S(2)}, u32[]{:S(2)}) collective-permute-start(bf16[512,384]{1,0:T(8,128)(2,1)S(1)} %slice.8), channel_id=1, source_target_pairs={{0,2},{2,0},{1,3},{3,1},{4,6},{6,4},{5,7},{7,5},{8,10},{10,8},{9,1... | collective-permute-start | bytes 1179656 | tf_op jit(solution)/shard_map/ppermute | solution.py:344
  4.0 0.0 copy-start.2
  4.0 1.4 %constant_dynamic-slice_fusion.4 = (bf16[256,384]{1,0:T(8,128)(2,1)S(1)}, bf16[256,384]{1,0:T(8,128)(2,1)S(1)}, bf16[256,384]{1,0:T(8,128)(2,1)S(1)}, bf16[256,384]{1,0:T(8,128)(2,1)S(1)}) fusion(bf16[512,768]{1,0:T(8,128)(2,1)} %bitcast.10, s32[]{:T(128)S(6)} %select_n.18, s32[]{:T(128)S(6)} %select_n.9, bf16[512,768]{1,0:T(8,128)(2,1)} %bitcast.4), kind=kLoop, calls=%fused_computation.8 | loop fusion | bytes 1572872 | tf_op jit(solution)/shard_map/dynamic_slice | solution.py:350
  5.4 0.0 copy-start.1
  5.4 0.0 copy-start
  5.5 1.6 %collective-permute-start.1 = (bf16[512,384]{1,0:T(8,128)(2,1)S(1)}, bf16[512,384]{1,0:T(8,128)(2,1)S(1)}, u32[]{:S(2)}, u32[]{:S(2)}) collective-permute-start(bf16[512,384]{1,0:T(8,128)(2,1)S(1)} %pad_maximum_fusion), channel_id=1, source_target_pairs={{0,4},{1,5},{4,0},{5,1},{8,12},{9,13},{12,8},{13,9},{2,6},{3,7},{6... | collective-permute-start | bytes 1179656 | tf_op jit(solution)/shard_map/ppermute | solution.py:353
  7.2 0.1 collective-permute-start.2
  7.2 0.0 copy-done.2
  7.3 0.6 %collective-permute-start.3 = (bf16[512,384]{1,0:T(8,128)(2,1)S(1)}, bf16[512,384]{1,0:T(8,128)(2,1)S(1)}, u32[]{:S(2)}, u32[]{:S(2)}) collective-permute-start(bf16[512,384]{1,0:T(8,128)(2,1)S(1)} %slice.7), channel_id=1, source_target_pairs={{0,2},{2,0},{1,3},{3,1},{4,6},{6,4},{5,7},{7,5},{8,10},{10,8},{9,1... | collective-permute-start | bytes 1179656 | tf_op jit(solution)/shard_map/ppermute | solution.py:344
  7.9 6.1 %collective-permute-done.q = bf16[512,384]{1,0:T(8,128)(2,1)S(1)} collective-permute-done((bf16[512,384]{1,0:T(8,128)(2,1)S(1)}, bf16[512,384]{1,0:T(8,128)(2,1)S(1)}, u32[]{:S(2)}, u32[]{:S(2)}) %collective-permute-start) | collective-permute-done | bytes 393248 | tf_op jit(solution)/shard_map/ppermute | solution.py:344
  14.0 0.0 copy-done.1
  14.0 0.0 copy-done
  14.0 0.1 constant_dynamic-slice_fusion.1
  14.2 2.2 %collective-permute-start.5 = (bf16[512,384]{1,0:T(8,128)(2,1)S(1)}, bf16[512,384]{1,0:T(8,128)(2,1)S(1)}, u32[]{:S(2)}, u32[]{:S(2)}) collective-permute-start(bf16[512,384]{1,0:T(8,128)(2,1)S(1)} %pad_maximum_fusion.2), channel_id=1, source_target_pairs={{0,4},{1,5},{4,0},{5,1},{8,12},{9,13},{12,8},{13,9},{2,6},{3,7},{6... | collective-permute-start | bytes 1179656 | tf_op jit(solution)/shard_map/ppermute | solution.py:353
  16.4 0.1 collective-permute-start.6
  16.5 0.4 %collective-permute-done.1.even.rest_0_ = bf16[512,384]{1,0:T(8,128)(2,1)S(1)} collective-permute-done((bf16[512,384]{1,0:T(8,128)(2,1)S(1)}, bf16[512,384]{1,0:T(8,128)(2,1)S(1)}, u32[]{:S(2)}, u32[]{:S(2)}) %collective-permute-start.1) | collective-permute-done | bytes 393248 | tf_op jit(solution)/shard_map/ppermute | solution.py:353
  16.9 0.0 collective-permute-done.2.odd.rest_1_
  16.9 1.0 %lead_part.1 = (bf16[512,128]{1,0:T(8,128)(2,1)S(1)}, f32[128,128]{1,0:T(8,128)S(1)}) custom-call(bf16[512,384]{1,0:T(8,128)(2,1)S(1)} %collective-permute-done.q, bf16[512,768]{1,0:T(8,128)(2,1)S(1)} %bitcast.6, bf16[512,768]{1,0:T(8,128)(2,1)S(1)} %bitcast.12, bf16[512,384]{1,0:T(8,128)(2,1)S(1)} %collective-permute-done.1.even.rest_0_, ...), custom_call_target="tpu_custom_call" | custom-call | flops 201326592 | bytes 524288 | tf_op jit(solution)/shard_map/lead_part/pallas_call | solution.py:218
  17.9 1.1 %collective-permute-start.4 = (bf16[512,128]{1,0:T(8,128)(2,1)S(1)}, bf16[512,128]{1,0:T(8,128)(2,1)S(1)}, u32[]{:S(2)}, u32[]{:S(2)}) collective-permute-start(bf16[512,128]{1,0:T(8,128)(2,1)S(1)} %get-tuple-element.28), channel_id=1, source_target_pairs={{0,2},{2,0},{1,3},{3,1},{4,6},{6,4},{5,7},{7,5},{8,10},{10,8},{9,1... | collective-permute-start | bytes 393224 | tf_op jit(solution)/shard_map/ppermute | solution.py:358
  19.0 1.5 %remote_part.2 = bf16[528,256]{1,0:T(8,128)(2,1)S(1)} custom-call(bf16[512,384]{1,0:T(8,128)(2,1)S(1)} %collective-permute-done.q, bf16[512,768]{1,0:T(8,128)(2,1)S(1)} %bitcast.7, bf16[512,768]{1,0:T(8,128)(2,1)S(1)} %bitcast.13, bf16[512,384]{1,0:T(8,128)(2,1)S(1)} %collective-permute-done.1.even.rest_0_, ...), custom_call_target="tpu_custom_call" | custom-call | flops 402653184 | bytes 1048576 | tf_op jit(solution)/shard_map/remote_part/pallas_call | solution.py:234
  20.5 1.0 %collective-permute-start.8 = (bf16[528,256]{1,0:T(8,128)(2,1)S(1)}, bf16[528,256]{1,0:T(8,128)(2,1)S(1)}, u32[]{:S(2)}, u32[]{:S(2)}) collective-permute-start(bf16[528,256]{1,0:T(8,128)(2,1)S(1)} %remote_part.2), channel_id=1, source_target_pairs={{0,2},{2,0},{1,3},{3,1},{4,6},{6,4},{5,7},{7,5},{8,10},{10,8},{9,1... | collective-permute-start | bytes 811016 | tf_op jit(solution)/shard_map/ppermute | solution.py:358
  21.5 3.7 %collective-permute-done.4.rest_0_ = bf16[512,128]{1,0:T(8,128)(2,1)S(1)} collective-permute-done((bf16[512,128]{1,0:T(8,128)(2,1)S(1)}, bf16[512,128]{1,0:T(8,128)(2,1)S(1)}, u32[]{:S(2)}, u32[]{:S(2)}) %collective-permute-start.4) | collective-permute-done | bytes 131104 | tf_op jit(solution)/shard_map/ppermute | solution.py:358
  25.2 0.0 collective-permute-done.3.q
  25.2 0.0 collective-permute-done.5.even.rest_2_
  25.2 0.0 collective-permute-done.6.odd.rest_3_
  25.2 2.0 %remote_part.3 = (bf16[528,256]{1,0:T(8,128)(2,1)S(1)}, bf16[512,128]{1,0:T(8,128)(2,1)S(1)}) custom-call(bf16[512,384]{1,0:T(8,128)(2,1)S(1)} %collective-permute-done.3.q, bf16[512,768]{1,0:T(8,128)(2,1)S(1)} %bitcast.8, bf16[512,768]{1,0:T(8,128)(2,1)S(1)} %bitcast.14, bf16[512,384]{1,0:T(8,128)(2,1)S(1)} %collective-permute-done.5.even.rest_2_, ...), custom_call_target="tpu_custom_call" | custom-call | flops 603979776 | bytes 1572864 | tf_op jit(solution)/shard_map/remote_part/pallas_call | solution.py:234
  27.2 2.1 %collective-permute-start.7 = (bf16[528,256]{1,0:T(8,128)(2,1)S(1)}, bf16[528,256]{1,0:T(8,128)(2,1)S(1)}, u32[]{:S(2)}, u32[]{:S(2)}) collective-permute-start(bf16[528,256]{1,0:T(8,128)(2,1)S(1)} %get-tuple-element.37), channel_id=1, source_target_pairs={{0,2},{2,0},{1,3},{3,1},{4,6},{6,4},{5,7},{7,5},{8,10},{10,8},{9,1... | collective-permute-start | bytes 811016 | tf_op jit(solution)/shard_map/ppermute | solution.py:358
  29.3 3.3 %local_part.1 = (f32[512,768]{1,0:T(8,128)S(1)}, f32[128,128]{1,0:T(8,128)S(1)}, f32[128,128]{1,0:T(8,128)S(1)}) custom-call(bf16[512,768]{1,0:T(8,128)(2,1)S(1)} %bitcast.18, bf16[512,768]{1,0:T(8,128)(2,1)S(1)} %bitcast.9, bf16[512,768]{1,0:T(8,128)(2,1)S(1)} %bitcast.15, bf16[512,384]{1,0:T(8,128)(2,1)S(1)} %collective-permute-done.1.even.rest_0_, ...), custom_call_target="tpu_custom_call" | custom-call | flops 1207959552 | bytes 3145728 | tf_op jit(solution)/shard_map/local_part/pallas_call | solution.py:247
  32.6 0.0 collective-permute-start.10
  32.7 2.0 %collective-permute-start.9 = (bf16[512,128]{1,0:T(8,128)(2,1)S(1)}, bf16[512,128]{1,0:T(8,128)(2,1)S(1)}, u32[]{:S(2)}, u32[]{:S(2)}) collective-permute-start(bf16[512,128]{1,0:T(8,128)(2,1)S(1)} %get-tuple-element.45), channel_id=1, source_target_pairs={{0,2},{2,3},{3,1},{1,0},{4,6},{6,7},{7,5},{5,4},{8,10},{10,11},{11... | collective-permute-start | bytes 393224 | tf_op jit(solution)/shard_map/ppermute | solution.py:386
  34.7 0.0 collective-permute-done.8.rest_1_
  34.7 1.3 %merge_part.2.rest_1_ = bf16[512,768]{1,0:T(8,128)(2,1)} custom-call(f32[512,768]{1,0:T(8,128)S(1)} %get-tuple-element.40.own, f32[128,128]{1,0:T(8,128)S(1)} %get-tuple-element.42.logs, bf16[512,128]{1,0:T(8,128)(2,1)S(1)} %collective-permute-done.4.rest_0_, bf16[528,256]{1,0:T(8,128)(2,1)S(1)} %collective-permute-done.8.rest_1_), custom_call_target="tpu_custom_call" | custom-call | flops 786432 | bytes 1572864 | tf_op jit(solution)/shard_map/merge_part/pallas_call | solution.py:275
  36.0 0.8 %collective-permute-done.7.rest_0_ = bf16[528,256]{1,0:T(8,128)(2,1)S(1)} collective-permute-done((bf16[528,256]{1,0:T(8,128)(2,1)S(1)}, bf16[528,256]{1,0:T(8,128)(2,1)S(1)}, u32[]{:S(2)}, u32[]{:S(2)}) %collective-permute-start.7) | collective-permute-done | bytes 270368 | tf_op jit(solution)/shard_map/ppermute | solution.py:358
  36.8 1.1 %merge_part.3 = (bf16[512,768]{1,0:T(8,128)(2,1)}, f32[512,128]{1,0:T(8,128)S(1)}, f32[512,128]{1,0:T(8,128)S(1)}) custom-call(f32[512,768]{1,0:T(8,128)S(1)} %get-tuple-element.40.own, f32[128,128]{1,0:T(8,128)S(1)} %get-tuple-element.41.logs, bf16[528,256]{1,0:T(8,128)(2,1)S(1)} %collective-permute-done.7.rest_0_, ...), custom_call_target="tpu_custom_call", output_to_operand_aliasing={{0}: (3, {})} | custom-call | flops 786432 | bytes 1572864 | tf_op jit(solution)/shard_map/merge_part/pallas_call | solution.py:275
  38.0 0.8 %collective-permute-done.10.rest_1_ = bf16[512,128]{1,0:T(8,128)(2,1)S(1)} collective-permute-done((bf16[512,128]{1,0:T(8,128)(2,1)S(1)}, bf16[512,128]{1,0:T(8,128)(2,1)S(1)}, u32[]{:S(2)}, u32[]{:S(2)}) %collective-permute-start.10) | collective-permute-done | bytes 131104 | tf_op jit(solution)/shard_map/ppermute | solution.py:386
  38.8 0.7 %finish_part.2.rest_2_ = bf16[512,768]{1,0:T(8,128)(2,1)} custom-call(f32[512,128]{1,0:T(8,128)S(1)} %get-tuple-element.43.scaled, f32[512,128]{1,0:T(8,128)S(1)} %get-tuple-element.44.rest_0_, bf16[512,128]{1,0:T(8,128)(2,1)S(1)} %collective-permute-done.10.rest_1_, bf16[512,768]{1,0:T(8,128)(2,1)} %get-tuple-element.46.rest_2_), custom_call_target="tpu_custom_call", output_to_operand_aliasing={{}: (3, {})} | custom-call | flops 262144 | bytes 524288 | tf_op jit(solution)/shard_map/finish_part/pallas_call | solution.py:291
  39.5 0.0 collective-permute-done.9.rest_1_
  39.5 0.1 finish_part.3
  (6 shorter events, 0.2 us)
Async XLA Ops:
  1.0 12.9 %collective-permute-start = (bf16[512,384]{1,0:T(8,128)(2,1)S(1)}, bf16[512,384]{1,0:T(8,128)(2,1)S(1)}, u32[]{:S(2)}, u32[]{:S(2)}) collective-permute-start(bf16[512,384]{1,0:T(8,128)(2,1)S(1)} %slice.8), channel_id=1, source_target_pairs={{0,2},{2,0},{1,3},{3,1},{4,6},{6,4},{5,7},{7,5},{8,10},{10,8},{9,1... | collective-permute-start | bytes 1179656 | tf_op jit(solution)/shard_map/ppermute | solution.py:344
  4.0 3.2 %copy-start.2 = (bf16[8,8,8,768]{3,2,1,0:T(8,128)(2,1)S(1)}, bf16[8,8,8,768]{3,2,1,0:T(8,128)(2,1)}, u32[]{:S(2)}) copy-start(bf16[8,8,8,768]{3,2,1,0:T(8,128)(2,1)} %param.3) | copy-start | bytes 2359300
  5.4 8.6 %copy-start.1 = (bf16[8,8,8,768]{3,2,1,0:T(8,128)(2,1)S(1)}, bf16[8,8,8,768]{3,2,1,0:T(8,128)(2,1)}, u32[]{:S(2)}) copy-start(bf16[8,8,8,768]{3,2,1,0:T(8,128)(2,1)} %param.5) | copy-start | bytes 2359300
  5.4 8.6 %copy-start = (bf16[8,8,8,768]{3,2,1,0:T(8,128)(2,1)S(1)}, bf16[8,8,8,768]{3,2,1,0:T(8,128)(2,1)}, u32[]{:S(2)}) copy-start(bf16[8,8,8,768]{3,2,1,0:T(8,128)(2,1)} %param.4) | copy-start | bytes 2359300
  5.5 11.4 %collective-permute-start.1 = (bf16[512,384]{1,0:T(8,128)(2,1)S(1)}, bf16[512,384]{1,0:T(8,128)(2,1)S(1)}, u32[]{:S(2)}, u32[]{:S(2)}) collective-permute-start(bf16[512,384]{1,0:T(8,128)(2,1)S(1)} %pad_maximum_fusion), channel_id=1, source_target_pairs={{0,4},{1,5},{4,0},{5,1},{8,12},{9,13},{12,8},{13,9},{2,6},{3,7},{6... | collective-permute-start | bytes 1179656 | tf_op jit(solution)/shard_map/ppermute | solution.py:353
  7.2 9.8 %collective-permute-start.2 = (bf16[512,384]{1,0:T(8,128)(2,1)S(1)}, bf16[512,384]{1,0:T(8,128)(2,1)S(1)}, u32[]{:S(2)}, u32[]{:S(2)}) collective-permute-start(bf16[512,384]{1,0:T(8,128)(2,1)S(1)} %pad_maximum_fusion.1), channel_id=1, source_target_pairs={{0,1},{1,0},{4,8},{5,9},{8,4},{9,5},{12,13},{13,12},{2,3},{3,2},{6... | collective-permute-start | bytes 1179656 | tf_op jit(solution)/shard_map/ppermute | solution.py:353
  7.3 17.9 %collective-permute-start.3 = (bf16[512,384]{1,0:T(8,128)(2,1)S(1)}, bf16[512,384]{1,0:T(8,128)(2,1)S(1)}, u32[]{:S(2)}, u32[]{:S(2)}) collective-permute-start(bf16[512,384]{1,0:T(8,128)(2,1)S(1)} %slice.7), channel_id=1, source_target_pairs={{0,2},{2,0},{1,3},{3,1},{4,6},{6,4},{5,7},{7,5},{8,10},{10,8},{9,1... | collective-permute-start | bytes 1179656 | tf_op jit(solution)/shard_map/ppermute | solution.py:344
  14.2 11.1 %collective-permute-start.5 = (bf16[512,384]{1,0:T(8,128)(2,1)S(1)}, bf16[512,384]{1,0:T(8,128)(2,1)S(1)}, u32[]{:S(2)}, u32[]{:S(2)}) collective-permute-start(bf16[512,384]{1,0:T(8,128)(2,1)S(1)} %pad_maximum_fusion.2), channel_id=1, source_target_pairs={{0,4},{1,5},{4,0},{5,1},{8,12},{9,13},{12,8},{13,9},{2,6},{3,7},{6... | collective-permute-start | bytes 1179656 | tf_op jit(solution)/shard_map/ppermute | solution.py:353
  16.4 8.8 %collective-permute-start.6 = (bf16[512,384]{1,0:T(8,128)(2,1)S(1)}, bf16[512,384]{1,0:T(8,128)(2,1)S(1)}, u32[]{:S(2)}, u32[]{:S(2)}) collective-permute-start(bf16[512,384]{1,0:T(8,128)(2,1)S(1)} %pad_maximum_fusion.3), channel_id=1, source_target_pairs={{0,1},{1,0},{4,8},{5,9},{8,4},{9,5},{12,13},{13,12},{2,3},{3,2},{6... | collective-permute-start | bytes 1179656 | tf_op jit(solution)/shard_map/ppermute | solution.py:353
  17.9 7.3 %collective-permute-start.4 = (bf16[512,128]{1,0:T(8,128)(2,1)S(1)}, bf16[512,128]{1,0:T(8,128)(2,1)S(1)}, u32[]{:S(2)}, u32[]{:S(2)}) collective-permute-start(bf16[512,128]{1,0:T(8,128)(2,1)S(1)} %get-tuple-element.28), channel_id=1, source_target_pairs={{0,2},{2,0},{1,3},{3,1},{4,6},{6,4},{5,7},{7,5},{8,10},{10,8},{9,1... | collective-permute-start | bytes 393224 | tf_op jit(solution)/shard_map/ppermute | solution.py:358
  20.5 14.1 %collective-permute-start.8 = (bf16[528,256]{1,0:T(8,128)(2,1)S(1)}, bf16[528,256]{1,0:T(8,128)(2,1)S(1)}, u32[]{:S(2)}, u32[]{:S(2)}) collective-permute-start(bf16[528,256]{1,0:T(8,128)(2,1)S(1)} %remote_part.2), channel_id=1, source_target_pairs={{0,2},{2,0},{1,3},{3,1},{4,6},{6,4},{5,7},{7,5},{8,10},{10,8},{9,1... | collective-permute-start | bytes 811016 | tf_op jit(solution)/shard_map/ppermute | solution.py:358
  27.2 9.6 %collective-permute-start.7 = (bf16[528,256]{1,0:T(8,128)(2,1)S(1)}, bf16[528,256]{1,0:T(8,128)(2,1)S(1)}, u32[]{:S(2)}, u32[]{:S(2)}) collective-permute-start(bf16[528,256]{1,0:T(8,128)(2,1)S(1)} %get-tuple-element.37), channel_id=1, source_target_pairs={{0,2},{2,0},{1,3},{3,1},{4,6},{6,4},{5,7},{7,5},{8,10},{10,8},{9,1... | collective-permute-start | bytes 811016 | tf_op jit(solution)/shard_map/ppermute | solution.py:358
  32.6 6.1 %collective-permute-start.10 = (bf16[512,128]{1,0:T(8,128)(2,1)S(1)}, bf16[512,128]{1,0:T(8,128)(2,1)S(1)}, u32[]{:S(2)}, u32[]{:S(2)}) collective-permute-start(bf16[512,128]{1,0:T(8,128)(2,1)S(1)} %get-tuple-element.45), channel_id=1, source_target_pairs={{2,0},{0,1},{1,3},{3,2},{6,4},{4,5},{5,7},{7,6},{10,8},{8,9},{9,11... | collective-permute-start | bytes 393224 | tf_op jit(solution)/shard_map/ppermute | solution.py:386
  32.7 6.8 %collective-permute-start.9 = (bf16[512,128]{1,0:T(8,128)(2,1)S(1)}, bf16[512,128]{1,0:T(8,128)(2,1)S(1)}, u32[]{:S(2)}, u32[]{:S(2)}) collective-permute-start(bf16[512,128]{1,0:T(8,128)(2,1)S(1)} %get-tuple-element.45), channel_id=1, source_target_pairs={{0,2},{2,3},{3,1},{1,0},{4,6},{6,7},{7,5},{5,4},{8,10},{10,11},{11... | collective-permute-start | bytes 393224 | tf_op jit(solution)/shard_map/ppermute | solution.py:386

commit v5 on v4

--- a/solution.py
+++ b/solution.py
@@ -22,7 +22,7 @@
 CHUNKS = (3, 3)
 LEADS = (1, 0)
 TAILS = (0, 1)
-CYCLES = (((2, 0), (0, 1), (1, 3), (3, 2)), ((0, 2), (2, 3), (3, 1), (1, 0)))
+CYCLES = (((0, 2), (2, 3), (3, 1), (1, 0)), ((2, 0), (0, 1), (1, 3), (3, 2)))
 VMEM_BYTES = 48 * 1024 * 1024
 
 
@@ -200,7 +200,7 @@
         finish()
     else:
         place = lax.axis_index("row") + lax.axis_index("head")
-        pl.when(lax.rem(place, 2) == turn)(finish)
+        pl.when(lax.rem(place, 2) != turn)(finish)
 
 
 def cost(heads, tiles=6):

time: 39.7 us -> 39.7 us (level)
  starting transfers between devices: 13.9 us -> 12.3 us
  waiting for transfers between devices: 11.9 us -> 13.3 us
    ppermute x3, waiting for transfers between devices: 4.52 us -> 6.04 us  [send_back(): return [lax.ppermute(x, 'row', p) for x, p in zip(parts, back)]]
    ppermute x2, starting transfers between devices: 2.03 us -> 0.52 us  [per_device(): came = [lax.ppermute(last[0], ('row', 'head'), cycle)]]
  transfers between devices with their start and end apart: 11 -> 11, of which waited for: 5 -> 6; matrix products, arithmetic and copies ran while one was open for 4% -> 4% of each run, Pallas kernels for 28% -> 26%
where the time goes in v5:
time: 39.7 us; the launch traced here: 39.5 us
  waiting for transfers between devices  13.3 us (34%)
  starting transfers between devices  12.3 us (31%)
  Pallas kernels  10.9 us (27%)
  local copies, waits for them, and re-layouts  2.55 us (6%)
    ppermute x2, waiting for transfers between devices, per_device(): got_q.append([lax.ppermute(sent, 'row', there) for there, _ in routes])  6.08 us
    ppermute x3, waiting for transfers between devices, send_back(): return [lax.ppermute(x, 'row', p) for x, p in zip(parts, back)]  6.04 us
    ppermute x3, starting transfers between devices, send_back(): return [lax.ppermute(x, 'row', p) for x, p in zip(parts, back)]  4.22 us
    ppermute x4, starting transfers between devices, per_device(): lax.ppermute(h, ('frame', 'head'), p)  3.99 us
    ppermute x2, starting transfers between devices, per_device(): got_q.append([lax.ppermute(sent, 'row', there) for there, _ in routes])  3.6 us
    pallas_call x2, Pallas kernels, remote_part(): pl.pallas_call(functools.partial(remote_kernel, first, heads, lead, tail)...  3.46 us
    pallas_call x1, Pallas kernels, local_part(): pl.pallas_call(functools.partial(local_kernel, splits), in_specs=[in_vmem...  3.33 us
    pallas_call x2, Pallas kernels, merge_part(): pl.pallas_call(functools.partial(merge_kernel, first, lead, heads, tail,...  2.44 us
  transfers between devices with their start and end apart: 11, of which 6 were waited for; matrix products, arithmetic and copies ran while one was open for 4% of the time, Pallas kernels for 26%

profile of v5, /device:TPU:0, one launch (start us, length us, event | category | flops | bytes accessed | tf_op | source)
XLA Modules:
  0.0 39.5 jit_solution(4357188664923369822)
XLA Ops:
  0.0 1.0 %slice.8 = bf16[512,384]{1,0:T(8,128)(2,1)S(1)} slice(bf16[512,768]{1,0:T(8,128)(2,1)} %bitcast.16), slice={[0:512], [0:384]} | slice | bytes 786432 | tf_op jit(solution)/shard_map/slice | solution.py:343
  1.0 3.0 %collective-permute-start = (bf16[512,384]{1,0:T(8,128)(2,1)S(1)}, bf16[512,384]{1,0:T(8,128)(2,1)S(1)}, u32[]{:S(2)}, u32[]{:S(2)}) collective-permute-start(bf16[512,384]{1,0:T(8,128)(2,1)S(1)} %slice.8), channel_id=1, source_target_pairs={{0,2},{2,0},{1,3},{3,1},{4,6},{6,4},{5,7},{7,5},{8,10},{10,8},{9,1... | collective-permute-start | bytes 1179656 | tf_op jit(solution)/shard_map/ppermute | solution.py:344
  4.0 0.0 copy-start.2
  4.0 1.4 %constant_dynamic-slice_fusion.4 = (bf16[256,384]{1,0:T(8,128)(2,1)S(1)}, bf16[256,384]{1,0:T(8,128)(2,1)S(1)}, bf16[256,384]{1,0:T(8,128)(2,1)S(1)}, bf16[256,384]{1,0:T(8,128)(2,1)S(1)}) fusion(bf16[512,768]{1,0:T(8,128)(2,1)} %bitcast.10, s32[]{:T(128)S(6)} %select_n.18, s32[]{:T(128)S(6)} %select_n.9, bf16[512,768]{1,0:T(8,128)(2,1)} %bitcast.4), kind=kLoop, calls=%fused_computation.8 | loop fusion | bytes 1572872 | tf_op jit(solution)/shard_map/dynamic_slice | solution.py:350
  5.4 0.0 copy-start.1
  5.4 0.0 copy-start
  5.5 1.6 %collective-permute-start.1 = (bf16[512,384]{1,0:T(8,128)(2,1)S(1)}, bf16[512,384]{1,0:T(8,128)(2,1)S(1)}, u32[]{:S(2)}, u32[]{:S(2)}) collective-permute-start(bf16[512,384]{1,0:T(8,128)(2,1)S(1)} %pad_maximum_fusion), channel_id=1, source_target_pairs={{0,4},{1,5},{4,0},{5,1},{8,12},{9,13},{12,8},{13,9},{2,6},{3,7},{6... | collective-permute-start | bytes 1179656 | tf_op jit(solution)/shard_map/ppermute | solution.py:353
  7.2 0.1 collective-permute-start.2
  7.2 0.0 copy-done.2
  7.3 0.6 %collective-permute-start.3 = (bf16[512,384]{1,0:T(8,128)(2,1)S(1)}, bf16[512,384]{1,0:T(8,128)(2,1)S(1)}, u32[]{:S(2)}, u32[]{:S(2)}) collective-permute-start(bf16[512,384]{1,0:T(8,128)(2,1)S(1)} %slice.7), channel_id=1, source_target_pairs={{0,2},{2,0},{1,3},{3,1},{4,6},{6,4},{5,7},{7,5},{8,10},{10,8},{9,1... | collective-permute-start | bytes 1179656 | tf_op jit(solution)/shard_map/ppermute | solution.py:344
  7.9 6.1 %collective-permute-done.q = bf16[512,384]{1,0:T(8,128)(2,1)S(1)} collective-permute-done((bf16[512,384]{1,0:T(8,128)(2,1)S(1)}, bf16[512,384]{1,0:T(8,128)(2,1)S(1)}, u32[]{:S(2)}, u32[]{:S(2)}) %collective-permute-start) | collective-permute-done | bytes 393248 | tf_op jit(solution)/shard_map/ppermute | solution.py:344
  14.0 0.0 copy-done.1
  14.0 0.0 copy-done
  14.0 0.1 constant_dynamic-slice_fusion.1
  14.2 2.2 %collective-permute-start.5 = (bf16[512,384]{1,0:T(8,128)(2,1)S(1)}, bf16[512,384]{1,0:T(8,128)(2,1)S(1)}, u32[]{:S(2)}, u32[]{:S(2)}) collective-permute-start(bf16[512,384]{1,0:T(8,128)(2,1)S(1)} %pad_maximum_fusion.2), channel_id=1, source_target_pairs={{0,4},{1,5},{4,0},{5,1},{8,12},{9,13},{12,8},{13,9},{2,6},{3,7},{6... | collective-permute-start | bytes 1179656 | tf_op jit(solution)/shard_map/ppermute | solution.py:353
  16.4 0.1 collective-permute-start.6
  16.5 0.4 %collective-permute-done.1.even.rest_0_ = bf16[512,384]{1,0:T(8,128)(2,1)S(1)} collective-permute-done((bf16[512,384]{1,0:T(8,128)(2,1)S(1)}, bf16[512,384]{1,0:T(8,128)(2,1)S(1)}, u32[]{:S(2)}, u32[]{:S(2)}) %collective-permute-start.1) | collective-permute-done | bytes 393248 | tf_op jit(solution)/shard_map/ppermute | solution.py:353
  16.9 0.0 collective-permute-done.2.odd.rest_1_
  16.9 1.0 %lead_part.1 = (bf16[512,128]{1,0:T(8,128)(2,1)S(1)}, f32[128,128]{1,0:T(8,128)S(1)}) custom-call(bf16[512,384]{1,0:T(8,128)(2,1)S(1)} %collective-permute-done.q, bf16[512,768]{1,0:T(8,128)(2,1)S(1)} %bitcast.6, bf16[512,768]{1,0:T(8,128)(2,1)S(1)} %bitcast.12, bf16[512,384]{1,0:T(8,128)(2,1)S(1)} %collective-permute-done.1.even.rest_0_, ...), custom_call_target="tpu_custom_call" | custom-call | flops 201326592 | bytes 524288 | tf_op jit(solution)/shard_map/lead_part/pallas_call | solution.py:218
  17.9 1.1 %collective-permute-start.4 = (bf16[512,128]{1,0:T(8,128)(2,1)S(1)}, bf16[512,128]{1,0:T(8,128)(2,1)S(1)}, u32[]{:S(2)}, u32[]{:S(2)}) collective-permute-start(bf16[512,128]{1,0:T(8,128)(2,1)S(1)} %get-tuple-element.28), channel_id=1, source_target_pairs={{0,2},{2,0},{1,3},{3,1},{4,6},{6,4},{5,7},{7,5},{8,10},{10,8},{9,1... | collective-permute-start | bytes 393224 | tf_op jit(solution)/shard_map/ppermute | solution.py:358
  19.0 1.5 %remote_part.2 = bf16[528,256]{1,0:T(8,128)(2,1)S(1)} custom-call(bf16[512,384]{1,0:T(8,128)(2,1)S(1)} %collective-permute-done.q, bf16[512,768]{1,0:T(8,128)(2,1)S(1)} %bitcast.7, bf16[512,768]{1,0:T(8,128)(2,1)S(1)} %bitcast.13, bf16[512,384]{1,0:T(8,128)(2,1)S(1)} %collective-permute-done.1.even.rest_0_, ...), custom_call_target="tpu_custom_call" | custom-call | flops 402653184 | bytes 1048576 | tf_op jit(solution)/shard_map/remote_part/pallas_call | solution.py:234
  20.5 1.0 %collective-permute-start.8 = (bf16[528,256]{1,0:T(8,128)(2,1)S(1)}, bf16[528,256]{1,0:T(8,128)(2,1)S(1)}, u32[]{:S(2)}, u32[]{:S(2)}) collective-permute-start(bf16[528,256]{1,0:T(8,128)(2,1)S(1)} %remote_part.2), channel_id=1, source_target_pairs={{0,2},{2,0},{1,3},{3,1},{4,6},{6,4},{5,7},{7,5},{8,10},{10,8},{9,1... | collective-permute-start | bytes 811016 | tf_op jit(solution)/shard_map/ppermute | solution.py:358
  21.5 3.7 %collective-permute-done.4.rest_0_ = bf16[512,128]{1,0:T(8,128)(2,1)S(1)} collective-permute-done((bf16[512,128]{1,0:T(8,128)(2,1)S(1)}, bf16[512,128]{1,0:T(8,128)(2,1)S(1)}, u32[]{:S(2)}, u32[]{:S(2)}) %collective-permute-start.4) | collective-permute-done | bytes 131104 | tf_op jit(solution)/shard_map/ppermute | solution.py:358
  25.2 0.0 collective-permute-done.3.q
  25.2 0.0 collective-permute-done.5.even.rest_2_
  25.2 0.0 collective-permute-done.6.odd.rest_3_
  25.2 2.0 %remote_part.3 = (bf16[528,256]{1,0:T(8,128)(2,1)S(1)}, bf16[512,128]{1,0:T(8,128)(2,1)S(1)}) custom-call(bf16[512,384]{1,0:T(8,128)(2,1)S(1)} %collective-permute-done.3.q, bf16[512,768]{1,0:T(8,128)(2,1)S(1)} %bitcast.8, bf16[512,768]{1,0:T(8,128)(2,1)S(1)} %bitcast.14, bf16[512,384]{1,0:T(8,128)(2,1)S(1)} %collective-permute-done.5.even.rest_2_, ...), custom_call_target="tpu_custom_call" | custom-call | flops 603979776 | bytes 1572864 | tf_op jit(solution)/shard_map/remote_part/pallas_call | solution.py:234
  27.2 2.1 %collective-permute-start.7 = (bf16[528,256]{1,0:T(8,128)(2,1)S(1)}, bf16[528,256]{1,0:T(8,128)(2,1)S(1)}, u32[]{:S(2)}, u32[]{:S(2)}) collective-permute-start(bf16[528,256]{1,0:T(8,128)(2,1)S(1)} %get-tuple-element.37), channel_id=1, source_target_pairs={{0,2},{2,0},{1,3},{3,1},{4,6},{6,4},{5,7},{7,5},{8,10},{10,8},{9,1... | collective-permute-start | bytes 811016 | tf_op jit(solution)/shard_map/ppermute | solution.py:358
  29.3 3.3 %local_part.1 = (f32[512,768]{1,0:T(8,128)S(1)}, f32[128,128]{1,0:T(8,128)S(1)}, f32[128,128]{1,0:T(8,128)S(1)}) custom-call(bf16[512,768]{1,0:T(8,128)(2,1)S(1)} %bitcast.18, bf16[512,768]{1,0:T(8,128)(2,1)S(1)} %bitcast.9, bf16[512,768]{1,0:T(8,128)(2,1)S(1)} %bitcast.15, bf16[512,384]{1,0:T(8,128)(2,1)S(1)} %collective-permute-done.1.even.rest_0_, ...), custom_call_target="tpu_custom_call" | custom-call | flops 1207959552 | bytes 3145728 | tf_op jit(solution)/shard_map/local_part/pallas_call | solution.py:247
  32.6 0.0 collective-permute-start.10
  32.7 0.5 %collective-permute-start.9 = (bf16[512,128]{1,0:T(8,128)(2,1)S(1)}, bf16[512,128]{1,0:T(8,128)(2,1)S(1)}, u32[]{:S(2)}, u32[]{:S(2)}) collective-permute-start(bf16[512,128]{1,0:T(8,128)(2,1)S(1)} %get-tuple-element.45), channel_id=1, source_target_pairs={{2,0},{0,1},{1,3},{3,2},{6,4},{4,5},{5,7},{7,6},{10,8},{8,9},{9,11... | collective-permute-start | bytes 393224 | tf_op jit(solution)/shard_map/ppermute | solution.py:386
  33.2 0.0 collective-permute-done.8.rest_1_
  33.2 1.3 %merge_part.2.rest_1_ = bf16[512,768]{1,0:T(8,128)(2,1)} custom-call(f32[512,768]{1,0:T(8,128)S(1)} %get-tuple-element.40.own, f32[128,128]{1,0:T(8,128)S(1)} %get-tuple-element.42.logs, bf16[512,128]{1,0:T(8,128)(2,1)S(1)} %collective-permute-done.4.rest_0_, bf16[528,256]{1,0:T(8,128)(2,1)S(1)} %collective-permute-done.8.rest_1_), custom_call_target="tpu_custom_call" | custom-call | flops 786432 | bytes 1572864 | tf_op jit(solution)/shard_map/merge_part/pallas_call | solution.py:275
  34.5 2.3 %collective-permute-done.7.rest_0_ = bf16[528,256]{1,0:T(8,128)(2,1)S(1)} collective-permute-done((bf16[528,256]{1,0:T(8,128)(2,1)S(1)}, bf16[528,256]{1,0:T(8,128)(2,1)S(1)}, u32[]{:S(2)}, u32[]{:S(2)}) %collective-permute-start.7) | collective-permute-done | bytes 270368 | tf_op jit(solution)/shard_map/ppermute | solution.py:358
  36.8 1.1 %merge_part.3 = (bf16[512,768]{1,0:T(8,128)(2,1)}, f32[512,128]{1,0:T(8,128)S(1)}, f32[512,128]{1,0:T(8,128)S(1)}) custom-call(f32[512,768]{1,0:T(8,128)S(1)} %get-tuple-element.40.own, f32[128,128]{1,0:T(8,128)S(1)} %get-tuple-element.41.logs, bf16[528,256]{1,0:T(8,128)(2,1)S(1)} %collective-permute-done.7.rest_0_, ...), custom_call_target="tpu_custom_call", output_to_operand_aliasing={{0}: (3, {})} | custom-call | flops 786432 | bytes 1572864 | tf_op jit(solution)/shard_map/merge_part/pallas_call | solution.py:275
  38.0 0.1 collective-permute-done.10.rest_1_
  38.1 0.7 %collective-permute-done.9.rest_1_ = bf16[512,128]{1,0:T(8,128)(2,1)S(1)} collective-permute-done((bf16[512,128]{1,0:T(8,128)(2,1)S(1)}, bf16[512,128]{1,0:T(8,128)(2,1)S(1)}, u32[]{:S(2)}, u32[]{:S(2)}) %collective-permute-start.9) | collective-permute-done | bytes 131104 | tf_op jit(solution)/shard_map/ppermute | solution.py:386
  38.8 0.7 %finish_part.3 = bf16[512,768]{1,0:T(8,128)(2,1)} custom-call(f32[512,128]{1,0:T(8,128)S(1)} %get-tuple-element.43.scaled, f32[512,128]{1,0:T(8,128)S(1)} %get-tuple-element.44.rest_0_, bf16[512,128]{1,0:T(8,128)(2,1)S(1)} %collective-permute-done.9.rest_1_, bf16[512,768]{1,0:T(8,128)(2,1)} %finish_part.2.rest_2_), custom_call_target="tpu_custom_call", output_to_operand_aliasing={{}: (3, {})} | custom-call | flops 262144 | bytes 524288 | tf_op jit(solution)/shard_map/finish_part/pallas_call | solution.py:291
  (7 shorter events, 0.3 us)
Async XLA Ops:
  1.0 12.9 %collective-permute-start = (bf16[512,384]{1,0:T(8,128)(2,1)S(1)}, bf16[512,384]{1,0:T(8,128)(2,1)S(1)}, u32[]{:S(2)}, u32[]{:S(2)}) collective-permute-start(bf16[512,384]{1,0:T(8,128)(2,1)S(1)} %slice.8), channel_id=1, source_target_pairs={{0,2},{2,0},{1,3},{3,1},{4,6},{6,4},{5,7},{7,5},{8,10},{10,8},{9,1... | collective-permute-start | bytes 1179656 | tf_op jit(solution)/shard_map/ppermute | solution.py:344
  4.0 3.2 %copy-start.2 = (bf16[8,8,8,768]{3,2,1,0:T(8,128)(2,1)S(1)}, bf16[8,8,8,768]{3,2,1,0:T(8,128)(2,1)}, u32[]{:S(2)}) copy-start(bf16[8,8,8,768]{3,2,1,0:T(8,128)(2,1)} %param.3) | copy-start | bytes 2359300
  5.4 8.6 %copy-start.1 = (bf16[8,8,8,768]{3,2,1,0:T(8,128)(2,1)S(1)}, bf16[8,8,8,768]{3,2,1,0:T(8,128)(2,1)}, u32[]{:S(2)}) copy-start(bf16[8,8,8,768]{3,2,1,0:T(8,128)(2,1)} %param.5) | copy-start | bytes 2359300
  5.4 8.6 %copy-start = (bf16[8,8,8,768]{3,2,1,0:T(8,128)(2,1)S(1)}, bf16[8,8,8,768]{3,2,1,0:T(8,128)(2,1)}, u32[]{:S(2)}) copy-start(bf16[8,8,8,768]{3,2,1,0:T(8,128)(2,1)} %param.4) | copy-start | bytes 2359300
  5.5 11.4 %collective-permute-start.1 = (bf16[512,384]{1,0:T(8,128)(2,1)S(1)}, bf16[512,384]{1,0:T(8,128)(2,1)S(1)}, u32[]{:S(2)}, u32[]{:S(2)}) collective-permute-start(bf16[512,384]{1,0:T(8,128)(2,1)S(1)} %pad_maximum_fusion), channel_id=1, source_target_pairs={{0,4},{1,5},{4,0},{5,1},{8,12},{9,13},{12,8},{13,9},{2,6},{3,7},{6... | collective-permute-start | bytes 1179656 | tf_op jit(solution)/shard_map/ppermute | solution.py:353
  7.2 9.8 %collective-permute-start.2 = (bf16[512,384]{1,0:T(8,128)(2,1)S(1)}, bf16[512,384]{1,0:T(8,128)(2,1)S(1)}, u32[]{:S(2)}, u32[]{:S(2)}) collective-permute-start(bf16[512,384]{1,0:T(8,128)(2,1)S(1)} %pad_maximum_fusion.1), channel_id=1, source_target_pairs={{0,1},{1,0},{4,8},{5,9},{8,4},{9,5},{12,13},{13,12},{2,3},{3,2},{6... | collective-permute-start | bytes 1179656 | tf_op jit(solution)/shard_map/ppermute | solution.py:353
  7.3 17.9 %collective-permute-start.3 = (bf16[512,384]{1,0:T(8,128)(2,1)S(1)}, bf16[512,384]{1,0:T(8,128)(2,1)S(1)}, u32[]{:S(2)}, u32[]{:S(2)}) collective-permute-start(bf16[512,384]{1,0:T(8,128)(2,1)S(1)} %slice.7), channel_id=1, source_target_pairs={{0,2},{2,0},{1,3},{3,1},{4,6},{6,4},{5,7},{7,5},{8,10},{10,8},{9,1... | collective-permute-start | bytes 1179656 | tf_op jit(solution)/shard_map/ppermute | solution.py:344
  14.2 11.1 %collective-permute-start.5 = (bf16[512,384]{1,0:T(8,128)(2,1)S(1)}, bf16[512,384]{1,0:T(8,128)(2,1)S(1)}, u32[]{:S(2)}, u32[]{:S(2)}) collective-permute-start(bf16[512,384]{1,0:T(8,128)(2,1)S(1)} %pad_maximum_fusion.2), channel_id=1, source_target_pairs={{0,4},{1,5},{4,0},{5,1},{8,12},{9,13},{12,8},{13,9},{2,6},{3,7},{6... | collective-permute-start | bytes 1179656 | tf_op jit(solution)/shard_map/ppermute | solution.py:353
  16.4 8.8 %collective-permute-start.6 = (bf16[512,384]{1,0:T(8,128)(2,1)S(1)}, bf16[512,384]{1,0:T(8,128)(2,1)S(1)}, u32[]{:S(2)}, u32[]{:S(2)}) collective-permute-start(bf16[512,384]{1,0:T(8,128)(2,1)S(1)} %pad_maximum_fusion.3), channel_id=1, source_target_pairs={{0,1},{1,0},{4,8},{5,9},{8,4},{9,5},{12,13},{13,12},{2,3},{3,2},{6... | collective-permute-start | bytes 1179656 | tf_op jit(solution)/shard_map/ppermute | solution.py:353
  17.9 7.3 %collective-permute-start.4 = (bf16[512,128]{1,0:T(8,128)(2,1)S(1)}, bf16[512,128]{1,0:T(8,128)(2,1)S(1)}, u32[]{:S(2)}, u32[]{:S(2)}) collective-permute-start(bf16[512,128]{1,0:T(8,128)(2,1)S(1)} %get-tuple-element.28), channel_id=1, source_target_pairs={{0,2},{2,0},{1,3},{3,1},{4,6},{6,4},{5,7},{7,5},{8,10},{10,8},{9,1... | collective-permute-start | bytes 393224 | tf_op jit(solution)/shard_map/ppermute | solution.py:358
  20.5 12.6 %collective-permute-start.8 = (bf16[528,256]{1,0:T(8,128)(2,1)S(1)}, bf16[528,256]{1,0:T(8,128)(2,1)S(1)}, u32[]{:S(2)}, u32[]{:S(2)}) collective-permute-start(bf16[528,256]{1,0:T(8,128)(2,1)S(1)} %remote_part.2), channel_id=1, source_target_pairs={{0,2},{2,0},{1,3},{3,1},{4,6},{6,4},{5,7},{7,5},{8,10},{10,8},{9,1... | collective-permute-start | bytes 811016 | tf_op jit(solution)/shard_map/ppermute | solution.py:358
  27.2 9.6 %collective-permute-start.7 = (bf16[528,256]{1,0:T(8,128)(2,1)S(1)}, bf16[528,256]{1,0:T(8,128)(2,1)S(1)}, u32[]{:S(2)}, u32[]{:S(2)}) collective-permute-start(bf16[528,256]{1,0:T(8,128)(2,1)S(1)} %get-tuple-element.37), channel_id=1, source_target_pairs={{0,2},{2,0},{1,3},{3,1},{4,6},{6,4},{5,7},{7,5},{8,10},{10,8},{9,1... | collective-permute-start | bytes 811016 | tf_op jit(solution)/shard_map/ppermute | solution.py:358
  32.6 5.4 %collective-permute-start.10 = (bf16[512,128]{1,0:T(8,128)(2,1)S(1)}, bf16[512,128]{1,0:T(8,128)(2,1)S(1)}, u32[]{:S(2)}, u32[]{:S(2)}) collective-permute-start(bf16[512,128]{1,0:T(8,128)(2,1)S(1)} %get-tuple-element.45), channel_id=1, source_target_pairs={{0,2},{2,3},{3,1},{1,0},{4,6},{6,7},{7,5},{5,4},{8,10},{10,11},{11... | collective-permute-start | bytes 393224 | tf_op jit(solution)/shard_map/ppermute | solution.py:386
  32.7 6.1 %collective-permute-start.9 = (bf16[512,128]{1,0:T(8,128)(2,1)S(1)}, bf16[512,128]{1,0:T(8,128)(2,1)S(1)}, u32[]{:S(2)}, u32[]{:S(2)}) collective-permute-start(bf16[512,128]{1,0:T(8,128)(2,1)S(1)} %get-tuple-element.45), channel_id=1, source_target_pairs={{2,0},{0,1},{1,3},{3,2},{6,4},{4,5},{5,7},{7,6},{10,8},{8,9},{9,11... | collective-permute-start | bytes 393224 | tf_op jit(solution)/shard_map/ppermute | solution.py:386

commit v6 on v5

--- a/solution.py
+++ b/solution.py
@@ -22,7 +22,8 @@
 CHUNKS = (3, 3)
 LEADS = (1, 0)
 TAILS = (0, 1)
-CYCLES = (((0, 2), (2, 3), (3, 1), (1, 0)), ((2, 0), (0, 1), (1, 3), (3, 2)))
+ONE_ALONG_X = tuple((i, i ^ 2 if i % 2 else i ^ 4) for i in range(8))
+ZERO_ALONG_X = tuple((i, i ^ 2) for i in range(0, 8, 2))
 VMEM_BYTES = 48 * 1024 * 1024
 
 
@@ -79,14 +80,25 @@
     return jnp.concatenate([flat, jnp.zeros((HD - LOG_ROWS, HD), jnp.float32)], 0).T
 
 
-def lead_kernel(first, heads, q, k, v, even, odd, out, logs):
+def came(q, first, skip, heads):
+    chunk = q[0][:, skip * HD : (skip + heads) * HD]
+    if len(q) == 1:
+        return chunk
+    whole = q[1][:, first * HD : (first + heads) * HD]
+    return jnp.where(lax.axis_index("head") == 1, whole, chunk)
+
+
+def lead_kernel(first, heads, count, *refs):
+    q, (k, v, even, odd, out, logs) = refs[:count], refs[count:]
+
     def store(rows, here, block):
         out[rows, here] = block.astype(out.dtype)
 
-    logs[...] = attend(first, heads, q, k, v, even, odd, store)
-
-
-def remote_kernel(first, heads, lead, tail, q, k, v, even, odd, *rest):
+    logs[...] = attend(first, heads, came(q, first, 0, heads), k, v, even, odd, store)
+
+
+def remote_kernel(first, heads, lead, tail, count, *refs):
+    q, (k, v, even, odd, *rest) = refs[:count], refs[count:]
     earlier, (out, *last) = rest[: lead > 0], rest[lead > 0 :]
 
     def store(rows, here, block):
@@ -96,7 +108,7 @@
         else:
             last[0][rows, start : start + HD] = block.astype(out.dtype)
 
-    q_here = q.at[:, lead * HD : (lead + heads) * HD]
+    q_here = came(q, first, lead, heads)
     sides = [x.at[:, lead * HD : (lead + heads) * HD] for x in (even, odd)]
     logs = attend(first, heads, q_here, k, v, *sides, store, lead)
     packed = pack_logs(logs + earlier[0][...] if lead else logs)
@@ -182,7 +194,7 @@
         copy.wait()
 
 
-def finish_kernel(first, heads, groups, turn, scaled, *rest):
+def finish_kernel(first, heads, groups, scaled, *rest):
     shares, theirs = rest[:groups], rest[groups : 2 * groups]
     out, mixed, done = rest[-3:]
 
@@ -192,15 +204,8 @@
             summed = summed + share[rows, :] * part[rows, :].astype(jnp.float32)
         mixed[rows, :] = summed.astype(mixed.dtype)
 
-    def finish():
-        for copy in write_columns(first, heads, mixed, out, done, fill):
-            copy.wait()
-
-    if turn is None:
-        finish()
-    else:
-        place = lax.axis_index("row") + lax.axis_index("head")
-        pl.when(lax.rem(place, 2) != turn)(finish)
+    for copy in write_columns(first, heads, mixed, out, done, fill):
+        copy.wait()
 
 
 def cost(heads, tiles=6):
@@ -216,8 +221,8 @@
 
 def lead_part(first, heads, q, k, v, even, odd):
     return pl.pallas_call(
-        functools.partial(lead_kernel, first, heads),
-        in_specs=[in_vmem()] * 5,
+        functools.partial(lead_kernel, first, heads, len(q)),
+        in_specs=[in_vmem()] * (4 + len(q)),
         out_specs=[in_vmem()] * 2,
         out_shape=[
             jax.ShapeDtypeStruct((ROWS, heads * HD), jnp.bfloat16),
@@ -226,20 +231,20 @@
         compiler_params=pltpu.CompilerParams(vmem_limit_bytes=VMEM_BYTES),
         cost_estimate=cost(heads),
         name="lead_part",
-    )(q, k, v, even, odd)
+    )(*q, k, v, even, odd)
 
 
 def remote_part(first, heads, lead, tail, q, k, v, even, odd, *earlier):
     shapes = [(ROWS + LOG_ROWS, (heads - tail) * HD)] + [(ROWS, tail * HD)] * (tail > 0)
     return pl.pallas_call(
-        functools.partial(remote_kernel, first, heads, lead, tail),
-        in_specs=[in_vmem()] * (5 + len(earlier)),
+        functools.partial(remote_kernel, first, heads, lead, tail, len(q)),
+        in_specs=[in_vmem()] * (4 + len(q) + len(earlier)),
         out_specs=[in_vmem()] * len(shapes),
         out_shape=[jax.ShapeDtypeStruct(shape, jnp.bfloat16) for shape in shapes],
         compiler_params=pltpu.CompilerParams(vmem_limit_bytes=VMEM_BYTES),
         cost_estimate=cost(heads),
         name="remote_part",
-    )(q, k, v, even, odd, *earlier)
+    )(*q, k, v, even, odd, *earlier)
 
 
 def local_part(splits, q, k, v, sides):
@@ -286,10 +291,10 @@
     return out, later
 
 
-def finish_part(first, heads, scaled, shares, theirs, out, turn=None):
+def finish_part(first, heads, scaled, shares, theirs, out):
     groups = len(theirs)
     return pl.pallas_call(
-        functools.partial(finish_kernel, first, heads, groups, turn),
+        functools.partial(finish_kernel, first, heads, groups),
         in_specs=[in_vmem()] * (1 + 2 * groups) + [pl.BlockSpec(memory_space=pl.ANY)],
         out_specs=pl.BlockSpec(memory_space=pl.ANY),
         out_shape=jax.ShapeDtypeStruct(out.shape, out.dtype),
@@ -336,21 +341,36 @@
         bounds.append((start, start + count))
         start += count
 
+    axes = ("clips", "row", "head")
+    by_core = [lax.axis_size(axis) for axis in axes] == [2, 2, 2]
+    if by_core:
+        whole = lax.ppermute(q, axes, ONE_ALONG_X)
     got_q, sides = [], []
     q_now, gate = q, ()
     for a, b in bounds:
         a, b = a * HD, b * HD
-        sent = q_now[:, a:b]
-        got_q.append([lax.ppermute(sent, "row", there) for there, _ in routes])
-        k_now, v_now, _ = lax.optimization_barrier((k, v, (sent, gate)))
-        gate = got_q[-1]
+        if not by_core:
+            sent = q_now[:, a:b]
+            got_q.append([(lax.ppermute(sent, "row", there),) for there, _ in routes])
+            gate = (gate, sent)
+        k_now, v_now, _ = lax.optimization_barrier((k, v, gate))
         halves = []
         for first in (0, 1):
+            if first and by_core and sides:
+                k_now, v_now, _ = lax.optimization_barrier((k, v, (halves, sides[0][0])))
             row = jnp.where(lax.rem(place, 2) == first, TILE, 0)
             half = [lax.dynamic_slice(x, (row, a), (TILE, b - a)) for x in (k_now, v_now)]
             halves.append(jnp.concatenate(half, 0))
+        sides.append([lax.ppermute(h, ("frame", "head"), p) for h, p in zip(halves, pairs)])
         q_now, _ = lax.optimization_barrier((q, halves))
-        sides.append([lax.ppermute(h, ("frame", "head"), p) for h, p in zip(halves, pairs)])
+        if not by_core:
+            gate = [one[0] for one in got_q[-1]]
+        elif not got_q:
+            for c, d in bounds:
+                sent = q_now[:, c * HD : d * HD]
+                got_q.append([(lax.ppermute(sent, axes, ZERO_ALONG_X), whole)])
+                q_now, _ = lax.optimization_barrier((q, sent))
+            gate = (whole, sent)
 
     back = [route for _, route in routes]
 
@@ -381,12 +401,7 @@
         out, later = merge_part(a, lead, b - a - tail, tail, own, log, leads, theirs, out)
         if tail:
             last, _ = lax.optimization_barrier((parts[1], log))
-            if rows == 2 and lax.axis_size("head") == 2:
-                for turn, cycle in enumerate(CYCLES):
-                    came = [lax.ppermute(last[0], ("row", "head"), cycle)]
-                    out = finish_part(b - tail, tail, later[0], later[1:], came, out, turn)
-            else:
-                out = finish_part(b - tail, tail, later[0], later[1:], send_back(last), out)
+            out = finish_part(b - tail, tail, later[0], later[1:], send_back(last), out)
         out = (out,)
     (out,) = out
     return out.reshape(query.shape)

time: 39.7 us -> 39.4 us (level)
  starting transfers between devices: 12.3 us -> 18 us
  waiting for transfers between devices: 13.3 us -> 8.37 us
  local copies, waits for them, and re-layouts: 2.55 us -> 1.56 us
    ppermute x4 -> x3, waiting for transfers between devices: 6.86 us -> 1.01 us  [the longest x1 1 us: per_device(): whole = lax.ppermute(q, axes, ONE_ALONG_X)]
    ppermute x4 -> x3, starting transfers between devices: 4.13 us -> 8.81 us  [the longest x2 5.84 us: per_device(): got_q.append([(lax.ppermute(sent, axes, ZERO_ALONG_X), whole)])]
    ppermute x4, waiting for transfers between devices: 0.45 us -> 2.71 us  [per_device(): lax.ppermute(h, ('frame', 'head'), p)]
    ppermute x3 -> x4, waiting for transfers between devices: 6.04 us -> 4.65 us  [send_back(): return [lax.ppermute(x, 'row', p) for x, p in zip(parts, back)]]
    slice x2, local copies, waits for them, and re-layouts: 1.08 us -> 0.08 us  [per_device(): sent = q_now[:, c * HD:d * HD]]
    ppermute x4, starting transfers between devices: 3.99 us -> 4.92 us  [per_device(): lax.ppermute(h, ('frame', 'head'), p)]
    ppermute x3 -> x4, starting transfers between devices: 4.22 us -> 4.26 us  [send_back(): return [lax.ppermute(x, 'row', p) for x, p in zip(parts, back)]]
    dynamic_slice x3 -> x5, local copies, waits for them, and re-layouts: 1.45 us -> 1.46 us  [per_device(): lax.dynamic_slice(x, (row, a), (TILE, b - a))]
where the time goes in v6:
time: 39.4 us; the launch traced here: 39.2 us
  starting transfers between devices  18 us (46%)
  Pallas kernels  10.9 us (28%)
  waiting for transfers between devices  8.37 us (21%)
  local copies, waits for them, and re-layouts  1.56 us (4%)
    ppermute x2, starting transfers between devices, per_device(): got_q.append([(lax.ppermute(sent, axes, ZERO_ALONG_X), whole)])  5.84 us
    ppermute x4, starting transfers between devices, per_device(): lax.ppermute(h, ('frame', 'head'), p)  4.92 us
    ppermute x4, waiting for transfers between devices, send_back(): return [lax.ppermute(x, 'row', p) for x, p in zip(parts, back)]  4.65 us
    ppermute x4, starting transfers between devices, send_back(): return [lax.ppermute(x, 'row', p) for x, p in zip(parts, back)]  4.26 us
    pallas_call x2, Pallas kernels, remote_part(): pl.pallas_call(functools.partial(remote_kernel, first, heads, lead, tail,...  3.5 us
    pallas_call x1, Pallas kernels, local_part(): pl.pallas_call(functools.partial(local_kernel, splits), in_specs=[in_vmem...  3.33 us
    ppermute x1, starting transfers between devices, per_device(): whole = lax.ppermute(q, axes, ONE_ALONG_X)  2.97 us
    ppermute x4, waiting for transfers between devices, per_device(): lax.ppermute(h, ('frame', 'head'), p)  2.71 us
  transfers between devices with their start and end apart: 11, of which 6 were waited for; matrix products, arithmetic and copies ran while one was open for 4% of the time, Pallas kernels for 26%

profile of v6, /device:TPU:0, one launch (start us, length us, event | category | flops | bytes accessed | tf_op | source)
XLA Modules:
  0.0 39.2 jit_solution(16693842444477622434)
XLA Ops:
  0.0 3.0 %collective-permute-start.1 = (bf16[512,768]{1,0:T(8,128)(2,1)}, bf16[512,768]{1,0:T(8,128)(2,1)S(1)}, u32[]{:S(2)}, u32[]{:S(2)}) collective-permute-start(bf16[512,768]{1,0:T(8,128)(2,1)} %bitcast.18), channel_id=1, source_target_pairs={{0,16},{1,3},{2,18},{3,1},{16,0},{17,19},{18,2},{19,17},{4,20},{5,... | collective-permute-start | bytes 2359304 | tf_op jit(solution)/shard_map/ppermute | solution.py:347
  3.0 0.0 copy-start.2
  3.0 1.4 %constant_dynamic-slice_fusion.4 = (bf16[256,384]{1,0:T(8,128)(2,1)S(1)}, bf16[256,384]{1,0:T(8,128)(2,1)S(1)}, bf16[256,384]{1,0:T(8,128)(2,1)S(1)}, bf16[256,384]{1,0:T(8,128)(2,1)S(1)}) fusion(bf16[512,768]{1,0:T(8,128)(2,1)} %bitcast.11, s32[]{:T(128)S(6)} %select_n.18, s32[]{:T(128)S(6)} %select_n.9, bf16[512,768]{1,0:T(8,128)(2,1)} %bitcast.4), kind=kLoop, calls=%fused_computation.8 | loop fusion | bytes 1572872 | tf_op jit(solution)/shard_map/dynamic_slice | solution.py:362
  4.3 0.0 copy-start
  4.4 0.0 copy-start.1
  4.4 1.6 %collective-permute-start.2 = (bf16[512,384]{1,0:T(8,128)(2,1)S(1)}, bf16[512,384]{1,0:T(8,128)(2,1)S(1)}, u32[]{:S(2)}, u32[]{:S(2)}) collective-permute-start(bf16[512,384]{1,0:T(8,128)(2,1)S(1)} %pad_maximum_fusion), channel_id=1, source_target_pairs={{0,4},{1,5},{4,0},{5,1},{8,12},{9,13},{12,8},{13,9},{2,6},{3,7},{6... | collective-permute-start | bytes 1179656 | tf_op jit(solution)/shard_map/ppermute | solution.py:364
  6.1 0.1 collective-permute-start.3
  6.2 0.0 copy-done.2
  6.2 3.4 %collective-permute-start = (bf16[512,384]{1,0:T(8,128)(2,1)S(1)}, bf16[512,384]{1,0:T(8,128)(2,1)S(1)}, u32[]{:S(2)}, u32[]{:S(2)}) collective-permute-start(bf16[512,384]{1,0:T(8,128)(2,1)S(1)} %slice.6), channel_id=1, source_target_pairs={{0,2},{2,0},{16,18},{18,16},{4,6},{6,4},{20,22},{22,20},{8,10},{10... | collective-permute-start | bytes 1179656 | tf_op jit(solution)/shard_map/ppermute | solution.py:371
  9.7 2.4 %collective-permute-start.4 = (bf16[512,384]{1,0:T(8,128)(2,1)S(1)}, bf16[512,384]{1,0:T(8,128)(2,1)S(1)}, u32[]{:S(2)}, u32[]{:S(2)}) collective-permute-start(bf16[512,384]{1,0:T(8,128)(2,1)S(1)} %slice.7), channel_id=1, source_target_pairs={{0,2},{2,0},{16,18},{18,16},{4,6},{6,4},{20,22},{22,20},{8,10},{10... | collective-permute-start | bytes 1179656 | tf_op jit(solution)/shard_map/ppermute | solution.py:371
  12.1 1.0 %collective-permute-done.1.refs_1_ = bf16[512,768]{1,0:T(8,128)(2,1)S(1)} collective-permute-done((bf16[512,768]{1,0:T(8,128)(2,1)}, bf16[512,768]{1,0:T(8,128)(2,1)S(1)}, u32[]{:S(2)}, u32[]{:S(2)}) %collective-permute-start.1) | collective-permute-done | bytes 786464 | tf_op jit(solution)/shard_map/ppermute | solution.py:347
  13.1 0.0 copy-done
  13.2 0.0 copy-done.1
  13.3 1.8 %collective-permute-done.2.refs_4_.rest_0_ = bf16[512,384]{1,0:T(8,128)(2,1)S(1)} collective-permute-done((bf16[512,384]{1,0:T(8,128)(2,1)S(1)}, bf16[512,384]{1,0:T(8,128)(2,1)S(1)}, u32[]{:S(2)}, u32[]{:S(2)}) %collective-permute-start.2) | collective-permute-done | bytes 393248 | tf_op jit(solution)/shard_map/ppermute | solution.py:364
  15.1 0.1 collective-permute-start.7
  15.2 3.1 %collective-permute-start.6 = (bf16[512,384]{1,0:T(8,128)(2,1)S(1)}, bf16[512,384]{1,0:T(8,128)(2,1)S(1)}, u32[]{:S(2)}, u32[]{:S(2)}) collective-permute-start(bf16[512,384]{1,0:T(8,128)(2,1)S(1)} %pad_maximum_fusion.2), channel_id=1, source_target_pairs={{0,4},{1,5},{4,0},{5,1},{8,12},{9,13},{12,8},{13,9},{2,6},{3,7},{6... | collective-permute-start | bytes 1179656 | tf_op jit(solution)/shard_map/ppermute | solution.py:364
  18.4 0.0 collective-permute-done.refs_0_
  18.4 0.0 collective-permute-done.3.refs_5_.rest_1_
  18.4 1.0 %lead_part.1 = (bf16[512,128]{1,0:T(8,128)(2,1)S(1)}, f32[128,128]{1,0:T(8,128)S(1)}) custom-call(bf16[512,384]{1,0:T(8,128)(2,1)S(1)} %collective-permute-done.refs_0_, bf16[512,768]{1,0:T(8,128)(2,1)S(1)} %collective-permute-done.1.refs_1_, bf16[512,768]{1,0:T(8,128)(2,1)S(1)} %bitcast.7, bf16[512,768]{1,0:T(8,128)(2,1)S(1)} %bitcast.14, ...), custom_call_target="tpu_custom_call" | custom-call | flops 201326592 | bytes 524288 | tf_op jit(solution)/shard_map/lead_part/pallas_call | solution.py:223
  19.3 0.6 %collective-permute-start.5 = (bf16[512,128]{1,0:T(8,128)(2,1)S(1)}, bf16[512,128]{1,0:T(8,128)(2,1)S(1)}, u32[]{:S(2)}, u32[]{:S(2)}) collective-permute-start(bf16[512,128]{1,0:T(8,128)(2,1)S(1)} %get-tuple-element.32), channel_id=1, source_target_pairs={{0,2},{2,0},{1,3},{3,1},{4,6},{6,4},{5,7},{7,5},{8,10},{10,8},{9,1... | collective-permute-start | bytes 393224 | tf_op jit(solution)/shard_map/ppermute | solution.py:378
  19.9 1.5 %remote_part.2 = bf16[528,256]{1,0:T(8,128)(2,1)S(1)} custom-call(bf16[512,384]{1,0:T(8,128)(2,1)S(1)} %collective-permute-done.refs_0_, bf16[512,768]{1,0:T(8,128)(2,1)S(1)} %collective-permute-done.1.refs_1_, bf16[512,768]{1,0:T(8,128)(2,1)S(1)} %bitcast.8, bf16[512,768]{1,0:T(8,128)(2,1)S(1)} %bitcast.15, ...), custom_call_target="tpu_custom_call" | custom-call | flops 402653184 | bytes 1048576 | tf_op jit(solution)/shard_map/remote_part/pallas_call | solution.py:239
  21.4 1.5 %collective-permute-start.9 = (bf16[528,256]{1,0:T(8,128)(2,1)S(1)}, bf16[528,256]{1,0:T(8,128)(2,1)S(1)}, u32[]{:S(2)}, u32[]{:S(2)}) collective-permute-start(bf16[528,256]{1,0:T(8,128)(2,1)S(1)} %remote_part.2), channel_id=1, source_target_pairs={{0,2},{2,0},{1,3},{3,1},{4,6},{6,4},{5,7},{7,5},{8,10},{10,8},{9,1... | collective-permute-start | bytes 811016 | tf_op jit(solution)/shard_map/ppermute | solution.py:378
  23.0 2.8 %collective-permute-done.5.rest_0_ = bf16[512,128]{1,0:T(8,128)(2,1)S(1)} collective-permute-done((bf16[512,128]{1,0:T(8,128)(2,1)S(1)}, bf16[512,128]{1,0:T(8,128)(2,1)S(1)}, u32[]{:S(2)}, u32[]{:S(2)}) %collective-permute-start.5) | collective-permute-done | bytes 131104 | tf_op jit(solution)/shard_map/ppermute | solution.py:378
  25.8 0.0 collective-permute-done.4.refs_0_
  25.8 0.0 collective-permute-done.7.refs_5_.rest_3_
  25.8 1.0 %collective-permute-done.6.refs_4_.rest_2_ = bf16[512,384]{1,0:T(8,128)(2,1)S(1)} collective-permute-done((bf16[512,384]{1,0:T(8,128)(2,1)S(1)}, bf16[512,384]{1,0:T(8,128)(2,1)S(1)}, u32[]{:S(2)}, u32[]{:S(2)}) %collective-permute-start.6) | collective-permute-done | bytes 393248 | tf_op jit(solution)/shard_map/ppermute | solution.py:364
  26.7 2.0 %remote_part.3 = (bf16[528,256]{1,0:T(8,128)(2,1)S(1)}, bf16[512,128]{1,0:T(8,128)(2,1)S(1)}) custom-call(bf16[512,384]{1,0:T(8,128)(2,1)S(1)} %collective-permute-done.4.refs_0_, bf16[512,768]{1,0:T(8,128)(2,1)S(1)} %collective-permute-done.1.refs_1_, bf16[512,768]{1,0:T(8,128)(2,1)S(1)} %bitcast.9, bf16[512,768]{1,0:T(8,128)(2,1)S(1)} %bitcast.16, ...), custom_call_target="tpu_custom_call" | custom-call | flops 603979776 | bytes 1572864 | tf_op jit(solution)/shard_map/remote_part/pallas_call | solution.py:239
  28.7 0.6 %collective-permute-start.8 = (bf16[528,256]{1,0:T(8,128)(2,1)S(1)}, bf16[528,256]{1,0:T(8,128)(2,1)S(1)}, u32[]{:S(2)}, u32[]{:S(2)}) collective-permute-start(bf16[528,256]{1,0:T(8,128)(2,1)S(1)} %get-tuple-element.43), channel_id=1, source_target_pairs={{0,2},{2,0},{1,3},{3,1},{4,6},{6,4},{5,7},{7,5},{8,10},{10,8},{9,1... | collective-permute-start | bytes 811016 | tf_op jit(solution)/shard_map/ppermute | solution.py:378
  29.4 3.3 %local_part.1 = (f32[512,768]{1,0:T(8,128)S(1)}, f32[128,128]{1,0:T(8,128)S(1)}, f32[128,128]{1,0:T(8,128)S(1)}) custom-call(bf16[512,768]{1,0:T(8,128)(2,1)S(1)} %bitcast.21, bf16[512,768]{1,0:T(8,128)(2,1)S(1)} %bitcast.10, bf16[512,768]{1,0:T(8,128)(2,1)S(1)} %bitcast.17, bf16[512,384]{1,0:T(8,128)(2,1)S(1)} %collective-permute-done.2.refs_4_.rest_0_, ...), custom_call_target="tpu_custom_call" | custom-call | flops 1207959552 | bytes 3145728 | tf_op jit(solution)/shard_map/local_part/pallas_call | solution.py:252
  32.7 1.5 %collective-permute-start.10 = (bf16[512,128]{1,0:T(8,128)(2,1)S(1)}, bf16[512,128]{1,0:T(8,128)(2,1)S(1)}, u32[]{:S(2)}, u32[]{:S(2)}) collective-permute-start(bf16[512,128]{1,0:T(8,128)(2,1)S(1)} %get-tuple-element.51), channel_id=1, source_target_pairs={{0,2},{2,0},{1,3},{3,1},{4,6},{6,4},{5,7},{7,5},{8,10},{10,8},{9,1... | collective-permute-start | bytes 393224 | tf_op jit(solution)/shard_map/ppermute | solution.py:378
  34.2 0.0 collective-permute-done.9.rest_1_
  34.2 1.3 %merge_part.2.rest_1_ = bf16[512,768]{1,0:T(8,128)(2,1)} custom-call(f32[512,768]{1,0:T(8,128)S(1)} %get-tuple-element.46.own, f32[128,128]{1,0:T(8,128)S(1)} %get-tuple-element.48.logs, bf16[512,128]{1,0:T(8,128)(2,1)S(1)} %collective-permute-done.5.rest_0_, bf16[528,256]{1,0:T(8,128)(2,1)S(1)} %collective-permute-done.9.rest_1_), custom_call_target="tpu_custom_call" | custom-call | flops 786432 | bytes 1572864 | tf_op jit(solution)/shard_map/merge_part/pallas_call | solution.py:280
  35.5 1.6 %collective-permute-done.8.rest_0_ = bf16[528,256]{1,0:T(8,128)(2,1)S(1)} collective-permute-done((bf16[528,256]{1,0:T(8,128)(2,1)S(1)}, bf16[528,256]{1,0:T(8,128)(2,1)S(1)}, u32[]{:S(2)}, u32[]{:S(2)}) %collective-permute-start.8) | collective-permute-done | bytes 270368 | tf_op jit(solution)/shard_map/ppermute | solution.py:378
  37.1 1.1 %merge_part.3 = (bf16[512,768]{1,0:T(8,128)(2,1)}, f32[512,128]{1,0:T(8,128)S(1)}, f32[512,128]{1,0:T(8,128)S(1)}) custom-call(f32[512,768]{1,0:T(8,128)S(1)} %get-tuple-element.46.own, f32[128,128]{1,0:T(8,128)S(1)} %get-tuple-element.47.logs, bf16[528,256]{1,0:T(8,128)(2,1)S(1)} %collective-permute-done.8.rest_0_, ...), custom_call_target="tpu_custom_call", output_to_operand_aliasing={{0}: (3, {})} | custom-call | flops 786432 | bytes 1572864 | tf_op jit(solution)/shard_map/merge_part/pallas_call | solution.py:280
  38.3 0.2 collective-permute-done.10.rest_1_
  38.5 0.7 %finish_part.1 = bf16[512,768]{1,0:T(8,128)(2,1)} custom-call(f32[512,128]{1,0:T(8,128)S(1)} %get-tuple-element.49.scaled, f32[512,128]{1,0:T(8,128)S(1)} %get-tuple-element.50.rest_0_, bf16[512,128]{1,0:T(8,128)(2,1)S(1)} %collective-permute-done.10.rest_1_, bf16[512,768]{1,0:T(8,128)(2,1)} %get-tuple-element.52.rest_2_), custom_call_target="tpu_custom_call", output_to_operand_aliasing={{}: (3, {})} | custom-call | flops 262144 | bytes 524288 | tf_op jit(solution)/shard_map/finish_part/pallas_call | solution.py:296
  (10 shorter events, 0.3 us)
Async XLA Ops:
  0.0 13.1 %collective-permute-start.1 = (bf16[512,768]{1,0:T(8,128)(2,1)}, bf16[512,768]{1,0:T(8,128)(2,1)S(1)}, u32[]{:S(2)}, u32[]{:S(2)}) collective-permute-start(bf16[512,768]{1,0:T(8,128)(2,1)} %bitcast.18), channel_id=1, source_target_pairs={{0,16},{1,3},{2,18},{3,1},{16,0},{17,19},{18,2},{19,17},{4,20},{5,... | collective-permute-start | bytes 2359304 | tf_op jit(solution)/shard_map/ppermute | solution.py:347
  3.0 3.2 %copy-start.2 = (bf16[8,8,8,768]{3,2,1,0:T(8,128)(2,1)S(1)}, bf16[8,8,8,768]{3,2,1,0:T(8,128)(2,1)}, u32[]{:S(2)}) copy-start(bf16[8,8,8,768]{3,2,1,0:T(8,128)(2,1)} %param.3) | copy-start | bytes 2359300
  4.3 8.8 %copy-start = (bf16[8,8,8,768]{3,2,1,0:T(8,128)(2,1)S(1)}, bf16[8,8,8,768]{3,2,1,0:T(8,128)(2,1)}, u32[]{:S(2)}) copy-start(bf16[8,8,8,768]{3,2,1,0:T(8,128)(2,1)} %param.4) | copy-start | bytes 2359300
  4.4 8.8 %copy-start.1 = (bf16[8,8,8,768]{3,2,1,0:T(8,128)(2,1)S(1)}, bf16[8,8,8,768]{3,2,1,0:T(8,128)(2,1)}, u32[]{:S(2)}) copy-start(bf16[8,8,8,768]{3,2,1,0:T(8,128)(2,1)} %param.5) | copy-start | bytes 2359300
  4.4 10.6 %collective-permute-start.2 = (bf16[512,384]{1,0:T(8,128)(2,1)S(1)}, bf16[512,384]{1,0:T(8,128)(2,1)S(1)}, u32[]{:S(2)}, u32[]{:S(2)}) collective-permute-start(bf16[512,384]{1,0:T(8,128)(2,1)S(1)} %pad_maximum_fusion), channel_id=1, source_target_pairs={{0,4},{1,5},{4,0},{5,1},{8,12},{9,13},{12,8},{13,9},{2,6},{3,7},{6... | collective-permute-start | bytes 1179656 | tf_op jit(solution)/shard_map/ppermute | solution.py:364
  6.1 12.3 %collective-permute-start.3 = (bf16[512,384]{1,0:T(8,128)(2,1)S(1)}, bf16[512,384]{1,0:T(8,128)(2,1)S(1)}, u32[]{:S(2)}, u32[]{:S(2)}) collective-permute-start(bf16[512,384]{1,0:T(8,128)(2,1)S(1)} %pad_maximum_fusion.1), channel_id=1, source_target_pairs={{0,1},{1,0},{4,8},{5,9},{8,4},{9,5},{12,13},{13,12},{2,3},{3,2},{6... | collective-permute-start | bytes 1179656 | tf_op jit(solution)/shard_map/ppermute | solution.py:364
  6.2 12.1 %collective-permute-start = (bf16[512,384]{1,0:T(8,128)(2,1)S(1)}, bf16[512,384]{1,0:T(8,128)(2,1)S(1)}, u32[]{:S(2)}, u32[]{:S(2)}) collective-permute-start(bf16[512,384]{1,0:T(8,128)(2,1)S(1)} %slice.6), channel_id=1, source_target_pairs={{0,2},{2,0},{16,18},{18,16},{4,6},{6,4},{20,22},{22,20},{8,10},{10... | collective-permute-start | bytes 1179656 | tf_op jit(solution)/shard_map/ppermute | solution.py:371
  9.7 16.1 %collective-permute-start.4 = (bf16[512,384]{1,0:T(8,128)(2,1)S(1)}, bf16[512,384]{1,0:T(8,128)(2,1)S(1)}, u32[]{:S(2)}, u32[]{:S(2)}) collective-permute-start(bf16[512,384]{1,0:T(8,128)(2,1)S(1)} %slice.7), channel_id=1, source_target_pairs={{0,2},{2,0},{16,18},{18,16},{4,6},{6,4},{20,22},{22,20},{8,10},{10... | collective-permute-start | bytes 1179656 | tf_op jit(solution)/shard_map/ppermute | solution.py:371
  15.1 10.7 %collective-permute-start.7 = (bf16[512,384]{1,0:T(8,128)(2,1)S(1)}, bf16[512,384]{1,0:T(8,128)(2,1)S(1)}, u32[]{:S(2)}, u32[]{:S(2)}) collective-permute-start(bf16[512,384]{1,0:T(8,128)(2,1)S(1)} %pad_maximum_fusion.3), channel_id=1, source_target_pairs={{0,1},{1,0},{4,8},{5,9},{8,4},{9,5},{12,13},{13,12},{2,3},{3,2},{6... | collective-permute-start | bytes 1179656 | tf_op jit(solution)/shard_map/ppermute | solution.py:364
  15.2 11.5 %collective-permute-start.6 = (bf16[512,384]{1,0:T(8,128)(2,1)S(1)}, bf16[512,384]{1,0:T(8,128)(2,1)S(1)}, u32[]{:S(2)}, u32[]{:S(2)}) collective-permute-start(bf16[512,384]{1,0:T(8,128)(2,1)S(1)} %pad_maximum_fusion.2), channel_id=1, source_target_pairs={{0,4},{1,5},{4,0},{5,1},{8,12},{9,13},{12,8},{13,9},{2,6},{3,7},{6... | collective-permute-start | bytes 1179656 | tf_op jit(solution)/shard_map/ppermute | solution.py:364
  19.3 6.4 %collective-permute-start.5 = (bf16[512,128]{1,0:T(8,128)(2,1)S(1)}, bf16[512,128]{1,0:T(8,128)(2,1)S(1)}, u32[]{:S(2)}, u32[]{:S(2)}) collective-permute-start(bf16[512,128]{1,0:T(8,128)(2,1)S(1)} %get-tuple-element.32), channel_id=1, source_target_pairs={{0,2},{2,0},{1,3},{3,1},{4,6},{6,4},{5,7},{7,5},{8,10},{10,8},{9,1... | collective-permute-start | bytes 393224 | tf_op jit(solution)/shard_map/ppermute | solution.py:378
  21.4 12.8 %collective-permute-start.9 = (bf16[528,256]{1,0:T(8,128)(2,1)S(1)}, bf16[528,256]{1,0:T(8,128)(2,1)S(1)}, u32[]{:S(2)}, u32[]{:S(2)}) collective-permute-start(bf16[528,256]{1,0:T(8,128)(2,1)S(1)} %remote_part.2), channel_id=1, source_target_pairs={{0,2},{2,0},{1,3},{3,1},{4,6},{6,4},{5,7},{7,5},{8,10},{10,8},{9,1... | collective-permute-start | bytes 811016 | tf_op jit(solution)/shard_map/ppermute | solution.py:378
  28.7 8.4 %collective-permute-start.8 = (bf16[528,256]{1,0:T(8,128)(2,1)S(1)}, bf16[528,256]{1,0:T(8,128)(2,1)S(1)}, u32[]{:S(2)}, u32[]{:S(2)}) collective-permute-start(bf16[528,256]{1,0:T(8,128)(2,1)S(1)} %get-tuple-element.43), channel_id=1, source_target_pairs={{0,2},{2,0},{1,3},{3,1},{4,6},{6,4},{5,7},{7,5},{8,10},{10,8},{9,1... | collective-permute-start | bytes 811016 | tf_op jit(solution)/shard_map/ppermute | solution.py:378
  32.7 5.8 %collective-permute-start.10 = (bf16[512,128]{1,0:T(8,128)(2,1)S(1)}, bf16[512,128]{1,0:T(8,128)(2,1)S(1)}, u32[]{:S(2)}, u32[]{:S(2)}) collective-permute-start(bf16[512,128]{1,0:T(8,128)(2,1)S(1)} %get-tuple-element.51), channel_id=1, source_target_pairs={{0,2},{2,0},{1,3},{3,1},{4,6},{6,4},{5,7},{7,5},{8,10},{10,8},{9,1... | collective-permute-start | bytes 393224 | tf_op jit(solution)/shard_map/ppermute | solution.py:378

commit v7 on v6

--- a/solution.py
+++ b/solution.py
@@ -354,13 +354,15 @@
             got_q.append([(lax.ppermute(sent, "row", there),) for there, _ in routes])
             gate = (gate, sent)
         k_now, v_now, _ = lax.optimization_barrier((k, v, gate))
-        halves = []
-        for first in (0, 1):
-            if first and by_core and sides:
-                k_now, v_now, _ = lax.optimization_barrier((k, v, (halves, sides[0][0])))
+        halves = {}
+        for first in (1, 0) if by_core and sides else (0, 1):
+            if by_core and sides:
+                held = (sent, whole) if first else (sent, sides[0][0])
+                k_now, v_now, _ = lax.optimization_barrier((k, v, held))
             row = jnp.where(lax.rem(place, 2) == first, TILE, 0)
             half = [lax.dynamic_slice(x, (row, a), (TILE, b - a)) for x in (k_now, v_now)]
-            halves.append(jnp.concatenate(half, 0))
+            halves[first] = jnp.concatenate(half, 0)
+        halves = [halves[0], halves[1]]
         sides.append([lax.ppermute(h, ("frame", "head"), p) for h, p in zip(halves, pairs)])
         q_now, _ = lax.optimization_barrier((q, halves))
         if not by_core:

time: 39.4 us -> 39.2 us (level)
  starting transfers between devices: 18 us -> 16.5 us
  waiting for transfers between devices: 8.37 us -> 9.69 us
    ppermute x4, waiting for transfers between devices: 4.65 us -> 6.32 us  [send_back(): return [lax.ppermute(x, 'row', p) for x, p in zip(parts, back)]]
    ppermute x4, starting transfers between devices: 4.92 us -> 3.43 us  [per_device(): lax.ppermute(h, ('frame', 'head'), p)]
    ppermute x1, waiting for transfers between devices: 1 us -> 0.01 us  [per_device(): whole = lax.ppermute(q, axes, ONE_ALONG_X)]
    ppermute x4, waiting for transfers between devices: 2.71 us -> 3.36 us  [per_device(): lax.ppermute(h, ('frame', 'head'), p)]
  transfers between devices with their start and end apart: 11 -> 11, of which waited for: 6 -> 5; matrix products, arithmetic and copies ran while one was open for 4% -> 4% of each run, Pallas kernels for 26% -> 26%
where the time goes in v7:
time: 39.2 us; the launch traced here: 39 us
  starting transfers between devices  16.5 us (42%)
  Pallas kernels  10.9 us (28%)
  waiting for transfers between devices  9.69 us (25%)
  local copies, waits for them, and re-layouts  1.56 us (4%)
    ppermute x4, waiting for transfers between devices, send_back(): return [lax.ppermute(x, 'row', p) for x, p in zip(parts, back)]  6.32 us
    ppermute x2, starting transfers between devices, per_device(): got_q.append([(lax.ppermute(sent, axes, ZERO_ALONG_X), whole)])  5.84 us
    ppermute x4, starting transfers between devices, send_back(): return [lax.ppermute(x, 'row', p) for x, p in zip(parts, back)]  4.26 us
    pallas_call x2, Pallas kernels, remote_part(): pl.pallas_call(functools.partial(remote_kernel, first, heads, lead, tail,...  3.5 us
    ppermute x4, starting transfers between devices, per_device(): lax.ppermute(h, ('frame', 'head'), p)  3.43 us
    ppermute x4, waiting for transfers between devices, per_device(): lax.ppermute(h, ('frame', 'head'), p)  3.36 us
    pallas_call x1, Pallas kernels, local_part(): pl.pallas_call(functools.partial(local_kernel, splits), in_specs=[in_vmem...  3.33 us
    ppermute x1, starting transfers between devices, per_device(): whole = lax.ppermute(q, axes, ONE_ALONG_X)  2.97 us
  transfers between devices with their start and end apart: 11, of which 5 were waited for; matrix products, arithmetic and copies ran while one was open for 4% of the time, Pallas kernels for 26%

profile of v7, /device:TPU:0, one launch (start us, length us, event | category | flops | bytes accessed | tf_op | source)
XLA Modules:
  0.0 39.0 jit_solution(7139678003534376968)
XLA Ops:
  0.0 3.0 %collective-permute-start.1 = (bf16[512,768]{1,0:T(8,128)(2,1)}, bf16[512,768]{1,0:T(8,128)(2,1)S(1)}, u32[]{:S(2)}, u32[]{:S(2)}) collective-permute-start(bf16[512,768]{1,0:T(8,128)(2,1)} %bitcast.18), channel_id=1, source_target_pairs={{0,16},{1,3},{2,18},{3,1},{16,0},{17,19},{18,2},{19,17},{4,20},{5,... | collective-permute-start | bytes 2359304 | tf_op jit(solution)/shard_map/ppermute | solution.py:347
  3.0 0.0 copy-start.2
  3.0 1.4 %constant_dynamic-slice_fusion.4 = (bf16[256,384]{1,0:T(8,128)(2,1)S(1)}, bf16[256,384]{1,0:T(8,128)(2,1)S(1)}, bf16[256,384]{1,0:T(8,128)(2,1)S(1)}, bf16[256,384]{1,0:T(8,128)(2,1)S(1)}) fusion(bf16[512,768]{1,0:T(8,128)(2,1)} %bitcast.11, s32[]{:T(128)S(6)} %select_n.18, s32[]{:T(128)S(6)} %select_n.9, bf16[512,768]{1,0:T(8,128)(2,1)} %bitcast.4), kind=kLoop, calls=%fused_computation.8 | loop fusion | bytes 1572872 | tf_op jit(solution)/shard_map/dynamic_slice | solution.py:363
  4.3 0.0 copy-start
  4.4 0.0 copy-start.1
  4.4 1.6 %collective-permute-start.2 = (bf16[512,384]{1,0:T(8,128)(2,1)S(1)}, bf16[512,384]{1,0:T(8,128)(2,1)S(1)}, u32[]{:S(2)}, u32[]{:S(2)}) collective-permute-start(bf16[512,384]{1,0:T(8,128)(2,1)S(1)} %pad_maximum_fusion), channel_id=1, source_target_pairs={{0,4},{1,5},{4,0},{5,1},{8,12},{9,13},{12,8},{13,9},{2,6},{3,7},{6... | collective-permute-start | bytes 1179656 | tf_op jit(solution)/shard_map/ppermute | solution.py:366
  6.1 0.1 collective-permute-start.3
  6.2 0.0 copy-done.2
  6.2 3.4 %collective-permute-start = (bf16[512,384]{1,0:T(8,128)(2,1)S(1)}, bf16[512,384]{1,0:T(8,128)(2,1)S(1)}, u32[]{:S(2)}, u32[]{:S(2)}) collective-permute-start(bf16[512,384]{1,0:T(8,128)(2,1)S(1)} %slice.6), channel_id=1, source_target_pairs={{0,2},{2,0},{16,18},{18,16},{4,6},{6,4},{20,22},{22,20},{8,10},{10... | collective-permute-start | bytes 1179656 | tf_op jit(solution)/shard_map/ppermute | solution.py:373
  9.7 2.4 %collective-permute-start.4 = (bf16[512,384]{1,0:T(8,128)(2,1)S(1)}, bf16[512,384]{1,0:T(8,128)(2,1)S(1)}, u32[]{:S(2)}, u32[]{:S(2)}) collective-permute-start(bf16[512,384]{1,0:T(8,128)(2,1)S(1)} %slice.7), channel_id=1, source_target_pairs={{0,2},{2,0},{16,18},{18,16},{4,6},{6,4},{20,22},{22,20},{8,10},{10... | collective-permute-start | bytes 1179656 | tf_op jit(solution)/shard_map/ppermute | solution.py:373
  12.1 2.9 %collective-permute-done.2.refs_4_.rest_0_ = bf16[512,384]{1,0:T(8,128)(2,1)S(1)} collective-permute-done((bf16[512,384]{1,0:T(8,128)(2,1)S(1)}, bf16[512,384]{1,0:T(8,128)(2,1)S(1)}, u32[]{:S(2)}, u32[]{:S(2)}) %collective-permute-start.2) | collective-permute-done | bytes 393248 | tf_op jit(solution)/shard_map/ppermute | solution.py:366
  15.0 0.0 copy-done
  15.1 0.0 copy-done.1
  15.1 1.6 %collective-permute-start.6 = (bf16[512,384]{1,0:T(8,128)(2,1)S(1)}, bf16[512,384]{1,0:T(8,128)(2,1)S(1)}, u32[]{:S(2)}, u32[]{:S(2)}) collective-permute-start(bf16[512,384]{1,0:T(8,128)(2,1)S(1)} %pad_maximum_fusion.2), channel_id=1, source_target_pairs={{0,4},{1,5},{4,0},{5,1},{8,12},{9,13},{12,8},{13,9},{2,6},{3,7},{6... | collective-permute-start | bytes 1179656 | tf_op jit(solution)/shard_map/ppermute | solution.py:366
  16.8 0.0 collective-permute-done.1.refs_1_
  16.9 0.1 collective-permute-start.7
  17.0 0.0 collective-permute-done.refs_0_
  17.0 0.0 collective-permute-done.3.refs_5_.rest_1_
  17.0 1.0 %lead_part.1 = (bf16[512,128]{1,0:T(8,128)(2,1)S(1)}, f32[128,128]{1,0:T(8,128)S(1)}) custom-call(bf16[512,384]{1,0:T(8,128)(2,1)S(1)} %collective-permute-done.refs_0_, bf16[512,768]{1,0:T(8,128)(2,1)S(1)} %collective-permute-done.1.refs_1_, bf16[512,768]{1,0:T(8,128)(2,1)S(1)} %bitcast.7, bf16[512,768]{1,0:T(8,128)(2,1)S(1)} %bitcast.14, ...), custom_call_target="tpu_custom_call" | custom-call | flops 201326592 | bytes 524288 | tf_op jit(solution)/shard_map/lead_part/pallas_call | solution.py:223
  18.0 1.3 %collective-permute-start.5 = (bf16[512,128]{1,0:T(8,128)(2,1)S(1)}, bf16[512,128]{1,0:T(8,128)(2,1)S(1)}, u32[]{:S(2)}, u32[]{:S(2)}) collective-permute-start(bf16[512,128]{1,0:T(8,128)(2,1)S(1)} %get-tuple-element.32), channel_id=1, source_target_pairs={{0,2},{2,0},{1,3},{3,1},{4,6},{6,4},{5,7},{7,5},{8,10},{10,8},{9,1... | collective-permute-start | bytes 393224 | tf_op jit(solution)/shard_map/ppermute | solution.py:380
  19.3 1.5 %remote_part.2 = bf16[528,256]{1,0:T(8,128)(2,1)S(1)} custom-call(bf16[512,384]{1,0:T(8,128)(2,1)S(1)} %collective-permute-done.refs_0_, bf16[512,768]{1,0:T(8,128)(2,1)S(1)} %collective-permute-done.1.refs_1_, bf16[512,768]{1,0:T(8,128)(2,1)S(1)} %bitcast.8, bf16[512,768]{1,0:T(8,128)(2,1)S(1)} %bitcast.15, ...), custom_call_target="tpu_custom_call" | custom-call | flops 402653184 | bytes 1048576 | tf_op jit(solution)/shard_map/remote_part/pallas_call | solution.py:239
  20.8 0.8 %collective-permute-start.9 = (bf16[528,256]{1,0:T(8,128)(2,1)S(1)}, bf16[528,256]{1,0:T(8,128)(2,1)S(1)}, u32[]{:S(2)}, u32[]{:S(2)}) collective-permute-start(bf16[528,256]{1,0:T(8,128)(2,1)S(1)} %remote_part.2), channel_id=1, source_target_pairs={{0,2},{2,0},{1,3},{3,1},{4,6},{6,4},{5,7},{7,5},{8,10},{10,8},{9,1... | collective-permute-start | bytes 811016 | tf_op jit(solution)/shard_map/ppermute | solution.py:380
  21.6 2.7 %collective-permute-done.5.rest_0_ = bf16[512,128]{1,0:T(8,128)(2,1)S(1)} collective-permute-done((bf16[512,128]{1,0:T(8,128)(2,1)S(1)}, bf16[512,128]{1,0:T(8,128)(2,1)S(1)}, u32[]{:S(2)}, u32[]{:S(2)}) %collective-permute-start.5) | collective-permute-done | bytes 131104 | tf_op jit(solution)/shard_map/ppermute | solution.py:380
  24.4 0.0 collective-permute-done.4.refs_0_
  24.4 0.5 %collective-permute-done.6.refs_4_.rest_2_ = bf16[512,384]{1,0:T(8,128)(2,1)S(1)} collective-permute-done((bf16[512,384]{1,0:T(8,128)(2,1)S(1)}, bf16[512,384]{1,0:T(8,128)(2,1)S(1)}, u32[]{:S(2)}, u32[]{:S(2)}) %collective-permute-start.6) | collective-permute-done | bytes 393248 | tf_op jit(solution)/shard_map/ppermute | solution.py:366
  24.8 0.0 collective-permute-done.7.refs_5_.rest_3_
  24.8 2.0 %remote_part.3 = (bf16[528,256]{1,0:T(8,128)(2,1)S(1)}, bf16[512,128]{1,0:T(8,128)(2,1)S(1)}) custom-call(bf16[512,384]{1,0:T(8,128)(2,1)S(1)} %collective-permute-done.4.refs_0_, bf16[512,768]{1,0:T(8,128)(2,1)S(1)} %collective-permute-done.1.refs_1_, bf16[512,768]{1,0:T(8,128)(2,1)S(1)} %bitcast.9, bf16[512,768]{1,0:T(8,128)(2,1)S(1)} %bitcast.16, ...), custom_call_target="tpu_custom_call" | custom-call | flops 603979776 | bytes 1572864 | tf_op jit(solution)/shard_map/remote_part/pallas_call | solution.py:239
  26.8 1.1 %collective-permute-start.8 = (bf16[528,256]{1,0:T(8,128)(2,1)S(1)}, bf16[528,256]{1,0:T(8,128)(2,1)S(1)}, u32[]{:S(2)}, u32[]{:S(2)}) collective-permute-start(bf16[528,256]{1,0:T(8,128)(2,1)S(1)} %get-tuple-element.43), channel_id=1, source_target_pairs={{0,2},{2,0},{1,3},{3,1},{4,6},{6,4},{5,7},{7,5},{8,10},{10,8},{9,1... | collective-permute-start | bytes 811016 | tf_op jit(solution)/shard_map/ppermute | solution.py:380
  28.0 3.3 %local_part.1 = (f32[512,768]{1,0:T(8,128)S(1)}, f32[128,128]{1,0:T(8,128)S(1)}, f32[128,128]{1,0:T(8,128)S(1)}) custom-call(bf16[512,768]{1,0:T(8,128)(2,1)S(1)} %bitcast.21, bf16[512,768]{1,0:T(8,128)(2,1)S(1)} %bitcast.10, bf16[512,768]{1,0:T(8,128)(2,1)S(1)} %bitcast.17, bf16[512,384]{1,0:T(8,128)(2,1)S(1)} %collective-permute-done.2.refs_4_.rest_0_, ...), custom_call_target="tpu_custom_call" | custom-call | flops 1207959552 | bytes 3145728 | tf_op jit(solution)/shard_map/local_part/pallas_call | solution.py:252
  31.3 1.0 %collective-permute-start.10 = (bf16[512,128]{1,0:T(8,128)(2,1)S(1)}, bf16[512,128]{1,0:T(8,128)(2,1)S(1)}, u32[]{:S(2)}, u32[]{:S(2)}) collective-permute-start(bf16[512,128]{1,0:T(8,128)(2,1)S(1)} %get-tuple-element.51), channel_id=1, source_target_pairs={{0,2},{2,0},{1,3},{3,1},{4,6},{6,4},{5,7},{7,5},{8,10},{10,8},{9,1... | collective-permute-start | bytes 393224 | tf_op jit(solution)/shard_map/ppermute | solution.py:380
  32.3 0.0 collective-permute-done.9.rest_1_
  32.3 1.3 %merge_part.2.rest_1_ = bf16[512,768]{1,0:T(8,128)(2,1)} custom-call(f32[512,768]{1,0:T(8,128)S(1)} %get-tuple-element.46.own, f32[128,128]{1,0:T(8,128)S(1)} %get-tuple-element.48.logs, bf16[512,128]{1,0:T(8,128)(2,1)S(1)} %collective-permute-done.5.rest_0_, bf16[528,256]{1,0:T(8,128)(2,1)S(1)} %collective-permute-done.9.rest_1_), custom_call_target="tpu_custom_call" | custom-call | flops 786432 | bytes 1572864 | tf_op jit(solution)/shard_map/merge_part/pallas_call | solution.py:280
  33.6 2.7 %collective-permute-done.8.rest_0_ = bf16[528,256]{1,0:T(8,128)(2,1)S(1)} collective-permute-done((bf16[528,256]{1,0:T(8,128)(2,1)S(1)}, bf16[528,256]{1,0:T(8,128)(2,1)S(1)}, u32[]{:S(2)}, u32[]{:S(2)}) %collective-permute-start.8) | collective-permute-done | bytes 270368 | tf_op jit(solution)/shard_map/ppermute | solution.py:380
  36.3 1.1 %merge_part.3 = (bf16[512,768]{1,0:T(8,128)(2,1)}, f32[512,128]{1,0:T(8,128)S(1)}, f32[512,128]{1,0:T(8,128)S(1)}) custom-call(f32[512,768]{1,0:T(8,128)S(1)} %get-tuple-element.46.own, f32[128,128]{1,0:T(8,128)S(1)} %get-tuple-element.47.logs, bf16[528,256]{1,0:T(8,128)(2,1)S(1)} %collective-permute-done.8.rest_0_, ...), custom_call_target="tpu_custom_call", output_to_operand_aliasing={{0}: (3, {})} | custom-call | flops 786432 | bytes 1572864 | tf_op jit(solution)/shard_map/merge_part/pallas_call | solution.py:280
  37.4 0.9 %collective-permute-done.10.rest_1_ = bf16[512,128]{1,0:T(8,128)(2,1)S(1)} collective-permute-done((bf16[512,128]{1,0:T(8,128)(2,1)S(1)}, bf16[512,128]{1,0:T(8,128)(2,1)S(1)}, u32[]{:S(2)}, u32[]{:S(2)}) %collective-permute-start.10) | collective-permute-done | bytes 131104 | tf_op jit(solution)/shard_map/ppermute | solution.py:380
  38.3 0.7 %finish_part.1 = bf16[512,768]{1,0:T(8,128)(2,1)} custom-call(f32[512,128]{1,0:T(8,128)S(1)} %get-tuple-element.49.scaled, f32[512,128]{1,0:T(8,128)S(1)} %get-tuple-element.50.rest_0_, bf16[512,128]{1,0:T(8,128)(2,1)S(1)} %collective-permute-done.10.rest_1_, bf16[512,768]{1,0:T(8,128)(2,1)} %get-tuple-element.52.rest_2_), custom_call_target="tpu_custom_call", output_to_operand_aliasing={{}: (3, {})} | custom-call | flops 262144 | bytes 524288 | tf_op jit(solution)/shard_map/finish_part/pallas_call | solution.py:296
  (10 shorter events, 0.3 us)
Async XLA Ops:
  0.0 16.8 %collective-permute-start.1 = (bf16[512,768]{1,0:T(8,128)(2,1)}, bf16[512,768]{1,0:T(8,128)(2,1)S(1)}, u32[]{:S(2)}, u32[]{:S(2)}) collective-permute-start(bf16[512,768]{1,0:T(8,128)(2,1)} %bitcast.18), channel_id=1, source_target_pairs={{0,16},{1,3},{2,18},{3,1},{16,0},{17,19},{18,2},{19,17},{4,20},{5,... | collective-permute-start | bytes 2359304 | tf_op jit(solution)/shard_map/ppermute | solution.py:347
  3.0 3.2 %copy-start.2 = (bf16[8,8,8,768]{3,2,1,0:T(8,128)(2,1)S(1)}, bf16[8,8,8,768]{3,2,1,0:T(8,128)(2,1)}, u32[]{:S(2)}) copy-start(bf16[8,8,8,768]{3,2,1,0:T(8,128)(2,1)} %param.3) | copy-start | bytes 2359300
  4.3 10.7 %copy-start = (bf16[8,8,8,768]{3,2,1,0:T(8,128)(2,1)S(1)}, bf16[8,8,8,768]{3,2,1,0:T(8,128)(2,1)}, u32[]{:S(2)}) copy-start(bf16[8,8,8,768]{3,2,1,0:T(8,128)(2,1)} %param.4) | copy-start | bytes 2359300
  4.4 10.7 %copy-start.1 = (bf16[8,8,8,768]{3,2,1,0:T(8,128)(2,1)S(1)}, bf16[8,8,8,768]{3,2,1,0:T(8,128)(2,1)}, u32[]{:S(2)}) copy-start(bf16[8,8,8,768]{3,2,1,0:T(8,128)(2,1)} %param.5) | copy-start | bytes 2359300
  4.4 10.6 %collective-permute-start.2 = (bf16[512,384]{1,0:T(8,128)(2,1)S(1)}, bf16[512,384]{1,0:T(8,128)(2,1)S(1)}, u32[]{:S(2)}, u32[]{:S(2)}) collective-permute-start(bf16[512,384]{1,0:T(8,128)(2,1)S(1)} %pad_maximum_fusion), channel_id=1, source_target_pairs={{0,4},{1,5},{4,0},{5,1},{8,12},{9,13},{12,8},{13,9},{2,6},{3,7},{6... | collective-permute-start | bytes 1179656 | tf_op jit(solution)/shard_map/ppermute | solution.py:366
  6.1 10.9 %collective-permute-start.3 = (bf16[512,384]{1,0:T(8,128)(2,1)S(1)}, bf16[512,384]{1,0:T(8,128)(2,1)S(1)}, u32[]{:S(2)}, u32[]{:S(2)}) collective-permute-start(bf16[512,384]{1,0:T(8,128)(2,1)S(1)} %pad_maximum_fusion.1), channel_id=1, source_target_pairs={{0,1},{1,0},{4,8},{5,9},{8,4},{9,5},{12,13},{13,12},{2,3},{3,2},{6... | collective-permute-start | bytes 1179656 | tf_op jit(solution)/shard_map/ppermute | solution.py:366
  6.2 10.8 %collective-permute-start = (bf16[512,384]{1,0:T(8,128)(2,1)S(1)}, bf16[512,384]{1,0:T(8,128)(2,1)S(1)}, u32[]{:S(2)}, u32[]{:S(2)}) collective-permute-start(bf16[512,384]{1,0:T(8,128)(2,1)S(1)} %slice.6), channel_id=1, source_target_pairs={{0,2},{2,0},{16,18},{18,16},{4,6},{6,4},{20,22},{22,20},{8,10},{10... | collective-permute-start | bytes 1179656 | tf_op jit(solution)/shard_map/ppermute | solution.py:373
  9.7 14.7 %collective-permute-start.4 = (bf16[512,384]{1,0:T(8,128)(2,1)S(1)}, bf16[512,384]{1,0:T(8,128)(2,1)S(1)}, u32[]{:S(2)}, u32[]{:S(2)}) collective-permute-start(bf16[512,384]{1,0:T(8,128)(2,1)S(1)} %slice.7), channel_id=1, source_target_pairs={{0,2},{2,0},{16,18},{18,16},{4,6},{6,4},{20,22},{22,20},{8,10},{10... | collective-permute-start | bytes 1179656 | tf_op jit(solution)/shard_map/ppermute | solution.py:373
  15.1 9.7 %collective-permute-start.6 = (bf16[512,384]{1,0:T(8,128)(2,1)S(1)}, bf16[512,384]{1,0:T(8,128)(2,1)S(1)}, u32[]{:S(2)}, u32[]{:S(2)}) collective-permute-start(bf16[512,384]{1,0:T(8,128)(2,1)S(1)} %pad_maximum_fusion.2), channel_id=1, source_target_pairs={{0,4},{1,5},{4,0},{5,1},{8,12},{9,13},{12,8},{13,9},{2,6},{3,7},{6... | collective-permute-start | bytes 1179656 | tf_op jit(solution)/shard_map/ppermute | solution.py:366
  16.9 7.9 %collective-permute-start.7 = (bf16[512,384]{1,0:T(8,128)(2,1)S(1)}, bf16[512,384]{1,0:T(8,128)(2,1)S(1)}, u32[]{:S(2)}, u32[]{:S(2)}) collective-permute-start(bf16[512,384]{1,0:T(8,128)(2,1)S(1)} %pad_maximum_fusion.3), channel_id=1, source_target_pairs={{0,1},{1,0},{4,8},{5,9},{8,4},{9,5},{12,13},{13,12},{2,3},{3,2},{6... | collective-permute-start | bytes 1179656 | tf_op jit(solution)/shard_map/ppermute | solution.py:366
  18.0 6.4 %collective-permute-start.5 = (bf16[512,128]{1,0:T(8,128)(2,1)S(1)}, bf16[512,128]{1,0:T(8,128)(2,1)S(1)}, u32[]{:S(2)}, u32[]{:S(2)}) collective-permute-start(bf16[512,128]{1,0:T(8,128)(2,1)S(1)} %get-tuple-element.32), channel_id=1, source_target_pairs={{0,2},{2,0},{1,3},{3,1},{4,6},{6,4},{5,7},{7,5},{8,10},{10,8},{9,1... | collective-permute-start | bytes 393224 | tf_op jit(solution)/shard_map/ppermute | solution.py:380
  20.8 11.5 %collective-permute-start.9 = (bf16[528,256]{1,0:T(8,128)(2,1)S(1)}, bf16[528,256]{1,0:T(8,128)(2,1)S(1)}, u32[]{:S(2)}, u32[]{:S(2)}) collective-permute-start(bf16[528,256]{1,0:T(8,128)(2,1)S(1)} %remote_part.2), channel_id=1, source_target_pairs={{0,2},{2,0},{1,3},{3,1},{4,6},{6,4},{5,7},{7,5},{8,10},{10,8},{9,1... | collective-permute-start | bytes 811016 | tf_op jit(solution)/shard_map/ppermute | solution.py:380
  26.8 9.5 %collective-permute-start.8 = (bf16[528,256]{1,0:T(8,128)(2,1)S(1)}, bf16[528,256]{1,0:T(8,128)(2,1)S(1)}, u32[]{:S(2)}, u32[]{:S(2)}) collective-permute-start(bf16[528,256]{1,0:T(8,128)(2,1)S(1)} %get-tuple-element.43), channel_id=1, source_target_pairs={{0,2},{2,0},{1,3},{3,1},{4,6},{6,4},{5,7},{7,5},{8,10},{10,8},{9,1... | collective-permute-start | bytes 811016 | tf_op jit(solution)/shard_map/ppermute | solution.py:380
  31.3 7.0 %collective-permute-start.10 = (bf16[512,128]{1,0:T(8,128)(2,1)S(1)}, bf16[512,128]{1,0:T(8,128)(2,1)S(1)}, u32[]{:S(2)}, u32[]{:S(2)}) collective-permute-start(bf16[512,128]{1,0:T(8,128)(2,1)S(1)} %get-tuple-element.51), channel_id=1, source_target_pairs={{0,2},{2,0},{1,3},{3,1},{4,6},{6,4},{5,7},{7,5},{8,10},{10,8},{9,1... | collective-permute-start | bytes 393224 | tf_op jit(solution)/shard_map/ppermute | solution.py:380

commit v8 on v7

--- a/solution.py
+++ b/solution.py
@@ -20,7 +20,7 @@
 BLOCKS = ROWS // HD
 LOG_ROWS = 16
 CHUNKS = (3, 3)
-LEADS = (1, 0)
+LEADS = (0, 0)
 TAILS = (0, 1)
 ONE_ALONG_X = tuple((i, i ^ 2 if i % 2 else i ^ 4) for i in range(8))
 ZERO_ALONG_X = tuple((i, i ^ 2) for i in range(0, 8, 2))
@@ -355,10 +355,9 @@
             gate = (gate, sent)
         k_now, v_now, _ = lax.optimization_barrier((k, v, gate))
         halves = {}
-        for first in (1, 0) if by_core and sides else (0, 1):
-            if by_core and sides:
-                held = (sent, whole) if first else (sent, sides[0][0])
-                k_now, v_now, _ = lax.optimization_barrier((k, v, held))
+        for first in (0, 1) if by_core and sides else (0, 1):
+            if by_core and sides and halves:
+                k_now, v_now, _ = lax.optimization_barrier((k, v, (halves, whole)))
             row = jnp.where(lax.rem(place, 2) == first, TILE, 0)
             half = [lax.dynamic_slice(x, (row, a), (TILE, b - a)) for x in (k_now, v_now)]
             halves[first] = jnp.concatenate(half, 0)

time: 39.2 us -> 39.2 us (level)
    ppermute x4 -> x3, waiting for transfers between devices: 6.32 us -> 2.47 us  [send_back(): return [lax.ppermute(x, 'row', p) for x, p in zip(parts, back)]]
    ppermute x2, waiting for transfers between devices: 0.01 us -> 3 us  [per_device(): got_q.append([(lax.ppermute(sent, axes, ZERO_ALONG_X), whole)])]
    ppermute x1, waiting for transfers between devices: 0.01 us -> 1 us  [per_device(): whole = lax.ppermute(q, axes, ONE_ALONG_X)]
    pallas_call x1 -> x0, Pallas kernels: 0.98 us -> none  [lead_part(): pl.pallas_call(functools.partial(lead_kernel, first, heads, len(q)), in_s...]
    ppermute x4, starting transfers between devices: 3.43 us -> 4.34 us  [per_device(): lax.ppermute(h, ('frame', 'head'), p)]
    ppermute x4 -> x3, starting transfers between devices: 4.26 us -> 3.66 us  [send_back(): return [lax.ppermute(x, 'row', p) for x, p in zip(parts, back)]]
    pallas_call x2, Pallas kernels: 3.5 us -> 4.06 us  [remote_part(): pl.pallas_call(functools.partial(remote_kernel, first, heads, lead, tail,...]
  transfers between devices with their start and end apart: 11 -> 10, of which waited for: 5 -> 5; matrix products, arithmetic and copies ran while one was open for 4% -> 4% of each run, Pallas kernels for 26% -> 25%
where the time goes in v8:
time: 39.2 us; the launch traced here: 39 us
  starting transfers between devices  16.8 us (43%)
  Pallas kernels  10.6 us (27%)
  waiting for transfers between devices  9.7 us (25%)
  local copies, waits for them, and re-layouts  1.57 us (4%)
    ppermute x2, starting transfers between devices, per_device(): got_q.append([(lax.ppermute(sent, axes, ZERO_ALONG_X), whole)])  5.84 us
    ppermute x4, starting transfers between devices, per_device(): lax.ppermute(h, ('frame', 'head'), p)  4.34 us
    pallas_call x2, Pallas kernels, remote_part(): pl.pallas_call(functools.partial(remote_kernel, first, heads, lead, tail,...  4.06 us
    ppermute x3, starting transfers between devices, send_back(): return [lax.ppermute(x, 'row', p) for x, p in zip(parts, back)]  3.66 us
    pallas_call x1, Pallas kernels, local_part(): pl.pallas_call(functools.partial(local_kernel, splits), in_specs=[in_vmem...  3.39 us
    ppermute x4, waiting for transfers between devices, per_device(): lax.ppermute(h, ('frame', 'head'), p)  3.22 us
    ppermute x2, waiting for transfers between devices, per_device(): got_q.append([(lax.ppermute(sent, axes, ZERO_ALONG_X), whole)])  3 us
    ppermute x1, starting transfers between devices, per_device(): whole = lax.ppermute(q, axes, ONE_ALONG_X)  2.97 us
  transfers between devices with their start and end apart: 10, of which 5 were waited for; matrix products, arithmetic and copies ran while one was open for 4% of the time, Pallas kernels for 25%

profile of v8, /device:TPU:0, one launch (start us, length us, event | category | flops | bytes accessed | tf_op | source)
XLA Modules:
  0.0 39.0 jit_solution(4231364653583415360)
XLA Ops:
  0.0 3.0 %collective-permute-start.1 = (bf16[512,768]{1,0:T(8,128)(2,1)}, bf16[512,768]{1,0:T(8,128)(2,1)S(1)}, u32[]{:S(2)}, u32[]{:S(2)}) collective-permute-start(bf16[512,768]{1,0:T(8,128)(2,1)} %bitcast.16), channel_id=1, source_target_pairs={{0,16},{1,3},{2,18},{3,1},{16,0},{17,19},{18,2},{19,17},{4,20},{5,... | collective-permute-start | bytes 2359304 | tf_op jit(solution)/shard_map/ppermute | solution.py:347
  3.0 0.0 copy-start.2
  3.0 1.4 %constant_dynamic-slice_fusion.4 = (bf16[256,384]{1,0:T(8,128)(2,1)S(1)}, bf16[256,384]{1,0:T(8,128)(2,1)S(1)}, bf16[256,384]{1,0:T(8,128)(2,1)S(1)}, bf16[256,384]{1,0:T(8,128)(2,1)S(1)}) fusion(bf16[512,768]{1,0:T(8,128)(2,1)} %bitcast.10, s32[]{:T(128)S(6)} %select_n.18, s32[]{:T(128)S(6)} %select_n.9, bf16[512,768]{1,0:T(8,128)(2,1)} %bitcast.4), kind=kLoop, calls=%fused_computation.8 | loop fusion | bytes 1572872 | tf_op jit(solution)/shard_map/dynamic_slice | solution.py:362
  4.3 0.0 copy-start
  4.4 0.0 copy-start.1
  4.4 1.6 %collective-permute-start.2 = (bf16[512,384]{1,0:T(8,128)(2,1)S(1)}, bf16[512,384]{1,0:T(8,128)(2,1)S(1)}, u32[]{:S(2)}, u32[]{:S(2)}) collective-permute-start(bf16[512,384]{1,0:T(8,128)(2,1)S(1)} %pad_maximum_fusion), channel_id=1, source_target_pairs={{0,4},{1,5},{4,0},{5,1},{8,12},{9,13},{12,8},{13,9},{2,6},{3,7},{6... | collective-permute-start | bytes 1179656 | tf_op jit(solution)/shard_map/ppermute | solution.py:365
  6.1 0.1 collective-permute-start.3
  6.2 0.0 copy-done.2
  6.2 3.4 %collective-permute-start = (bf16[512,384]{1,0:T(8,128)(2,1)S(1)}, bf16[512,384]{1,0:T(8,128)(2,1)S(1)}, u32[]{:S(2)}, u32[]{:S(2)}) collective-permute-start(bf16[512,384]{1,0:T(8,128)(2,1)S(1)} %slice.6), channel_id=1, source_target_pairs={{0,2},{2,0},{16,18},{18,16},{4,6},{6,4},{20,22},{22,20},{8,10},{10... | collective-permute-start | bytes 1179656 | tf_op jit(solution)/shard_map/ppermute | solution.py:372
  9.7 2.4 %collective-permute-start.4 = (bf16[512,384]{1,0:T(8,128)(2,1)S(1)}, bf16[512,384]{1,0:T(8,128)(2,1)S(1)}, u32[]{:S(2)}, u32[]{:S(2)}) collective-permute-start(bf16[512,384]{1,0:T(8,128)(2,1)S(1)} %slice.7), channel_id=1, source_target_pairs={{0,2},{2,0},{16,18},{18,16},{4,6},{6,4},{20,22},{22,20},{8,10},{10... | collective-permute-start | bytes 1179656 | tf_op jit(solution)/shard_map/ppermute | solution.py:372
  12.1 1.0 %collective-permute-done.1.refs_1_ = bf16[512,768]{1,0:T(8,128)(2,1)S(1)} collective-permute-done((bf16[512,768]{1,0:T(8,128)(2,1)}, bf16[512,768]{1,0:T(8,128)(2,1)S(1)}, u32[]{:S(2)}, u32[]{:S(2)}) %collective-permute-start.1) | collective-permute-done | bytes 786464 | tf_op jit(solution)/shard_map/ppermute | solution.py:347
  13.1 0.0 copy-done
  13.2 0.0 copy-done.1
  13.4 0.1 collective-permute-start.6
  13.5 3.0 %collective-permute-done.refs_0_ = bf16[512,384]{1,0:T(8,128)(2,1)S(1)} collective-permute-done((bf16[512,384]{1,0:T(8,128)(2,1)S(1)}, bf16[512,384]{1,0:T(8,128)(2,1)S(1)}, u32[]{:S(2)}, u32[]{:S(2)}) %collective-permute-start) | collective-permute-done | bytes 393248 | tf_op jit(solution)/shard_map/ppermute | solution.py:372
  16.5 2.6 %collective-permute-start.5 = (bf16[512,384]{1,0:T(8,128)(2,1)S(1)}, bf16[512,384]{1,0:T(8,128)(2,1)S(1)}, u32[]{:S(2)}, u32[]{:S(2)}) collective-permute-start(bf16[512,384]{1,0:T(8,128)(2,1)S(1)} %pad_maximum_fusion.2), channel_id=1, source_target_pairs={{0,4},{1,5},{4,0},{5,1},{8,12},{9,13},{12,8},{13,9},{2,6},{3,7},{6... | collective-permute-start | bytes 1179656 | tf_op jit(solution)/shard_map/ppermute | solution.py:365
  19.0 0.0 collective-permute-done.2.refs_4_.rest_0_
  19.0 0.0 collective-permute-done.3.refs_5_.rest_1_
  19.0 2.1 %remote_part.2 = bf16[528,384]{1,0:T(8,128)(2,1)S(1)} custom-call(bf16[512,384]{1,0:T(8,128)(2,1)S(1)} %collective-permute-done.refs_0_, bf16[512,768]{1,0:T(8,128)(2,1)S(1)} %collective-permute-done.1.refs_1_, bf16[512,768]{1,0:T(8,128)(2,1)S(1)} %bitcast.7, bf16[512,768]{1,0:T(8,128)(2,1)S(1)} %bitcast.13, ...), custom_call_target="tpu_custom_call" | custom-call | flops 603979776 | bytes 1572864 | tf_op jit(solution)/shard_map/remote_part/pallas_call | solution.py:239
  21.1 1.5 %collective-permute-start.8 = (bf16[528,384]{1,0:T(8,128)(2,1)S(1)}, bf16[528,384]{1,0:T(8,128)(2,1)S(1)}, u32[]{:S(2)}, u32[]{:S(2)}) collective-permute-start(bf16[528,384]{1,0:T(8,128)(2,1)S(1)} %remote_part.2), channel_id=1, source_target_pairs={{0,2},{2,0},{1,3},{3,1},{4,6},{6,4},{5,7},{7,5},{8,10},{10,8},{9,1... | collective-permute-start | bytes 1216520 | tf_op jit(solution)/shard_map/ppermute | solution.py:379
  22.6 0.0 collective-permute-done.4.refs_0_
  22.6 0.0 collective-permute-done.6.refs_5_.rest_3_
  22.6 3.2 %collective-permute-done.5.refs_4_.rest_2_ = bf16[512,384]{1,0:T(8,128)(2,1)S(1)} collective-permute-done((bf16[512,384]{1,0:T(8,128)(2,1)S(1)}, bf16[512,384]{1,0:T(8,128)(2,1)S(1)}, u32[]{:S(2)}, u32[]{:S(2)}) %collective-permute-start.5) | collective-permute-done | bytes 393248 | tf_op jit(solution)/shard_map/ppermute | solution.py:365
  25.9 2.0 %remote_part.3 = (bf16[528,256]{1,0:T(8,128)(2,1)S(1)}, bf16[512,128]{1,0:T(8,128)(2,1)S(1)}) custom-call(bf16[512,384]{1,0:T(8,128)(2,1)S(1)} %collective-permute-done.4.refs_0_, bf16[512,768]{1,0:T(8,128)(2,1)S(1)} %collective-permute-done.1.refs_1_, bf16[512,768]{1,0:T(8,128)(2,1)S(1)} %bitcast.8, bf16[512,768]{1,0:T(8,128)(2,1)S(1)} %bitcast.14, ...), custom_call_target="tpu_custom_call" | custom-call | flops 603979776 | bytes 1572864 | tf_op jit(solution)/shard_map/remote_part/pallas_call | solution.py:239
  27.8 1.5 %collective-permute-start.7 = (bf16[528,256]{1,0:T(8,128)(2,1)S(1)}, bf16[528,256]{1,0:T(8,128)(2,1)S(1)}, u32[]{:S(2)}, u32[]{:S(2)}) collective-permute-start(bf16[528,256]{1,0:T(8,128)(2,1)S(1)} %get-tuple-element.35), channel_id=1, source_target_pairs={{0,2},{2,0},{1,3},{3,1},{4,6},{6,4},{5,7},{7,5},{8,10},{10,8},{9,1... | collective-permute-start | bytes 811016 | tf_op jit(solution)/shard_map/ppermute | solution.py:379
  29.4 3.4 %local_part.1 = (f32[512,768]{1,0:T(8,128)S(1)}, f32[128,128]{1,0:T(8,128)S(1)}, f32[128,128]{1,0:T(8,128)S(1)}) custom-call(bf16[512,768]{1,0:T(8,128)(2,1)S(1)} %bitcast.19, bf16[512,768]{1,0:T(8,128)(2,1)S(1)} %bitcast.9, bf16[512,768]{1,0:T(8,128)(2,1)S(1)} %bitcast.15, bf16[512,384]{1,0:T(8,128)(2,1)S(1)} %collective-permute-done.2.refs_4_.rest_0_, ...), custom_call_target="tpu_custom_call" | custom-call | flops 1207959552 | bytes 3145728 | tf_op jit(solution)/shard_map/local_part/pallas_call | solution.py:252
  32.8 0.6 %collective-permute-start.9 = (bf16[512,128]{1,0:T(8,128)(2,1)S(1)}, bf16[512,128]{1,0:T(8,128)(2,1)S(1)}, u32[]{:S(2)}, u32[]{:S(2)}) collective-permute-start(bf16[512,128]{1,0:T(8,128)(2,1)S(1)} %get-tuple-element.43), channel_id=1, source_target_pairs={{0,2},{2,0},{1,3},{3,1},{4,6},{6,4},{5,7},{7,5},{8,10},{10,8},{9,1... | collective-permute-start | bytes 393224 | tf_op jit(solution)/shard_map/ppermute | solution.py:379
  33.4 0.0 collective-permute-done.8.rest_0_
  33.4 1.3 %merge_part.2.rest_1_ = bf16[512,768]{1,0:T(8,128)(2,1)} custom-call(f32[512,768]{1,0:T(8,128)S(1)} %get-tuple-element.38.own, f32[128,128]{1,0:T(8,128)S(1)} %get-tuple-element.40.logs, bf16[528,384]{1,0:T(8,128)(2,1)S(1)} %collective-permute-done.8.rest_0_), custom_call_target="tpu_custom_call" | custom-call | flops 786432 | bytes 1572864 | tf_op jit(solution)/shard_map/merge_part/pallas_call | solution.py:280
  34.7 2.2 %collective-permute-done.7.rest_0_ = bf16[528,256]{1,0:T(8,128)(2,1)S(1)} collective-permute-done((bf16[528,256]{1,0:T(8,128)(2,1)S(1)}, bf16[528,256]{1,0:T(8,128)(2,1)S(1)}, u32[]{:S(2)}, u32[]{:S(2)}) %collective-permute-start.7) | collective-permute-done | bytes 270368 | tf_op jit(solution)/shard_map/ppermute | solution.py:379
  36.9 1.1 %merge_part.3 = (bf16[512,768]{1,0:T(8,128)(2,1)}, f32[512,128]{1,0:T(8,128)S(1)}, f32[512,128]{1,0:T(8,128)S(1)}) custom-call(f32[512,768]{1,0:T(8,128)S(1)} %get-tuple-element.38.own, f32[128,128]{1,0:T(8,128)S(1)} %get-tuple-element.39.logs, bf16[528,256]{1,0:T(8,128)(2,1)S(1)} %collective-permute-done.7.rest_0_, ...), custom_call_target="tpu_custom_call", output_to_operand_aliasing={{0}: (3, {})} | custom-call | flops 786432 | bytes 1572864 | tf_op jit(solution)/shard_map/merge_part/pallas_call | solution.py:280
  38.0 0.3 collective-permute-done.9.rest_1_
  38.3 0.7 %finish_part.1 = bf16[512,768]{1,0:T(8,128)(2,1)} custom-call(f32[512,128]{1,0:T(8,128)S(1)} %get-tuple-element.41.scaled, f32[512,128]{1,0:T(8,128)S(1)} %get-tuple-element.42.rest_0_, bf16[512,128]{1,0:T(8,128)(2,1)S(1)} %collective-permute-done.9.rest_1_, bf16[512,768]{1,0:T(8,128)(2,1)} %get-tuple-element.44.rest_2_), custom_call_target="tpu_custom_call", output_to_operand_aliasing={{}: (3, {})} | custom-call | flops 262144 | bytes 524288 | tf_op jit(solution)/shard_map/finish_part/pallas_call | solution.py:296
  (10 shorter events, 0.4 us)
Async XLA Ops:
  0.0 13.1 %collective-permute-start.1 = (bf16[512,768]{1,0:T(8,128)(2,1)}, bf16[512,768]{1,0:T(8,128)(2,1)S(1)}, u32[]{:S(2)}, u32[]{:S(2)}) collective-permute-start(bf16[512,768]{1,0:T(8,128)(2,1)} %bitcast.16), channel_id=1, source_target_pairs={{0,16},{1,3},{2,18},{3,1},{16,0},{17,19},{18,2},{19,17},{4,20},{5,... | collective-permute-start | bytes 2359304 | tf_op jit(solution)/shard_map/ppermute | solution.py:347
  3.0 3.2 %copy-start.2 = (bf16[8,8,8,768]{3,2,1,0:T(8,128)(2,1)S(1)}, bf16[8,8,8,768]{3,2,1,0:T(8,128)(2,1)}, u32[]{:S(2)}) copy-start(bf16[8,8,8,768]{3,2,1,0:T(8,128)(2,1)} %param.3) | copy-start | bytes 2359300
  4.3 8.8 %copy-start = (bf16[8,8,8,768]{3,2,1,0:T(8,128)(2,1)S(1)}, bf16[8,8,8,768]{3,2,1,0:T(8,128)(2,1)}, u32[]{:S(2)}) copy-start(bf16[8,8,8,768]{3,2,1,0:T(8,128)(2,1)} %param.4) | copy-start | bytes 2359300
  4.4 8.8 %copy-start.1 = (bf16[8,8,8,768]{3,2,1,0:T(8,128)(2,1)S(1)}, bf16[8,8,8,768]{3,2,1,0:T(8,128)(2,1)}, u32[]{:S(2)}) copy-start(bf16[8,8,8,768]{3,2,1,0:T(8,128)(2,1)} %param.5) | copy-start | bytes 2359300
  4.4 14.6 %collective-permute-start.2 = (bf16[512,384]{1,0:T(8,128)(2,1)S(1)}, bf16[512,384]{1,0:T(8,128)(2,1)S(1)}, u32[]{:S(2)}, u32[]{:S(2)}) collective-permute-start(bf16[512,384]{1,0:T(8,128)(2,1)S(1)} %pad_maximum_fusion), channel_id=1, source_target_pairs={{0,4},{1,5},{4,0},{5,1},{8,12},{9,13},{12,8},{13,9},{2,6},{3,7},{6... | collective-permute-start | bytes 1179656 | tf_op jit(solution)/shard_map/ppermute | solution.py:365
  6.1 12.9 %collective-permute-start.3 = (bf16[512,384]{1,0:T(8,128)(2,1)S(1)}, bf16[512,384]{1,0:T(8,128)(2,1)S(1)}, u32[]{:S(2)}, u32[]{:S(2)}) collective-permute-start(bf16[512,384]{1,0:T(8,128)(2,1)S(1)} %pad_maximum_fusion.1), channel_id=1, source_target_pairs={{0,1},{1,0},{4,8},{5,9},{8,4},{9,5},{12,13},{13,12},{2,3},{3,2},{6... | collective-permute-start | bytes 1179656 | tf_op jit(solution)/shard_map/ppermute | solution.py:365
  6.2 10.2 %collective-permute-start = (bf16[512,384]{1,0:T(8,128)(2,1)S(1)}, bf16[512,384]{1,0:T(8,128)(2,1)S(1)}, u32[]{:S(2)}, u32[]{:S(2)}) collective-permute-start(bf16[512,384]{1,0:T(8,128)(2,1)S(1)} %slice.6), channel_id=1, source_target_pairs={{0,2},{2,0},{16,18},{18,16},{4,6},{6,4},{20,22},{22,20},{8,10},{10... | collective-permute-start | bytes 1179656 | tf_op jit(solution)/shard_map/ppermute | solution.py:372
  9.7 12.9 %collective-permute-start.4 = (bf16[512,384]{1,0:T(8,128)(2,1)S(1)}, bf16[512,384]{1,0:T(8,128)(2,1)S(1)}, u32[]{:S(2)}, u32[]{:S(2)}) collective-permute-start(bf16[512,384]{1,0:T(8,128)(2,1)S(1)} %slice.7), channel_id=1, source_target_pairs={{0,2},{2,0},{16,18},{18,16},{4,6},{6,4},{20,22},{22,20},{8,10},{10... | collective-permute-start | bytes 1179656 | tf_op jit(solution)/shard_map/ppermute | solution.py:372
  13.4 9.2 %collective-permute-start.6 = (bf16[512,384]{1,0:T(8,128)(2,1)S(1)}, bf16[512,384]{1,0:T(8,128)(2,1)S(1)}, u32[]{:S(2)}, u32[]{:S(2)}) collective-permute-start(bf16[512,384]{1,0:T(8,128)(2,1)S(1)} %pad_maximum_fusion.3), channel_id=1, source_target_pairs={{0,1},{1,0},{4,8},{5,9},{8,4},{9,5},{12,13},{13,12},{2,3},{3,2},{6... | collective-permute-start | bytes 1179656 | tf_op jit(solution)/shard_map/ppermute | solution.py:365
  16.5 9.4 %collective-permute-start.5 = (bf16[512,384]{1,0:T(8,128)(2,1)S(1)}, bf16[512,384]{1,0:T(8,128)(2,1)S(1)}, u32[]{:S(2)}, u32[]{:S(2)}) collective-permute-start(bf16[512,384]{1,0:T(8,128)(2,1)S(1)} %pad_maximum_fusion.2), channel_id=1, source_target_pairs={{0,4},{1,5},{4,0},{5,1},{8,12},{9,13},{12,8},{13,9},{2,6},{3,7},{6... | collective-permute-start | bytes 1179656 | tf_op jit(solution)/shard_map/ppermute | solution.py:365
  21.1 12.3 %collective-permute-start.8 = (bf16[528,384]{1,0:T(8,128)(2,1)S(1)}, bf16[528,384]{1,0:T(8,128)(2,1)S(1)}, u32[]{:S(2)}, u32[]{:S(2)}) collective-permute-start(bf16[528,384]{1,0:T(8,128)(2,1)S(1)} %remote_part.2), channel_id=1, source_target_pairs={{0,2},{2,0},{1,3},{3,1},{4,6},{6,4},{5,7},{7,5},{8,10},{10,8},{9,1... | collective-permute-start | bytes 1216520 | tf_op jit(solution)/shard_map/ppermute | solution.py:379
  27.8 9.0 %collective-permute-start.7 = (bf16[528,256]{1,0:T(8,128)(2,1)S(1)}, bf16[528,256]{1,0:T(8,128)(2,1)S(1)}, u32[]{:S(2)}, u32[]{:S(2)}) collective-permute-start(bf16[528,256]{1,0:T(8,128)(2,1)S(1)} %get-tuple-element.35), channel_id=1, source_target_pairs={{0,2},{2,0},{1,3},{3,1},{4,6},{6,4},{5,7},{7,5},{8,10},{10,8},{9,1... | collective-permute-start | bytes 811016 | tf_op jit(solution)/shard_map/ppermute | solution.py:379
  32.8 5.5 %collective-permute-start.9 = (bf16[512,128]{1,0:T(8,128)(2,1)S(1)}, bf16[512,128]{1,0:T(8,128)(2,1)S(1)}, u32[]{:S(2)}, u32[]{:S(2)}) collective-permute-start(bf16[512,128]{1,0:T(8,128)(2,1)S(1)} %get-tuple-element.43), channel_id=1, source_target_pairs={{0,2},{2,0},{1,3},{3,1},{4,6},{6,4},{5,7},{7,5},{8,10},{10,8},{9,1... | collective-permute-start | bytes 393224 | tf_op jit(solution)/shard_map/ppermute | solution.py:379

commit v9 on v7

--- a/solution.py
+++ b/solution.py
@@ -117,19 +117,12 @@
         out[ROWS:, 2 * HD :] = jnp.zeros((LOG_ROWS, out.shape[1] - 2 * HD), out.dtype)
 
 
-def local_kernel(splits, q, k, v, *rest):
-    sides, out, logs = rest[: -1 - len(splits)], rest[-1 - len(splits)], rest[-len(splits) :]
-    first = 0
-    for c, heads in enumerate(splits):
-        columns = slice(first * HD, (first + heads) * HD)
-
-        def store(rows, here, block, first=first):
-            out[rows, first * HD + here.start : first * HD + here.stop] = block
-
-        logs[c][...] = attend(
-            first, heads, q.at[:, columns], k, v, sides[2 * c], sides[2 * c + 1], store
-        )
-        first += heads
+def local_kernel(first, heads, q, k, v, even, odd, out, logs):
+    def store(rows, here, block):
+        out[rows, here] = block
+
+    mine = q.at[:, first * HD : (first + heads) * HD]
+    logs[...] = attend(first, heads, mine, k, v, even, odd, store)
 
 
 def shares_of(logs, theirs):
@@ -174,7 +167,7 @@
         for j in range(heads):
             here = slice(j * HD, (j + 1) * HD)
             at = b * (LOG_ROWS // BLOCKS) + j
-            summed = shares[0][:, at : at + 1] * own[rows, (first + j) * HD : (first + j + 1) * HD]
+            summed = shares[0][:, at : at + 1] * own[rows, here]
             parts, start = (leads, j * HD) if j < lead else (theirs, (j - lead) * HD)
             for share, part in zip(shares[1:], parts):
                 block = part[rows, start : start + HD].astype(jnp.float32)
@@ -186,7 +179,7 @@
         for j in range(tail):
             rows, here = slice(b * HD, (b + 1) * HD), slice(j * HD, (j + 1) * HD)
             at = b * (LOG_ROWS // BLOCKS) + heads + j
-            own_at = (first + heads + j) * HD
+            own_at = (heads + j) * HD
             later[0][rows, here] = shares[0][:, at : at + 1] * own[rows, own_at : own_at + HD]
             for share, spread in zip(shares[1:], later[1:]):
                 spread[rows, here] = jnp.broadcast_to(share[:, at : at + 1], (HD, HD))
@@ -247,20 +240,19 @@
     )(*q, k, v, even, odd, *earlier)
 
 
-def local_part(splits, q, k, v, sides):
-    heads = sum(splits)
+def local_part(first, heads, q, k, v, even, odd):
     return pl.pallas_call(
-        functools.partial(local_kernel, splits),
-        in_specs=[in_vmem()] * (3 + len(sides)),
-        out_specs=[in_vmem()] * (1 + len(splits)),
+        functools.partial(local_kernel, first, heads),
+        in_specs=[in_vmem()] * 5,
+        out_specs=[in_vmem()] * 2,
         out_shape=[
             jax.ShapeDtypeStruct((ROWS, heads * HD), jnp.float32),
-            *[jax.ShapeDtypeStruct((HD, HD), jnp.float32) for _ in splits],
+            jax.ShapeDtypeStruct((HD, HD), jnp.float32),
         ],
         compiler_params=pltpu.CompilerParams(vmem_limit_bytes=VMEM_BYTES),
         cost_estimate=cost(heads),
         name="local_part",
-    )(q, k, v, *sides)
+    )(q, k, v, even, odd)
 
 
 def merge_cost(heads):
@@ -273,7 +265,7 @@
     return [pltpu.VMEM((ROWS, heads * HD), jnp.bfloat16), pltpu.SemaphoreType.DMA((BLOCKS,))]
 
 
-def merge_part(first, lead, heads, tail, own, logs, leads, theirs, prior):
+def merge_part(first, lead, heads, tail, width, own, logs, leads, theirs, prior):
     groups = len(theirs)
     count = len(leads) + groups
     later = [jax.ShapeDtypeStruct((ROWS, tail * HD), jnp.float32)] * ((1 + groups) * (tail > 0))
@@ -281,7 +273,7 @@
         functools.partial(merge_kernel, first, lead, heads, tail, groups),
         in_specs=[in_vmem()] * (2 + count) + [pl.BlockSpec(memory_space=pl.ANY)] * len(prior),
         out_specs=[pl.BlockSpec(memory_space=pl.ANY)] + [in_vmem()] * len(later),
-        out_shape=[jax.ShapeDtypeStruct(own.shape, jnp.bfloat16)] + later,
+        out_shape=[jax.ShapeDtypeStruct((ROWS, width), jnp.bfloat16)] + later,
         scratch_shapes=copy_scratch(heads),
         input_output_aliases={2 + count: 0} if prior else {},
         compiler_params=pltpu.CompilerParams(vmem_limit_bytes=VMEM_BYTES),
@@ -379,7 +371,7 @@
     def send_back(parts):
         return [lax.ppermute(x, "row", p) for x, p in zip(parts, back)]
 
-    answers, led = [], []
+    answers, led, kept = [], [], []
     k_now, v_now = k, v
     for (a, b), lead, tail, chunk_q, (even, odd) in zip(bounds, LEADS, TAILS, got_q, sides):
         parts, firsts = [], []
@@ -393,14 +385,18 @@
             parts.append(remote_part(a + lead, b - a - lead, lead, tail, *operands, *earlier))
         led.append(send_back(firsts))
         answers.append([list(x) for x in zip(*parts)])
-        k_now, v_now, _ = lax.optimization_barrier((k, v, (parts, led[-1])))
-
-    q_local, _ = lax.optimization_barrier((q, answers))
-    own, *logs = local_part(splits, q_local, k, v, [s for pair in sides for s in pair])
+        q_now, _ = lax.optimization_barrier((q, parts))
+        kept.append(local_part(a, b - a, q_now, k, v, even, odd))
+        k_now, v_now, _ = lax.optimization_barrier((k, v, (parts, led[-1], kept[-1][1])))
+
     out = ()
-    for (a, b), lead, tail, log, leads, parts in zip(bounds, LEADS, TAILS, logs, led, answers):
+    for (a, b), lead, tail, (own, log), leads, parts in zip(
+        bounds, LEADS, TAILS, kept, led, answers
+    ):
         theirs = send_back(parts[0])
-        out, later = merge_part(a, lead, b - a - tail, tail, own, log, leads, theirs, out)
+        out, later = merge_part(
+            a, lead, b - a - tail, tail, features, own, log, leads, theirs, out
+        )
         if tail:
             last, _ = lax.optimization_barrier((parts[1], log))
             out = finish_part(b - tail, tail, later[0], later[1:], send_back(last), out)

time: 39.2 us -> 39.2 us (level)
  waiting for transfers between devices: 9.69 us -> 9.01 us
  Pallas kernels: 10.9 us -> 11.5 us
    ppermute x4, waiting for transfers between devices: 6.32 us -> 5.79 us  [send_back(): return [lax.ppermute(x, 'row', p) for x, p in zip(parts, back)]]
    pallas_call x1 -> x2, Pallas kernels: 3.33 us -> 3.85 us  [local_part(): pl.pallas_call(functools.partial(local_kernel, first, heads), in_specs=[i...]
  transfers between devices with their start and end apart: 11 -> 11, of which waited for: 5 -> 5; matrix products, arithmetic and copies ran while one was open for 4% -> 4% of each run, Pallas kernels for 26% -> 28%
where the time goes in v9:
time: 39.2 us; the launch traced here: 39 us
  starting transfers between devices  16.6 us (42%)
  Pallas kernels  11.5 us (29%)
  waiting for transfers between devices  9.01 us (23%)
  local copies, waits for them, and re-layouts  1.5 us (4%)
    ppermute x2, starting transfers between devices, per_device(): got_q.append([(lax.ppermute(sent, axes, ZERO_ALONG_X), whole)])  5.97 us
    ppermute x4, waiting for transfers between devices, send_back(): return [lax.ppermute(x, 'row', p) for x, p in zip(parts, back)]  5.79 us
    ppermute x4, starting transfers between devices, send_back(): return [lax.ppermute(x, 'row', p) for x, p in zip(parts, back)]  4.26 us
    pallas_call x2, Pallas kernels, local_part(): pl.pallas_call(functools.partial(local_kernel, first, heads), in_specs=[i...  3.85 us
    pallas_call x2, Pallas kernels, remote_part(): pl.pallas_call(functools.partial(remote_kernel, first, heads, lead, tail,...  3.5 us
    ppermute x4, starting transfers between devices, per_device(): lax.ppermute(h, ('frame', 'head'), p)  3.43 us
    ppermute x4, waiting for transfers between devices, per_device(): lax.ppermute(h, ('frame', 'head'), p)  3.21 us
    ppermute x1, starting transfers between devices, per_device(): whole = lax.ppermute(q, axes, ONE_ALONG_X)  2.97 us
  transfers between devices with their start and end apart: 11, of which 5 were waited for; matrix products, arithmetic and copies ran while one was open for 4% of the time, Pallas kernels for 28%

profile of v9, /device:TPU:0, one launch (start us, length us, event | category | flops | bytes accessed | tf_op | source)
XLA Modules:
  0.0 39.0 jit_solution(7948994026511113490)
XLA Ops:
  0.0 3.0 %collective-permute-start.1 = (bf16[512,768]{1,0:T(8,128)(2,1)}, bf16[512,768]{1,0:T(8,128)(2,1)S(1)}, u32[]{:S(2)}, u32[]{:S(2)}) collective-permute-start(bf16[512,768]{1,0:T(8,128)(2,1)} %bitcast.20), channel_id=1, source_target_pairs={{0,16},{1,3},{2,18},{3,1},{16,0},{17,19},{18,2},{19,17},{4,20},{5,... | collective-permute-start | bytes 2359304 | tf_op jit(solution)/shard_map/ppermute | solution.py:339
  3.0 1.3 %constant_dynamic-slice_fusion.4 = (bf16[256,384]{1,0:T(8,128)(2,1)S(1)}, bf16[256,384]{1,0:T(8,128)(2,1)S(1)}, bf16[256,384]{1,0:T(8,128)(2,1)S(1)}, bf16[256,384]{1,0:T(8,128)(2,1)S(1)}) fusion(bf16[512,768]{1,0:T(8,128)(2,1)} %bitcast.12, s32[]{:T(128)S(6)} %select_n.18, s32[]{:T(128)S(6)} %select_n.9, bf16[512,768]{1,0:T(8,128)(2,1)} %bitcast.4), kind=kLoop, calls=%fused_computation.8 | loop fusion | bytes 1572872 | tf_op jit(solution)/shard_map/dynamic_slice | solution.py:355
  4.3 0.0 copy-start.2
  4.3 1.6 %collective-permute-start.3 = (bf16[512,384]{1,0:T(8,128)(2,1)S(1)}, bf16[512,384]{1,0:T(8,128)(2,1)S(1)}, u32[]{:S(2)}, u32[]{:S(2)}) collective-permute-start(bf16[512,384]{1,0:T(8,128)(2,1)S(1)} %pad_maximum_fusion), channel_id=1, source_target_pairs={{0,4},{1,5},{4,0},{5,1},{8,12},{9,13},{12,8},{13,9},{2,6},{3,7},{6... | collective-permute-start | bytes 1179656 | tf_op jit(solution)/shard_map/ppermute | solution.py:358
  6.0 0.0 copy-start.1
  6.0 0.1 collective-permute-start.4
  6.1 0.0 copy-done.2
  6.2 0.0 copy-start
  6.2 3.5 %collective-permute-start.2 = (bf16[512,384]{1,0:T(8,128)(2,1)S(1)}, bf16[512,384]{1,0:T(8,128)(2,1)S(1)}, u32[]{:S(2)}, u32[]{:S(2)}) collective-permute-start(bf16[512,384]{1,0:T(8,128)(2,1)S(1)} %slice.6), channel_id=1, source_target_pairs={{0,2},{2,0},{16,18},{18,16},{4,6},{6,4},{20,22},{22,20},{8,10},{10... | collective-permute-start | bytes 1179656 | tf_op jit(solution)/shard_map/ppermute | solution.py:365
  9.8 2.4 %collective-permute-start = (bf16[512,384]{1,0:T(8,128)(2,1)S(1)}, bf16[512,384]{1,0:T(8,128)(2,1)S(1)}, u32[]{:S(2)}, u32[]{:S(2)}) collective-permute-start(bf16[512,384]{1,0:T(8,128)(2,1)S(1)} %slice.7), channel_id=1, source_target_pairs={{0,2},{2,0},{16,18},{18,16},{4,6},{6,4},{20,22},{22,20},{8,10},{10... | collective-permute-start | bytes 1179656 | tf_op jit(solution)/shard_map/ppermute | solution.py:365
  12.2 2.7 %collective-permute-done.3.refs_4_.even = bf16[512,384]{1,0:T(8,128)(2,1)S(1)} collective-permute-done((bf16[512,384]{1,0:T(8,128)(2,1)S(1)}, bf16[512,384]{1,0:T(8,128)(2,1)S(1)}, u32[]{:S(2)}, u32[]{:S(2)}) %collective-permute-start.3) | collective-permute-done | bytes 393248 | tf_op jit(solution)/shard_map/ppermute | solution.py:358
  14.9 0.0 copy-done.1
  15.0 0.0 copy-done
  15.1 1.6 %collective-permute-start.6 = (bf16[512,384]{1,0:T(8,128)(2,1)S(1)}, bf16[512,384]{1,0:T(8,128)(2,1)S(1)}, u32[]{:S(2)}, u32[]{:S(2)}) collective-permute-start(bf16[512,384]{1,0:T(8,128)(2,1)S(1)} %pad_maximum_fusion.2), channel_id=1, source_target_pairs={{0,4},{1,5},{4,0},{5,1},{8,12},{9,13},{12,8},{13,9},{2,6},{3,7},{6... | collective-permute-start | bytes 1179656 | tf_op jit(solution)/shard_map/ppermute | solution.py:358
  16.7 0.0 collective-permute-done.1.refs_1_
  16.8 0.1 collective-permute-start.7
  16.9 0.0 collective-permute-done.2.refs_0_
  16.9 0.0 collective-permute-done.4.refs_5_.odd
  16.9 1.0 %lead_part.1 = (bf16[512,128]{1,0:T(8,128)(2,1)S(1)}, f32[128,128]{1,0:T(8,128)S(1)}) custom-call(bf16[512,384]{1,0:T(8,128)(2,1)S(1)} %collective-permute-done.2.refs_0_, bf16[512,768]{1,0:T(8,128)(2,1)S(1)} %collective-permute-done.1.refs_1_, bf16[512,768]{1,0:T(8,128)(2,1)S(1)} %bitcast.7, bf16[512,768]{1,0:T(8,128)(2,1)S(1)} %bitcast.15, ...), custom_call_target="tpu_custom_call" | custom-call | flops 201326592 | bytes 524288 | tf_op jit(solution)/shard_map/lead_part/pallas_call | solution.py:216
  17.9 1.4 %collective-permute-start.5 = (bf16[512,128]{1,0:T(8,128)(2,1)S(1)}, bf16[512,128]{1,0:T(8,128)(2,1)S(1)}, u32[]{:S(2)}, u32[]{:S(2)}) collective-permute-start(bf16[512,128]{1,0:T(8,128)(2,1)S(1)} %get-tuple-element.35), channel_id=1, source_target_pairs={{0,2},{2,0},{1,3},{3,1},{4,6},{6,4},{5,7},{7,5},{8,10},{10,8},{9,1... | collective-permute-start | bytes 393224 | tf_op jit(solution)/shard_map/ppermute | solution.py:372
  19.3 1.5 %remote_part.2 = bf16[528,256]{1,0:T(8,128)(2,1)S(1)} custom-call(bf16[512,384]{1,0:T(8,128)(2,1)S(1)} %collective-permute-done.2.refs_0_, bf16[512,768]{1,0:T(8,128)(2,1)S(1)} %collective-permute-done.1.refs_1_, bf16[512,768]{1,0:T(8,128)(2,1)S(1)} %bitcast.8, bf16[512,768]{1,0:T(8,128)(2,1)S(1)} %bitcast.16, ...), custom_call_target="tpu_custom_call" | custom-call | flops 402653184 | bytes 1048576 | tf_op jit(solution)/shard_map/remote_part/pallas_call | solution.py:232
  20.8 0.8 %collective-permute-start.9 = (bf16[528,256]{1,0:T(8,128)(2,1)S(1)}, bf16[528,256]{1,0:T(8,128)(2,1)S(1)}, u32[]{:S(2)}, u32[]{:S(2)}) collective-permute-start(bf16[528,256]{1,0:T(8,128)(2,1)S(1)} %remote_part.2), channel_id=1, source_target_pairs={{0,2},{2,0},{1,3},{3,1},{4,6},{6,4},{5,7},{7,5},{8,10},{10,8},{9,1... | collective-permute-start | bytes 811016 | tf_op jit(solution)/shard_map/ppermute | solution.py:372
  21.5 1.9 %local_part.2 = (f32[512,384]{1,0:T(8,128)S(1)}, f32[128,128]{1,0:T(8,128)S(1)}) custom-call(bf16[512,768]{1,0:T(8,128)(2,1)S(1)} %bitcast.23, bf16[512,768]{1,0:T(8,128)(2,1)S(1)} %bitcast.9, bf16[512,768]{1,0:T(8,128)(2,1)S(1)} %bitcast.17, bf16[512,384]{1,0:T(8,128)(2,1)S(1)} %collective-permute-done.3.refs_4_.even, ...), custom_call_target="tpu_custom_call" | custom-call | flops 603979776 | bytes 1572864 | tf_op jit(solution)/shard_map/local_part/pallas_call | solution.py:244
  23.5 0.8 %collective-permute-done.5.rest_0_ = bf16[512,128]{1,0:T(8,128)(2,1)S(1)} collective-permute-done((bf16[512,128]{1,0:T(8,128)(2,1)S(1)}, bf16[512,128]{1,0:T(8,128)(2,1)S(1)}, u32[]{:S(2)}, u32[]{:S(2)}) %collective-permute-start.5) | collective-permute-done | bytes 131104 | tf_op jit(solution)/shard_map/ppermute | solution.py:372
  24.3 0.0 collective-permute-done.refs_0_
  24.3 0.5 %collective-permute-done.6.refs_4_.even = bf16[512,384]{1,0:T(8,128)(2,1)S(1)} collective-permute-done((bf16[512,384]{1,0:T(8,128)(2,1)S(1)}, bf16[512,384]{1,0:T(8,128)(2,1)S(1)}, u32[]{:S(2)}, u32[]{:S(2)}) %collective-permute-start.6) | collective-permute-done | bytes 393248 | tf_op jit(solution)/shard_map/ppermute | solution.py:358
  24.8 0.0 collective-permute-done.7.refs_5_.odd
  24.8 2.0 %remote_part.3 = (bf16[528,256]{1,0:T(8,128)(2,1)S(1)}, bf16[512,128]{1,0:T(8,128)(2,1)S(1)}) custom-call(bf16[512,384]{1,0:T(8,128)(2,1)S(1)} %collective-permute-done.refs_0_, bf16[512,768]{1,0:T(8,128)(2,1)S(1)} %collective-permute-done.1.refs_1_, bf16[512,768]{1,0:T(8,128)(2,1)S(1)} %bitcast.10, bf16[512,768]{1,0:T(8,128)(2,1)S(1)} %bitcast.18, ...), custom_call_target="tpu_custom_call" | custom-call | flops 603979776 | bytes 1572864 | tf_op jit(solution)/shard_map/remote_part/pallas_call | solution.py:232
  26.8 1.3 %collective-permute-start.8 = (bf16[528,256]{1,0:T(8,128)(2,1)S(1)}, bf16[528,256]{1,0:T(8,128)(2,1)S(1)}, u32[]{:S(2)}, u32[]{:S(2)}) collective-permute-start(bf16[528,256]{1,0:T(8,128)(2,1)S(1)} %get-tuple-element.47), channel_id=1, source_target_pairs={{0,2},{2,0},{1,3},{3,1},{4,6},{6,4},{5,7},{7,5},{8,10},{10,8},{9,1... | collective-permute-start | bytes 811016 | tf_op jit(solution)/shard_map/ppermute | solution.py:372
  28.1 1.9 %local_part.3 = (f32[512,384]{1,0:T(8,128)S(1)}, f32[128,128]{1,0:T(8,128)S(1)}) custom-call(bf16[512,768]{1,0:T(8,128)(2,1)S(1)} %bitcast.24, bf16[512,768]{1,0:T(8,128)(2,1)S(1)} %bitcast.11, bf16[512,768]{1,0:T(8,128)(2,1)S(1)} %bitcast.19, bf16[512,384]{1,0:T(8,128)(2,1)S(1)} %collective-permute-done.6.refs_4_.even, ...), custom_call_target="tpu_custom_call" | custom-call | flops 603979776 | bytes 1572864 | tf_op jit(solution)/shard_map/local_part/pallas_call | solution.py:244
  30.0 0.8 %collective-permute-start.10 = (bf16[512,128]{1,0:T(8,128)(2,1)S(1)}, bf16[512,128]{1,0:T(8,128)(2,1)S(1)}, u32[]{:S(2)}, u32[]{:S(2)}) collective-permute-start(bf16[512,128]{1,0:T(8,128)(2,1)S(1)} %get-tuple-element.55), channel_id=1, source_target_pairs={{0,2},{2,0},{1,3},{3,1},{4,6},{6,4},{5,7},{7,5},{8,10},{10,8},{9,1... | collective-permute-start | bytes 393224 | tf_op jit(solution)/shard_map/ppermute | solution.py:372
  30.8 0.0 collective-permute-done.9.rest_1_
  30.8 1.3 %merge_part.2.rest_1_ = bf16[512,768]{1,0:T(8,128)(2,1)} custom-call(f32[512,384]{1,0:T(8,128)S(1)} %get-tuple-element.52.own, f32[128,128]{1,0:T(8,128)S(1)} %get-tuple-element.40.logs, bf16[512,128]{1,0:T(8,128)(2,1)S(1)} %collective-permute-done.5.rest_0_, bf16[528,256]{1,0:T(8,128)(2,1)S(1)} %collective-permute-done.9.rest_1_), custom_call_target="tpu_custom_call" | custom-call | flops 786432 | bytes 1572864 | tf_op jit(solution)/shard_map/merge_part/pallas_call | solution.py:272
  32.1 4.1 %collective-permute-done.8.rest_0_ = bf16[528,256]{1,0:T(8,128)(2,1)S(1)} collective-permute-done((bf16[528,256]{1,0:T(8,128)(2,1)S(1)}, bf16[528,256]{1,0:T(8,128)(2,1)S(1)}, u32[]{:S(2)}, u32[]{:S(2)}) %collective-permute-start.8) | collective-permute-done | bytes 270368 | tf_op jit(solution)/shard_map/ppermute | solution.py:372
  36.2 1.1 %merge_part.3 = (bf16[512,768]{1,0:T(8,128)(2,1)}, f32[512,128]{1,0:T(8,128)S(1)}, f32[512,128]{1,0:T(8,128)S(1)}) custom-call(f32[512,384]{1,0:T(8,128)S(1)} %get-tuple-element.50.own, f32[128,128]{1,0:T(8,128)S(1)} %get-tuple-element.51.logs, bf16[528,256]{1,0:T(8,128)(2,1)S(1)} %collective-permute-done.8.rest_0_, ...), custom_call_target="tpu_custom_call", output_to_operand_aliasing={{0}: (3, {})} | custom-call | flops 786432 | bytes 1572864 | tf_op jit(solution)/shard_map/merge_part/pallas_call | solution.py:272
  37.4 0.9 %collective-permute-done.10.rest_1_ = bf16[512,128]{1,0:T(8,128)(2,1)S(1)} collective-permute-done((bf16[512,128]{1,0:T(8,128)(2,1)S(1)}, bf16[512,128]{1,0:T(8,128)(2,1)S(1)}, u32[]{:S(2)}, u32[]{:S(2)}) %collective-permute-start.10) | collective-permute-done | bytes 131104 | tf_op jit(solution)/shard_map/ppermute | solution.py:372
  38.3 0.7 %finish_part.1 = bf16[512,768]{1,0:T(8,128)(2,1)} custom-call(f32[512,128]{1,0:T(8,128)S(1)} %get-tuple-element.53.scaled, f32[512,128]{1,0:T(8,128)S(1)} %get-tuple-element.54.rest_0_, bf16[512,128]{1,0:T(8,128)(2,1)S(1)} %collective-permute-done.10.rest_1_, bf16[512,768]{1,0:T(8,128)(2,1)} %get-tuple-element.56.rest_2_), custom_call_target="tpu_custom_call", output_to_operand_aliasing={{}: (3, {})} | custom-call | flops 262144 | bytes 524288 | tf_op jit(solution)/shard_map/finish_part/pallas_call | solution.py:288
  (10 shorter events, 0.3 us)
Async XLA Ops:
  0.0 16.7 %collective-permute-start.1 = (bf16[512,768]{1,0:T(8,128)(2,1)}, bf16[512,768]{1,0:T(8,128)(2,1)S(1)}, u32[]{:S(2)}, u32[]{:S(2)}) collective-permute-start(bf16[512,768]{1,0:T(8,128)(2,1)} %bitcast.20), channel_id=1, source_target_pairs={{0,16},{1,3},{2,18},{3,1},{16,0},{17,19},{18,2},{19,17},{4,20},{5,... | collective-permute-start | bytes 2359304 | tf_op jit(solution)/shard_map/ppermute | solution.py:339
  4.3 1.8 %copy-start.2 = (bf16[8,8,8,768]{3,2,1,0:T(8,128)(2,1)S(1)}, bf16[8,8,8,768]{3,2,1,0:T(8,128)(2,1)}, u32[]{:S(2)}) copy-start(bf16[8,8,8,768]{3,2,1,0:T(8,128)(2,1)} %param.3) | copy-start | bytes 2359300
  4.3 10.6 %collective-permute-start.3 = (bf16[512,384]{1,0:T(8,128)(2,1)S(1)}, bf16[512,384]{1,0:T(8,128)(2,1)S(1)}, u32[]{:S(2)}, u32[]{:S(2)}) collective-permute-start(bf16[512,384]{1,0:T(8,128)(2,1)S(1)} %pad_maximum_fusion), channel_id=1, source_target_pairs={{0,4},{1,5},{4,0},{5,1},{8,12},{9,13},{12,8},{13,9},{2,6},{3,7},{6... | collective-permute-start | bytes 1179656 | tf_op jit(solution)/shard_map/ppermute | solution.py:358
  6.0 8.9 %copy-start.1 = (bf16[8,8,8,768]{3,2,1,0:T(8,128)(2,1)S(1)}, bf16[8,8,8,768]{3,2,1,0:T(8,128)(2,1)}, u32[]{:S(2)}) copy-start(bf16[8,8,8,768]{3,2,1,0:T(8,128)(2,1)} %param.5) | copy-start | bytes 2359300
  6.0 10.9 %collective-permute-start.4 = (bf16[512,384]{1,0:T(8,128)(2,1)S(1)}, bf16[512,384]{1,0:T(8,128)(2,1)S(1)}, u32[]{:S(2)}, u32[]{:S(2)}) collective-permute-start(bf16[512,384]{1,0:T(8,128)(2,1)S(1)} %pad_maximum_fusion.1), channel_id=1, source_target_pairs={{0,1},{1,0},{4,8},{5,9},{8,4},{9,5},{12,13},{13,12},{2,3},{3,2},{6... | collective-permute-start | bytes 1179656 | tf_op jit(solution)/shard_map/ppermute | solution.py:358
  6.2 8.8 %copy-start = (bf16[8,8,8,768]{3,2,1,0:T(8,128)(2,1)S(1)}, bf16[8,8,8,768]{3,2,1,0:T(8,128)(2,1)}, u32[]{:S(2)}) copy-start(bf16[8,8,8,768]{3,2,1,0:T(8,128)(2,1)} %param.4) | copy-start | bytes 2359300
  6.2 10.7 %collective-permute-start.2 = (bf16[512,384]{1,0:T(8,128)(2,1)S(1)}, bf16[512,384]{1,0:T(8,128)(2,1)S(1)}, u32[]{:S(2)}, u32[]{:S(2)}) collective-permute-start(bf16[512,384]{1,0:T(8,128)(2,1)S(1)} %slice.6), channel_id=1, source_target_pairs={{0,2},{2,0},{16,18},{18,16},{4,6},{6,4},{20,22},{22,20},{8,10},{10... | collective-permute-start | bytes 1179656 | tf_op jit(solution)/shard_map/ppermute | solution.py:365
  9.8 14.5 %collective-permute-start = (bf16[512,384]{1,0:T(8,128)(2,1)S(1)}, bf16[512,384]{1,0:T(8,128)(2,1)S(1)}, u32[]{:S(2)}, u32[]{:S(2)}) collective-permute-start(bf16[512,384]{1,0:T(8,128)(2,1)S(1)} %slice.7), channel_id=1, source_target_pairs={{0,2},{2,0},{16,18},{18,16},{4,6},{6,4},{20,22},{22,20},{8,10},{10... | collective-permute-start | bytes 1179656 | tf_op jit(solution)/shard_map/ppermute | solution.py:365
  15.1 9.7 %collective-permute-start.6 = (bf16[512,384]{1,0:T(8,128)(2,1)S(1)}, bf16[512,384]{1,0:T(8,128)(2,1)S(1)}, u32[]{:S(2)}, u32[]{:S(2)}) collective-permute-start(bf16[512,384]{1,0:T(8,128)(2,1)S(1)} %pad_maximum_fusion.2), channel_id=1, source_target_pairs={{0,4},{1,5},{4,0},{5,1},{8,12},{9,13},{12,8},{13,9},{2,6},{3,7},{6... | collective-permute-start | bytes 1179656 | tf_op jit(solution)/shard_map/ppermute | solution.py:358
  16.8 7.9 %collective-permute-start.7 = (bf16[512,384]{1,0:T(8,128)(2,1)S(1)}, bf16[512,384]{1,0:T(8,128)(2,1)S(1)}, u32[]{:S(2)}, u32[]{:S(2)}) collective-permute-start(bf16[512,384]{1,0:T(8,128)(2,1)S(1)} %pad_maximum_fusion.3), channel_id=1, source_target_pairs={{0,1},{1,0},{4,8},{5,9},{8,4},{9,5},{12,13},{13,12},{2,3},{3,2},{6... | collective-permute-start | bytes 1179656 | tf_op jit(solution)/shard_map/ppermute | solution.py:358
  17.9 6.4 %collective-permute-start.5 = (bf16[512,128]{1,0:T(8,128)(2,1)S(1)}, bf16[512,128]{1,0:T(8,128)(2,1)S(1)}, u32[]{:S(2)}, u32[]{:S(2)}) collective-permute-start(bf16[512,128]{1,0:T(8,128)(2,1)S(1)} %get-tuple-element.35), channel_id=1, source_target_pairs={{0,2},{2,0},{1,3},{3,1},{4,6},{6,4},{5,7},{7,5},{8,10},{10,8},{9,1... | collective-permute-start | bytes 393224 | tf_op jit(solution)/shard_map/ppermute | solution.py:372
  20.8 10.0 %collective-permute-start.9 = (bf16[528,256]{1,0:T(8,128)(2,1)S(1)}, bf16[528,256]{1,0:T(8,128)(2,1)S(1)}, u32[]{:S(2)}, u32[]{:S(2)}) collective-permute-start(bf16[528,256]{1,0:T(8,128)(2,1)S(1)} %remote_part.2), channel_id=1, source_target_pairs={{0,2},{2,0},{1,3},{3,1},{4,6},{6,4},{5,7},{7,5},{8,10},{10,8},{9,1... | collective-permute-start | bytes 811016 | tf_op jit(solution)/shard_map/ppermute | solution.py:372
  26.8 9.5 %collective-permute-start.8 = (bf16[528,256]{1,0:T(8,128)(2,1)S(1)}, bf16[528,256]{1,0:T(8,128)(2,1)S(1)}, u32[]{:S(2)}, u32[]{:S(2)}) collective-permute-start(bf16[528,256]{1,0:T(8,128)(2,1)S(1)} %get-tuple-element.47), channel_id=1, source_target_pairs={{0,2},{2,0},{1,3},{3,1},{4,6},{6,4},{5,7},{7,5},{8,10},{10,8},{9,1... | collective-permute-start | bytes 811016 | tf_op jit(solution)/shard_map/ppermute | solution.py:372
  30.0 8.3 %collective-permute-start.10 = (bf16[512,128]{1,0:T(8,128)(2,1)S(1)}, bf16[512,128]{1,0:T(8,128)(2,1)S(1)}, u32[]{:S(2)}, u32[]{:S(2)}) collective-permute-start(bf16[512,128]{1,0:T(8,128)(2,1)S(1)} %get-tuple-element.55), channel_id=1, source_target_pairs={{0,2},{2,0},{1,3},{3,1},{4,6},{6,4},{5,7},{7,5},{8,10},{10,8},{9,1... | collective-permute-start | bytes 393224 | tf_op jit(solution)/shard_map/ppermute | solution.py:372
